TPU v7x, 32 devices: a whole 2x2x4 slice. The times are simulated.
32 devices in a mesh: seq: 8 (over z, y), head: 4 (over x, core).
Axes of the slice: x: 2, y: 2, z: 4, core: 2. Of those that a mesh axis runs over, the one named last changes fastest.
Arguments:
- query: bfloat16 [4096, 4096], P('seq', 'head'), may hold values from -46 to 46
- key_rows: bfloat16 [4096, 256], P('seq'), may hold values from -6 to 6
- value_rows: bfloat16 [4096, 256], P('seq'), may hold values from -6 to 6
- grad_out: bfloat16 [4096, 4096], P('seq', 'head'), may hold values from -6 to 6
Outputs:
- grad_query: bfloat16 [4096, 4096], P('seq', 'head')
- grad_key: float32 [4096, 256], P('seq')
- grad_value: float32 [4096, 256], P('seq')
All inputs are finite; a program needn't handle non-finite values.
Results may differ from a plain program's by a relative error of at most 0.0051.
Values may be sent and summed in bfloat16 or wider, within the bound.
No kernel may reach another device: no remote copies, remote signals or barrier semaphores. Data moves between devices by JAX's collectives and lax.ppermute only.
A program may use at most 128 MiB of HBM per device.

v0:
```python
import functools

import jax
import jax.numpy as jnp
from jax import lax
from jax.experimental import pallas as pl
from jax.experimental.pallas import tpu as pltpu
from jax.sharding import PartitionSpec as P

WINDOW = 2048
LOW = -1e30
VMEM_BYTES = 56 * 1024 * 1024


def along_seq(block, distance):
    count = lax.axis_size("seq")
    route = [(i, (i + distance) % count) for i in range(count)]
    return lax.ppermute(block, "seq", route)


def swap_heads(block, bit):
    route = [(i, i ^ bit) for i in range(lax.axis_size("head"))]
    return lax.ppermute(block, "head", route)


def dot_t(left, right):
    return lax.dot_general(
        left, right, (((1,), (1,)), ((), ())), preferred_element_type=jnp.float32
    )


def dot(left, right):
    return jnp.dot(left, right, preferred_element_type=jnp.float32)


def fold_rows(block, combine):
    rows = block.shape[0]
    while rows > 8:
        rows //= 2
        block = combine(block[:rows], block[rows:])
    return block


def lower_mask(half):
    keys = lax.broadcasted_iota(jnp.int32, (half, half), 0)
    queries = lax.broadcasted_iota(jnp.int32, (half, half), 1)
    return queries >= keys


def load_rows(own_ref, mine_refs, other_refs, ext, sem, core, half, reach):
    copies = []

    def copy(source, first):
        copies.append(
            pltpu.make_async_copy(source, ext.at[pl.ds(first, source.shape[0])], sem.at[len(copies)])
        )

    copy(own_ref, reach * 2 * half)
    for d in range(1, reach + 1):
        base = (reach - d) * 2 * half
        copy(mine_refs[d - 1], pl.multiple_of(base + core * half, half))
        copy(other_refs[d - 1], pl.multiple_of(base + (1 - core) * half, half))
    for each in copies:
        each.start()
    for each in copies:
        each.wait()


def corner_products(product, ext, rows, half, reach):
    far, own = 0, reach * 2 * half
    lo, hi = rows[:half], rows[half:]
    own_lo = product(ext[own : own + half], rows)
    own_hi = product(ext[own + half : own + 2 * half], hi)
    far_lo = product(ext[far : far + half], lo)
    far_hi = product(ext[far + half : far + 2 * half], rows)
    return own_lo, own_hi, far_lo, far_hi


def add_corner(corner, acc, rows, half, reach, mask):
    zero = jnp.zeros((half, half), corner.dtype)
    lo_lo, lo_hi = corner[:half, :half], corner[:half, half:]
    hi_lo, hi_hi = corner[half:, :half], corner[half:, half:]
    lo, hi = rows[:half], rows[half:]
    far, own = 0, reach * 2 * half
    acc[own : own + half] += dot(jnp.where(mask, lo_lo, zero), lo) + dot(lo_hi, hi)
    acc[own + half : own + 2 * half] += dot(jnp.where(mask, hi_hi, zero), hi)
    acc[far : far + half] += dot(jnp.where(mask, zero, lo_lo), lo)
    acc[far + half : far + 2 * half] += dot(hi_lo, lo) + dot(jnp.where(mask, zero, hi_hi), hi)


def split_out(acc, keep_ref, send_ref, core, half, reach):
    for d in range(reach + 1):
        base = (reach - d) * 2 * half
        keep_ref[d] = acc[pl.ds(pl.multiple_of(base + core * half, half), half), :]
        send_ref[d] = acc[pl.ds(pl.multiple_of(base + (1 - core) * half, half), half), :].astype(
            send_ref.dtype
        )


def probs_kernel(reach, scale, place, q_ref, g_ref, own_ref, *rest):
    mine_refs, other_refs, rest = rest[:reach], rest[reach : 2 * reach], rest[2 * reach :]
    e_ref, gs_ref, inv_ref, keep_ref, send_ref, ext, s_buf, acc, sem = rest
    head, heads = pl.program_id(0), pl.num_programs(0)
    rank, core = place[0], place[1]
    half = own_ref.shape[0] // 2
    full = 2 * half

    @pl.when(head == 0)
    def _():
        load_rows(own_ref, mine_refs, other_refs, ext, sem, core, half, reach)
        acc[...] = jnp.zeros_like(acc)

    mask = lower_mask(half)
    rows = q_ref[...] * jnp.asarray(scale, q_ref.dtype)
    far_bias = jnp.where(rank >= reach, 0.0, LOW).astype(jnp.float32)
    own_lo, own_hi, far_lo, far_hi = corner_products(dot_t, ext, rows, half, reach)
    s_buf[:half, :half] = jnp.where(mask, own_lo[:, :half], far_lo + far_bias)
    s_buf[:half, half:] = own_lo[:, half:]
    s_buf[half:full, :half] = far_hi[:, :half] + far_bias
    s_buf[half:full, half:] = jnp.where(mask, own_hi, far_hi[:, half:] + far_bias)
    top = fold_rows(s_buf[:full], jnp.maximum)
    for d in range(reach - 1, 0, -1):
        at = (reach - d) * full
        for first in (at, at + half):
            block = dot_t(ext[first : first + half], rows)
            s_buf[first : first + half] = block
            part = fold_rows(block, jnp.maximum)
            top = jnp.maximum(top, jnp.where(rank >= d, part, LOW))
    top = jnp.max(top, axis=0, keepdims=True)
    total = jnp.zeros((8, full), jnp.float32)
    for d in range(reach, 0, -1):
        at = (reach - d) * full
        level = top if d == reach else jnp.where(rank >= d, top, -LOW)
        for first in (at, at + half):
            expo = jnp.exp(s_buf[first : first + half] - level)
            total = total + fold_rows(expo, jnp.add)
            e_ref[0, first : first + half] = expo.astype(jnp.bfloat16)
    inv = 1.0 / jnp.sum(total, axis=0, keepdims=True)
    inv_rows = jnp.broadcast_to(inv, (8, full))
    inv_ref[0] = inv_rows
    scaled = (g_ref[...].astype(jnp.float32) * jnp.transpose(inv_rows)[:, :1]).astype(jnp.bfloat16)
    gs_ref[...] = scaled
    add_corner(e_ref[0, :full], acc, scaled, half, reach, mask)
    for d in range(reach - 1, 0, -1):
        at = (reach - d) * full
        acc[at : at + full] += dot(e_ref[0, at : at + full], scaled)

    @pl.when(head == heads - 1)
    def _():
        split_out(acc, keep_ref, send_ref, core, half, reach)


def dscores_kernel(reach, scale, place, q_ref, gs_ref, inv_ref, e_ref, own_ref, *rest):
    mine_refs, other_refs, rest = rest[:reach], rest[reach : 2 * reach], rest[2 * reach :]
    ds_ref, keep_ref, send_ref, ext, dp_buf, acc, sem = rest
    head, heads = pl.program_id(0), pl.num_programs(0)
    core = place[1]
    half = own_ref.shape[0] // 2
    full = 2 * half

    @pl.when(head == 0)
    def _():
        load_rows(own_ref, mine_refs, other_refs, ext, sem, core, half, reach)
        acc[...] = jnp.zeros_like(acc)

    mask = lower_mask(half)
    rows = gs_ref[...]
    own_lo, own_hi, far_lo, far_hi = corner_products(dot_t, ext, rows, half, reach)
    dp_buf[:half, :half] = jnp.where(mask, own_lo[:, :half], far_lo)
    dp_buf[:half, half:] = own_lo[:, half:]
    dp_buf[half:full, :half] = far_hi[:, :half]
    dp_buf[half:full, half:] = jnp.where(mask, own_hi, far_hi[:, half:])
    total = fold_rows(dp_buf[:full] * e_ref[0, :full].astype(jnp.float32), jnp.add)
    for first in range(full, reach * full, half):
        block = dot_t(ext[first : first + half], rows)
        dp_buf[first : first + half] = block
        total = total + fold_rows(
            block * e_ref[0, first : first + half].astype(jnp.float32), jnp.add
        )
    delta = jnp.sum(total, axis=0, keepdims=True) * inv_ref[0, :1]
    rows = q_ref[...] * jnp.asarray(scale, q_ref.dtype)
    for first in range(0, reach * full, half):
        block = e_ref[0, first : first + half].astype(jnp.float32) * (
            dp_buf[first : first + half] - delta
        )
        ds_ref[0, first : first + half] = block.astype(jnp.bfloat16)
    add_corner(ds_ref[0, :full], acc, rows, half, reach, mask)
    for first in range(full, reach * full, full):
        acc[first : first + full] += dot(ds_ref[0, first : first + full], rows)

    @pl.when(head == heads - 1)
    def _():
        split_out(acc, keep_ref, send_ref, core, half, reach)


def dquery_kernel(reach, scale, place, ds_ref, own_ref, *rest):
    mine_refs, other_refs, rest = rest[:reach], rest[reach : 2 * reach], rest[2 * reach :]
    dq_ref, ext, ext_t, sem = rest
    core = place[1]
    half = own_ref.shape[0] // 2
    full = 2 * half

    @pl.when(pl.program_id(0) == 0)
    def _():
        load_rows(own_ref, mine_refs, other_refs, ext, sem, core, half, reach)
        for first in range(0, (reach + 1) * full, half):
            ext_t[:, first : first + half] = jnp.transpose(ext[first : first + half])

    mask = lower_mask(half)
    zero = jnp.zeros((half, half), jnp.bfloat16)
    own = reach * full
    lo_lo, lo_hi = ds_ref[0, :half, :half], ds_ref[0, :half, half:]
    hi_lo, hi_hi = ds_ref[0, half:full, :half], ds_ref[0, half:full, half:]
    lo = (
        dot(ext_t[:, own : own + half], jnp.where(mask, lo_lo, zero))
        + dot(ext_t[:, :half], jnp.where(mask, zero, lo_lo))
        + dot(ext_t[:, half:full], hi_lo)
    )
    hi = (
        dot(ext_t[:, own : own + half], lo_hi)
        + dot(ext_t[:, own + half : own + full], jnp.where(mask, hi_hi, zero))
        + dot(ext_t[:, half:full], jnp.where(mask, zero, hi_hi))
    )
    total = dot(ext_t[:, full:own], ds_ref[0, full:own])
    lo = lo + total[:, :half]
    hi = hi + total[:, half:]
    dq_ref[:half] = jnp.transpose(lo * scale).astype(dq_ref.dtype)
    dq_ref[half:] = jnp.transpose(hi * scale).astype(dq_ref.dtype)


def gather_halo(rows, core, half, reach):
    piece = lax.dynamic_slice_in_dim(rows, core * half, half, 0)
    mine = [along_seq(piece, 1), along_seq(piece, 2)]
    for d in range(3, reach + 1):
        mine.append(along_seq(mine[d - 3], 2))
    other = [swap_heads(block, 1) for block in mine]
    return mine, other


def return_halo(keep, send, core, half, reach):
    total = keep + swap_heads(send, 1).astype(jnp.float32)
    parts = [total[d] for d in range(reach + 1)]
    for d in range(reach, 2, -1):
        back = along_seq(parts[d].astype(jnp.bfloat16), -2)
        parts[d - 2] = parts[d - 2] + back.astype(jnp.float32)
    own = parts[0]
    for d in (2, 1):
        own = own + along_seq(parts[d].astype(jnp.bfloat16), -d).astype(jnp.float32)
    bit = 2
    while bit < lax.axis_size("head"):
        low = own.astype(jnp.bfloat16)
        own = low.astype(jnp.float32) + swap_heads(low, bit).astype(jnp.float32)
        bit *= 2
    other = swap_heads(own, 1)
    first = jnp.where(core == 0, own, other)
    second = jnp.where(core == 0, other, own)
    return jnp.concatenate([first, second], axis=0)


def on_device(query, key_rows, value_rows, grad_out):
    tok_rows, head_dim = key_rows.shape
    heads = query.shape[1] // head_dim
    reach = WINDOW // tok_rows
    half = tok_rows // 2
    scale = head_dim ** (-0.5)
    core = lax.axis_index("head") % 2
    place = jnp.stack([lax.axis_index("seq"), core]).astype(jnp.int32)
    ext_rows = (reach + 1) * tok_rows
    span = reach * tok_rows

    smem = pl.BlockSpec(memory_space=pltpu.SMEM)
    hbm = pl.BlockSpec(memory_space=pl.ANY)
    by_head = pl.BlockSpec((tok_rows, head_dim), lambda h: (0, h))
    tiles = pl.BlockSpec((1, span, tok_rows), lambda h: (h, 0, 0))
    row = pl.BlockSpec((1, 8, tok_rows), lambda h: (h, 0, 0))
    whole = pl.BlockSpec((reach + 1, half, head_dim), lambda h: (0, 0, 0))
    tile_shape = jax.ShapeDtypeStruct((heads, span, tok_rows), jnp.bfloat16)
    keep_shape = jax.ShapeDtypeStruct((reach + 1, half, head_dim), jnp.float32)
    send_shape = jax.ShapeDtypeStruct((reach + 1, half, head_dim), jnp.bfloat16)
    ext = pltpu.VMEM((ext_rows, head_dim), jnp.bfloat16)
    acc = pltpu.VMEM((ext_rows, head_dim), jnp.float32)
    tile = pltpu.VMEM((span, tok_rows), jnp.float32)
    sems = pltpu.SemaphoreType.DMA((2 * reach + 1,))
    product = 2 * heads * tok_rows * (reach * tok_rows + half) * head_dim

    def call(body, name, products, **spec):
        return pl.pallas_call(
            functools.partial(body, reach, scale),
            grid=(heads,),
            compiler_params=pltpu.CompilerParams(vmem_limit_bytes=VMEM_BYTES),
            cost_estimate=pl.CostEstimate(
                flops=products * product, bytes_accessed=16 * 2**20, transcendentals=0
            ),
            name=name,
            **spec,
        )

    keys_mine, keys_other = gather_halo(key_rows, core, half, reach)
    values_mine, values_other = gather_halo(value_rows, core, half, reach)

    expo, grads, inv, dv_keep, dv_send = call(
        probs_kernel,
        "probs",
        2,
        in_specs=[smem, by_head, by_head] + [hbm] * (2 * reach + 1),
        out_specs=[tiles, by_head, row, whole, whole],
        out_shape=[
            tile_shape,
            jax.ShapeDtypeStruct(grad_out.shape, jnp.bfloat16),
            jax.ShapeDtypeStruct((heads, 8, tok_rows), jnp.float32),
            keep_shape,
            send_shape,
        ],
        scratch_shapes=[ext, tile, acc, sems],
    )(place, query, grad_out, key_rows, *keys_mine, *keys_other)

    dscores, dk_keep, dk_send = call(
        dscores_kernel,
        "dscores",
        2,
        in_specs=[smem, by_head, by_head, row, tiles] + [hbm] * (2 * reach + 1),
        out_specs=[tiles, whole, whole],
        out_shape=[tile_shape, keep_shape, send_shape],
        scratch_shapes=[ext, tile, acc, sems],
    )(place, query, grads, inv, expo, value_rows, *values_mine, *values_other)

    grad_value = return_halo(dv_keep, dv_send, core, half, reach)

    (grad_query,) = call(
        dquery_kernel,
        "dquery",
        1,
        in_specs=[smem, tiles] + [hbm] * (2 * reach + 1),
        out_specs=[by_head],
        out_shape=[jax.ShapeDtypeStruct(query.shape, query.dtype)],
        scratch_shapes=[ext, pltpu.VMEM((head_dim, ext_rows), jnp.bfloat16), sems],
    )(place, dscores, key_rows, *keys_mine, *keys_other)

    grad_key = return_halo(dk_keep, dk_send, core, half, reach)
    return grad_query, grad_key, grad_value


def solution(mesh):
    return jax.shard_map(
        on_device,
        mesh=mesh,
        in_specs=(P("seq", "head"), P("seq", None), P("seq", None), P("seq", "head")),
        out_specs=(P("seq", "head"), P("seq", None), P("seq", None)),
        check_vma=False,
    )
```

profile of v0, /device:TPU:0, one launch (start us, length us, event | category | flops | bytes accessed | tf_op | source)
XLA Modules:
  0.0 101.8 jit_solution(8502673576678592624)
XLA Ops:
  0.6 0.9 constant_dynamic-slice_fusion.1
  1.6 3.0 %collective-permute-start = (bf16[256,256]{1,0:T(8,128)(2,1)S(1)}, bf16[256,256]{1,0:T(8,128)(2,1)S(1)}, u32[]{:S(2)}, u32[]{:S(2)}) collective-permute-start(bf16[256,256]{1,0:T(8,128)(2,1)S(1)} %constant_dynamic-slice_fusion.1), channel_id=1, source_target_pairs={{0,4},{4,8},{8,12},{12,16},{16,20},{20,24},{24,28},{28,0},{1,5},{5... | collective-permute-start | bytes 393224 | tf_op jit(solution)/shard_map/ppermute | solution.py:18
  4.6 1.6 %collective-permute-start.1 = (bf16[256,256]{1,0:T(8,128)(2,1)S(1)}, bf16[256,256]{1,0:T(8,128)(2,1)S(1)}, u32[]{:S(2)}, u32[]{:S(2)}) collective-permute-start(bf16[256,256]{1,0:T(8,128)(2,1)S(1)} %constant_dynamic-slice_fusion.1), channel_id=1, source_target_pairs={{0,8},{4,12},{8,16},{12,20},{16,24},{20,28},{24,0},{28,4},{1,9},{5... | collective-permute-start | bytes 393224 | tf_op jit(solution)/shard_map/ppermute | solution.py:18
  6.2 0.9 constant_dynamic-slice_fusion
  7.1 1.6 %collective-permute-start.8 = (bf16[256,256]{1,0:T(8,128)(2,1)S(1)}, bf16[256,256]{1,0:T(8,128)(2,1)S(1)}, u32[]{:S(2)}, u32[]{:S(2)}) collective-permute-start(bf16[256,256]{1,0:T(8,128)(2,1)S(1)} %constant_dynamic-slice_fusion), channel_id=1, source_target_pairs={{0,4},{4,8},{8,12},{12,16},{16,20},{20,24},{24,28},{28,0},{1,5},{5... | collective-permute-start | bytes 393224 | tf_op jit(solution)/shard_map/ppermute | solution.py:18
  8.7 1.6 %collective-permute-start.9 = (bf16[256,256]{1,0:T(8,128)(2,1)S(1)}, bf16[256,256]{1,0:T(8,128)(2,1)S(1)}, u32[]{:S(2)}, u32[]{:S(2)}) collective-permute-start(bf16[256,256]{1,0:T(8,128)(2,1)S(1)} %constant_dynamic-slice_fusion), channel_id=1, source_target_pairs={{0,8},{4,12},{8,16},{12,20},{16,24},{20,28},{24,0},{28,4},{1,9},{5... | collective-permute-start | bytes 393224 | tf_op jit(solution)/shard_map/ppermute | solution.py:18
  10.2 1.7 %collective-permute-done.rest_0_ = bf16[256,256]{1,0:T(8,128)(2,1)S(1)} collective-permute-done((bf16[256,256]{1,0:T(8,128)(2,1)S(1)}, bf16[256,256]{1,0:T(8,128)(2,1)S(1)}, u32[]{:S(2)}, u32[]{:S(2)}) %collective-permute-start) | collective-permute-done | bytes 131104 | tf_op jit(solution)/shard_map/ppermute | solution.py:18
  12.0 0.0 copy-start.3
  12.0 1.5 %collective-permute-start.3 = (bf16[256,256]{1,0:T(8,128)(2,1)S(1)}, bf16[256,256]{1,0:T(8,128)(2,1)S(1)}, u32[]{:S(2)}, u32[]{:S(2)}) collective-permute-start(bf16[256,256]{1,0:T(8,128)(2,1)S(1)} %collective-permute-done.1.rest_1_), channel_id=1, source_target_pairs={{0,8},{4,12},{8,16},{12,20},{16,24},{20,28},{24,0},{28,4},{1,9},{5... | collective-permute-start | bytes 393224 | tf_op jit(solution)/shard_map/ppermute | solution.py:18
  13.5 0.0 collective-permute-start.4
  13.5 4.1 %collective-permute-done.8.rest_0_ = bf16[256,256]{1,0:T(8,128)(2,1)S(1)} collective-permute-done((bf16[256,256]{1,0:T(8,128)(2,1)S(1)}, bf16[256,256]{1,0:T(8,128)(2,1)S(1)}, u32[]{:S(2)}, u32[]{:S(2)}) %collective-permute-start.8) | collective-permute-done | bytes 131104 | tf_op jit(solution)/shard_map/ppermute | solution.py:18
  17.6 0.0 collective-permute-start.5
  17.6 0.0 collective-permute-done.9.rest_1_
  17.6 0.1 collective-permute-start.10
  17.7 2.0 %collective-permute-done.2.rest_2_ = bf16[256,256]{1,0:T(8,128)(2,1)S(1)} collective-permute-done((bf16[256,256]{1,0:T(8,128)(2,1)S(1)}, bf16[256,256]{1,0:T(8,128)(2,1)S(1)}, u32[]{:S(2)}, u32[]{:S(2)}) %collective-permute-start.2) | collective-permute-done | bytes 131104 | tf_op jit(solution)/shard_map/ppermute | solution.py:18
  19.6 1.4 %collective-permute-done.3.rest_3_ = bf16[256,256]{1,0:T(8,128)(2,1)S(1)} collective-permute-done((bf16[256,256]{1,0:T(8,128)(2,1)S(1)}, bf16[256,256]{1,0:T(8,128)(2,1)S(1)}, u32[]{:S(2)}, u32[]{:S(2)}) %collective-permute-start.3) | collective-permute-done | bytes 131104 | tf_op jit(solution)/shard_map/ppermute | solution.py:18
  21.0 0.0 collective-permute-start.6
  21.0 0.0 collective-permute-done.4.rest_4_
  21.1 0.5 collective-permute-start.7
  21.6 0.6 pad_add_fusion.place
  22.2 0.1 collective-permute-start.12
  22.2 3.5 %collective-permute-done.10.rest_2_ = bf16[256,256]{1,0:T(8,128)(2,1)S(1)} collective-permute-done((bf16[256,256]{1,0:T(8,128)(2,1)S(1)}, bf16[256,256]{1,0:T(8,128)(2,1)S(1)}, u32[]{:S(2)}, u32[]{:S(2)}) %collective-permute-start.10) | collective-permute-done | bytes 131104 | tf_op jit(solution)/shard_map/ppermute | solution.py:18
  25.7 2.4 %collective-permute-done.11.rest_3_ = bf16[256,256]{1,0:T(8,128)(2,1)S(1)} collective-permute-done((bf16[256,256]{1,0:T(8,128)(2,1)S(1)}, bf16[256,256]{1,0:T(8,128)(2,1)S(1)}, u32[]{:S(2)}, u32[]{:S(2)}) %collective-permute-start.11) | collective-permute-done | bytes 131104 | tf_op jit(solution)/shard_map/ppermute | solution.py:18
  28.1 0.0 collective-permute-start.14
  28.1 0.5 collective-permute-start.15
  28.7 0.1 copy-done.8
  28.8 0.7 copy-done.9
  29.5 16.2 %probs.1 = (bf16[4,2048,512]{2,1,0:T(8,128)(2,1)}, bf16[512,1024]{1,0:T(8,128)(2,1)}, f32[4,8,512]{2,1,0:T(8,128)}, f32[5,256,256]{2,1,0:T(8,128)}, bf16[5,256,256]{2,1,0:T(8,128)(2,1)}) custom-call(s32[2]{0:T(128)} %pad_add_fusion.place, bf16[512,1024]{1,0:T(8,128)(2,1)} %q_ref.3, bf16[512,1024]{1,0:T(8,128)(2,1)} %g_ref.1, bf16[512,256]{1,0:T(8,128)(2,1)} %own_ref.5, ...), custom_call_target="tpu_custom_call" | custom-call | flops 4831838208 | bytes 16777216 | tf_op jit(solution)/shard_map/probs/pallas_call | solution.py:301
  45.7 0.5 collective-permute-start.23
  46.3 0.6 copy-done.14
  46.9 0.1 copy-done.15
  47.0 0.1 copy-done.16
  47.0 0.1 copy-done.17
  47.1 16.0 %dscores.1 = (bf16[4,2048,512]{2,1,0:T(8,128)(2,1)}, f32[5,256,256]{2,1,0:T(8,128)}, bf16[5,256,256]{2,1,0:T(8,128)(2,1)}) custom-call(s32[2]{0:T(128)} %pad_add_fusion.place, bf16[512,1024]{1,0:T(8,128)(2,1)} %q_ref.3, bf16[512,1024]{1,0:T(8,128)(2,1)} %get-tuple-element.11.gs_ref, f32[4,8,512]{2,1,0:T(8,128)} %get-tuple-element.12.inv_ref, ...), custom_call_target="tpu_custom_call" | custom-call | flops 4831838208 | bytes 16777216 | tf_op jit(solution)/shard_map/dscores/pallas_call | solution.py:317
  63.1 0.1 collective-permute-start.16
  63.2 0.2 fusion.14
  63.4 0.3 collective-permute-start.24
  63.7 0.4 collective-permute-start.26
  64.2 1.3 %collective-permute-done.16 = bf16[5,256,256]{2,1,0:T(8,128)(2,1)S(1)} collective-permute-done((bf16[5,256,256]{2,1,0:T(8,128)(2,1)}, bf16[5,256,256]{2,1,0:T(8,128)(2,1)S(1)}, u32[]{:S(2)}, u32[]{:S(2)}) %collective-permute-start.16) | collective-permute-done | bytes 655392 | tf_op jit(solution)/shard_map/ppermute | solution.py:23
  65.5 0.2 fusion.15
  65.7 0.3 collective-permute-start.17
  66.0 2.8 %collective-permute-start.19 = (bf16[256,256]{1,0:T(8,128)(2,1)S(1)}, bf16[256,256]{1,0:T(8,128)(2,1)S(1)}, u32[]{:S(2)}, u32[]{:S(2)}) collective-permute-start(bf16[256,256]{1,0:T(8,128)(2,1)S(1)} %get-tuple-element.30), channel_id=1, source_target_pairs={{0,24},{4,28},{8,0},{12,4},{16,8},{20,12},{24,16},{28,20},{1,25},{... | collective-permute-start | bytes 393224 | tf_op jit(solution)/shard_map/ppermute | solution.py:18
  68.8 1.0 %collective-permute-done.24 = bf16[256,256]{1,0:T(8,128)(2,1)S(1)} collective-permute-done((bf16[256,256]{1,0:T(8,128)(2,1)S(1)}, bf16[256,256]{1,0:T(8,128)(2,1)S(1)}, u32[]{:S(2)}, u32[]{:S(2)}) %collective-permute-start.24) | collective-permute-done | bytes 131104 | tf_op jit(solution)/shard_map/ppermute | solution.py:18
  69.8 2.8 %collective-permute-done.26 = bf16[256,256]{1,0:T(8,128)(2,1)S(1)} collective-permute-done((bf16[256,256]{1,0:T(8,128)(2,1)S(1)}, bf16[256,256]{1,0:T(8,128)(2,1)S(1)}, u32[]{:S(2)}, u32[]{:S(2)}) %collective-permute-start.26) | collective-permute-done | bytes 131104 | tf_op jit(solution)/shard_map/ppermute | solution.py:18
  72.6 0.1 fusion.3
  72.7 2.0 %collective-permute-start.25 = (bf16[256,256]{1,0:T(8,128)(2,1)S(1)}, bf16[256,256]{1,0:T(8,128)(2,1)S(1)}, u32[]{:S(2)}, u32[]{:S(2)}) collective-permute-start(bf16[256,256]{1,0:T(8,128)(2,1)S(1)} %get-tuple-element.23), channel_id=1, source_target_pairs={{0,24},{4,28},{8,0},{12,4},{16,8},{20,12},{24,16},{28,20},{1,25},{... | collective-permute-start | bytes 393224 | tf_op jit(solution)/shard_map/ppermute | solution.py:18
  74.7 4.2 %collective-permute-start.27 = (bf16[256,256]{1,0:T(8,128)(2,1)S(1)}, bf16[256,256]{1,0:T(8,128)(2,1)S(1)}, u32[]{:S(2)}, u32[]{:S(2)}) collective-permute-start(bf16[256,256]{1,0:T(8,128)(2,1)S(1)} %get-tuple-element.24), channel_id=1, source_target_pairs={{0,28},{4,0},{8,4},{12,8},{16,12},{20,16},{24,20},{28,24},{1,29},{... | collective-permute-start | bytes 393224 | tf_op jit(solution)/shard_map/ppermute | solution.py:18
  79.0 0.1 fusion.10
  79.0 1.3 %collective-permute-start.18 = (bf16[256,256]{1,0:T(8,128)(2,1)S(1)}, bf16[256,256]{1,0:T(8,128)(2,1)S(1)}, u32[]{:S(2)}, u32[]{:S(2)}) collective-permute-start(bf16[256,256]{1,0:T(8,128)(2,1)S(1)} %get-tuple-element.25), channel_id=1, source_target_pairs={{0,24},{4,28},{8,0},{12,4},{16,8},{20,12},{24,16},{28,20},{1,25},{... | collective-permute-start | bytes 393224 | tf_op jit(solution)/shard_map/ppermute | solution.py:18
  80.3 4.2 %collective-permute-start.20 = (bf16[256,256]{1,0:T(8,128)(2,1)S(1)}, bf16[256,256]{1,0:T(8,128)(2,1)S(1)}, u32[]{:S(2)}, u32[]{:S(2)}) collective-permute-start(bf16[256,256]{1,0:T(8,128)(2,1)S(1)} %get-tuple-element.26), channel_id=1, source_target_pairs={{0,28},{4,0},{8,4},{12,8},{16,12},{20,16},{24,20},{28,24},{1,29},{... | collective-permute-start | bytes 393224 | tf_op jit(solution)/shard_map/ppermute | solution.py:18
  84.6 0.1 fusion.6
  84.6 1.6 %collective-permute-start.28 = (bf16[256,256]{1,0:T(8,128)(2,1)S(1)}, bf16[256,256]{1,0:T(8,128)(2,1)S(1)}, u32[]{:S(2)}, u32[]{:S(2)}) collective-permute-start(bf16[256,256]{1,0:T(8,128)(2,1)S(1)} %fusion.6), channel_id=1, source_target_pairs={{0,2},{1,3},{2,0},{3,1},{4,6},{5,7},{6,4},{7,5},{8,10},{9,11},{10,... | collective-permute-start | bytes 393224 | tf_op jit(solution)/shard_map/ppermute | solution.py:23
  86.2 0.1 collective-permute-done.18
  86.3 1.7 %collective-permute-done.20 = bf16[256,256]{1,0:T(8,128)(2,1)S(1)} collective-permute-done((bf16[256,256]{1,0:T(8,128)(2,1)S(1)}, bf16[256,256]{1,0:T(8,128)(2,1)S(1)}, u32[]{:S(2)}, u32[]{:S(2)}) %collective-permute-start.20) | collective-permute-done | bytes 131104 | tf_op jit(solution)/shard_map/ppermute | solution.py:18
  88.0 0.1 fusion.13
  88.1 1.6 %collective-permute-start.21 = (bf16[256,256]{1,0:T(8,128)(2,1)S(1)}, bf16[256,256]{1,0:T(8,128)(2,1)S(1)}, u32[]{:S(2)}, u32[]{:S(2)}) collective-permute-start(bf16[256,256]{1,0:T(8,128)(2,1)S(1)} %fusion.13), channel_id=1, source_target_pairs={{0,2},{1,3},{2,0},{3,1},{4,6},{5,7},{6,4},{7,5},{8,10},{9,11},{10,... | collective-permute-start | bytes 393224 | tf_op jit(solution)/shard_map/ppermute | solution.py:23
  89.6 0.6 collective-permute-done.28
  90.3 0.1 collective-permute-start.29
  90.4 8.8 %dquery.1 = bf16[512,1024]{1,0:T(8,128)(2,1)} custom-call(s32[2]{0:T(128)} %pad_add_fusion.place, bf16[4,2048,512]{2,1,0:T(8,128)(2,1)} %get-tuple-element.14.ds_ref, bf16[512,256]{1,0:T(8,128)(2,1)} %own_ref.5, bf16[256,256]{1,0:T(8,128)(2,1)} %copy-done.2, bf16[256,256]{1,0:T(8,128)(2,1)} %copy-done.3, bf16[256,256]{1,0:T(8,128)(2,1)} %copy-done.4, ...), custom_call_target="tpu_custom_call" | custom-call | flops 2415919104 | bytes 16777216 | tf_op jit(solution)/shard_map/dquery/pallas_call | solution.py:329
  99.2 0.5 collective-permute-start.22
  99.8 0.8 pad_maximum_fusion.1
  100.6 0.3 collective-permute-done.22
  100.9 0.1 broadcast_select_fusion.3
  101.0 0.8 pad_maximum_fusion
  (52 shorter events, 0.2 us)
Async XLA Ops:
  1.6 10.4 %collective-permute-start = (bf16[256,256]{1,0:T(8,128)(2,1)S(1)}, bf16[256,256]{1,0:T(8,128)(2,1)S(1)}, u32[]{:S(2)}, u32[]{:S(2)}) collective-permute-start(bf16[256,256]{1,0:T(8,128)(2,1)S(1)} %constant_dynamic-slice_fusion.1), channel_id=1, source_target_pairs={{0,4},{4,8},{8,12},{12,16},{16,20},{20,24},{24,28},{28,0},{1,5},{5... | collective-permute-start | bytes 393224 | tf_op jit(solution)/shard_map/ppermute | solution.py:18
  4.6 7.4 %collective-permute-start.1 = (bf16[256,256]{1,0:T(8,128)(2,1)S(1)}, bf16[256,256]{1,0:T(8,128)(2,1)S(1)}, u32[]{:S(2)}, u32[]{:S(2)}) collective-permute-start(bf16[256,256]{1,0:T(8,128)(2,1)S(1)} %constant_dynamic-slice_fusion.1), channel_id=1, source_target_pairs={{0,8},{4,12},{8,16},{12,20},{16,24},{20,28},{24,0},{28,4},{1,9},{5... | collective-permute-start | bytes 393224 | tf_op jit(solution)/shard_map/ppermute | solution.py:18
  7.1 10.5 %collective-permute-start.8 = (bf16[256,256]{1,0:T(8,128)(2,1)S(1)}, bf16[256,256]{1,0:T(8,128)(2,1)S(1)}, u32[]{:S(2)}, u32[]{:S(2)}) collective-permute-start(bf16[256,256]{1,0:T(8,128)(2,1)S(1)} %constant_dynamic-slice_fusion), channel_id=1, source_target_pairs={{0,4},{4,8},{8,12},{12,16},{16,20},{20,24},{24,28},{28,0},{1,5},{5... | collective-permute-start | bytes 393224 | tf_op jit(solution)/shard_map/ppermute | solution.py:18
  8.7 8.9 %collective-permute-start.9 = (bf16[256,256]{1,0:T(8,128)(2,1)S(1)}, bf16[256,256]{1,0:T(8,128)(2,1)S(1)}, u32[]{:S(2)}, u32[]{:S(2)}) collective-permute-start(bf16[256,256]{1,0:T(8,128)(2,1)S(1)} %constant_dynamic-slice_fusion), channel_id=1, source_target_pairs={{0,8},{4,12},{8,16},{12,20},{16,24},{20,28},{24,0},{28,4},{1,9},{5... | collective-permute-start | bytes 393224 | tf_op jit(solution)/shard_map/ppermute | solution.py:18
  12.0 16.7 %copy-start.2 = (bf16[256,256]{1,0:T(8,128)(2,1)}, bf16[256,256]{1,0:T(8,128)(2,1)S(1)}, u32[]{:S(2)}) copy-start(bf16[256,256]{1,0:T(8,128)(2,1)S(1)} %collective-permute-done.rest_0_) | copy-start | bytes 393220
  12.0 7.7 %collective-permute-start.2 = (bf16[256,256]{1,0:T(8,128)(2,1)S(1)}, bf16[256,256]{1,0:T(8,128)(2,1)S(1)}, u32[]{:S(2)}, u32[]{:S(2)}) collective-permute-start(bf16[256,256]{1,0:T(8,128)(2,1)S(1)} %collective-permute-done.rest_0_), channel_id=1, source_target_pairs={{0,8},{4,12},{8,16},{12,20},{16,24},{20,28},{24,0},{28,4},{1,9},{5... | collective-permute-start | bytes 393224 | tf_op jit(solution)/shard_map/ppermute | solution.py:18
  12.0 16.7 %copy-start.3 = (bf16[256,256]{1,0:T(8,128)(2,1)}, bf16[256,256]{1,0:T(8,128)(2,1)S(1)}, u32[]{:S(2)}) copy-start(bf16[256,256]{1,0:T(8,128)(2,1)S(1)} %collective-permute-done.1.rest_1_) | copy-start | bytes 393220
  12.0 9.1 %collective-permute-start.3 = (bf16[256,256]{1,0:T(8,128)(2,1)S(1)}, bf16[256,256]{1,0:T(8,128)(2,1)S(1)}, u32[]{:S(2)}, u32[]{:S(2)}) collective-permute-start(bf16[256,256]{1,0:T(8,128)(2,1)S(1)} %collective-permute-done.1.rest_1_), channel_id=1, source_target_pairs={{0,8},{4,12},{8,16},{12,20},{16,24},{20,28},{24,0},{28,4},{1,9},{5... | collective-permute-start | bytes 393224 | tf_op jit(solution)/shard_map/ppermute | solution.py:18
  13.5 7.5 %collective-permute-start.4 = (bf16[256,256]{1,0:T(8,128)(2,1)S(1)}, bf16[256,256]{1,0:T(8,128)(2,1)S(1)}, u32[]{:S(2)}, u32[]{:S(2)}) collective-permute-start(bf16[256,256]{1,0:T(8,128)(2,1)S(1)} %collective-permute-done.rest_0_), channel_id=1, source_target_pairs={{0,1},{1,0},{2,3},{3,2},{4,5},{5,4},{6,7},{7,6},{8,9},{9,8},{10,11... | collective-permute-start | bytes 393224 | tf_op jit(solution)/shard_map/ppermute | solution.py:23
  17.6 28.1 %copy-start.10 = (bf16[256,256]{1,0:T(8,128)(2,1)}, bf16[256,256]{1,0:T(8,128)(2,1)S(1)}, u32[]{:S(2)}) copy-start(bf16[256,256]{1,0:T(8,128)(2,1)S(1)} %collective-permute-done.8.rest_0_) | copy-start | bytes 393220
  17.6 4.6 %collective-permute-start.5 = (bf16[256,256]{1,0:T(8,128)(2,1)S(1)}, bf16[256,256]{1,0:T(8,128)(2,1)S(1)}, u32[]{:S(2)}, u32[]{:S(2)}) collective-permute-start(bf16[256,256]{1,0:T(8,128)(2,1)S(1)} %collective-permute-done.1.rest_1_), channel_id=1, source_target_pairs={{0,1},{1,0},{2,3},{3,2},{4,5},{5,4},{6,7},{7,6},{8,9},{9,8},{10,11... | collective-permute-start | bytes 393224 | tf_op jit(solution)/shard_map/ppermute | solution.py:23
  17.6 28.1 %copy-start.11 = (bf16[256,256]{1,0:T(8,128)(2,1)}, bf16[256,256]{1,0:T(8,128)(2,1)S(1)}, u32[]{:S(2)}) copy-start(bf16[256,256]{1,0:T(8,128)(2,1)S(1)} %collective-permute-done.9.rest_1_) | copy-start | bytes 393220
  17.6 8.1 %collective-permute-start.10 = (bf16[256,256]{1,0:T(8,128)(2,1)S(1)}, bf16[256,256]{1,0:T(8,128)(2,1)S(1)}, u32[]{:S(2)}, u32[]{:S(2)}) collective-permute-start(bf16[256,256]{1,0:T(8,128)(2,1)S(1)} %collective-permute-done.8.rest_0_), channel_id=1, source_target_pairs={{0,8},{4,12},{8,16},{12,20},{16,24},{20,28},{24,0},{28,4},{1,9},{5... | collective-permute-start | bytes 393224 | tf_op jit(solution)/shard_map/ppermute | solution.py:18
  19.6 9.0 %copy-start.4 = (bf16[256,256]{1,0:T(8,128)(2,1)}, bf16[256,256]{1,0:T(8,128)(2,1)S(1)}, u32[]{:S(2)}) copy-start(bf16[256,256]{1,0:T(8,128)(2,1)S(1)} %collective-permute-done.2.rest_2_) | copy-start | bytes 393220
  19.6 8.5 %collective-permute-start.11 = (bf16[256,256]{1,0:T(8,128)(2,1)S(1)}, bf16[256,256]{1,0:T(8,128)(2,1)S(1)}, u32[]{:S(2)}, u32[]{:S(2)}) collective-permute-start(bf16[256,256]{1,0:T(8,128)(2,1)S(1)} %collective-permute-done.9.rest_1_), channel_id=1, source_target_pairs={{0,8},{4,12},{8,16},{12,20},{16,24},{20,28},{24,0},{28,4},{1,9},{5... | collective-permute-start | bytes 393224 | tf_op jit(solution)/shard_map/ppermute | solution.py:18
  21.0 7.6 %copy-start.5 = (bf16[256,256]{1,0:T(8,128)(2,1)}, bf16[256,256]{1,0:T(8,128)(2,1)S(1)}, u32[]{:S(2)}) copy-start(bf16[256,256]{1,0:T(8,128)(2,1)S(1)} %collective-permute-done.3.rest_3_) | copy-start | bytes 393220
  21.0 7.1 %collective-permute-start.6 = (bf16[256,256]{1,0:T(8,128)(2,1)S(1)}, bf16[256,256]{1,0:T(8,128)(2,1)S(1)}, u32[]{:S(2)}, u32[]{:S(2)}) collective-permute-start(bf16[256,256]{1,0:T(8,128)(2,1)S(1)} %collective-permute-done.2.rest_2_), channel_id=1, source_target_pairs={{0,1},{1,0},{2,3},{3,2},{4,5},{5,4},{6,7},{7,6},{8,9},{9,8},{10,11... | collective-permute-start | bytes 393224 | tf_op jit(solution)/shard_map/ppermute | solution.py:23
  21.0 7.6 %copy-start.6 = (bf16[256,256]{1,0:T(8,128)(2,1)}, bf16[256,256]{1,0:T(8,128)(2,1)S(1)}, u32[]{:S(2)}) copy-start(bf16[256,256]{1,0:T(8,128)(2,1)S(1)} %collective-permute-done.4.rest_4_) | copy-start | bytes 393220
  21.1 7.6 %collective-permute-start.7 = (bf16[256,256]{1,0:T(8,128)(2,1)S(1)}, bf16[256,256]{1,0:T(8,128)(2,1)S(1)}, u32[]{:S(2)}, u32[]{:S(2)}) collective-permute-start(bf16[256,256]{1,0:T(8,128)(2,1)S(1)} %collective-permute-done.3.rest_3_), channel_id=1, source_target_pairs={{0,1},{1,0},{2,3},{3,2},{4,5},{5,4},{6,7},{7,6},{8,9},{9,8},{10,11... | collective-permute-start | bytes 393224 | tf_op jit(solution)/shard_map/ppermute | solution.py:23
  22.2 6.5 %copy-start.7 = (bf16[256,256]{1,0:T(8,128)(2,1)}, bf16[256,256]{1,0:T(8,128)(2,1)S(1)}, u32[]{:S(2)}) copy-start(bf16[256,256]{1,0:T(8,128)(2,1)S(1)} %collective-permute-done.5.rest_5_) | copy-start | bytes 393220
  22.2 24.1 %collective-permute-start.12 = (bf16[256,256]{1,0:T(8,128)(2,1)S(1)}, bf16[256,256]{1,0:T(8,128)(2,1)S(1)}, u32[]{:S(2)}, u32[]{:S(2)}) collective-permute-start(bf16[256,256]{1,0:T(8,128)(2,1)S(1)} %collective-permute-done.8.rest_0_), channel_id=1, source_target_pairs={{0,1},{1,0},{2,3},{3,2},{4,5},{5,4},{6,7},{7,6},{8,9},{9,8},{10,11... | collective-permute-start | bytes 393224 | tf_op jit(solution)/shard_map/ppermute | solution.py:23
  25.7 20.0 %copy-start.12 = (bf16[256,256]{1,0:T(8,128)(2,1)}, bf16[256,256]{1,0:T(8,128)(2,1)S(1)}, u32[]{:S(2)}) copy-start(bf16[256,256]{1,0:T(8,128)(2,1)S(1)} %collective-permute-done.10.rest_2_) | copy-start | bytes 393220
  25.7 20.5 %collective-permute-start.13 = (bf16[256,256]{1,0:T(8,128)(2,1)S(1)}, bf16[256,256]{1,0:T(8,128)(2,1)S(1)}, u32[]{:S(2)}, u32[]{:S(2)}) collective-permute-start(bf16[256,256]{1,0:T(8,128)(2,1)S(1)} %collective-permute-done.9.rest_1_), channel_id=1, source_target_pairs={{0,1},{1,0},{2,3},{3,2},{4,5},{5,4},{6,7},{7,6},{8,9},{9,8},{10,11... | collective-permute-start | bytes 393224 | tf_op jit(solution)/shard_map/ppermute | solution.py:23
  28.1 17.6 %copy-start.13 = (bf16[256,256]{1,0:T(8,128)(2,1)}, bf16[256,256]{1,0:T(8,128)(2,1)S(1)}, u32[]{:S(2)}) copy-start(bf16[256,256]{1,0:T(8,128)(2,1)S(1)} %collective-permute-done.11.rest_3_) | copy-start | bytes 393220
  28.1 18.2 %collective-permute-start.14 = (bf16[256,256]{1,0:T(8,128)(2,1)S(1)}, bf16[256,256]{1,0:T(8,128)(2,1)S(1)}, u32[]{:S(2)}, u32[]{:S(2)}) collective-permute-start(bf16[256,256]{1,0:T(8,128)(2,1)S(1)} %collective-permute-done.10.rest_2_), channel_id=1, source_target_pairs={{0,1},{1,0},{2,3},{3,2},{4,5},{5,4},{6,7},{7,6},{8,9},{9,8},{10,11... | collective-permute-start | bytes 393224 | tf_op jit(solution)/shard_map/ppermute | solution.py:23
  28.1 0.7 copy-start.8
  28.1 18.2 %collective-permute-start.15 = (bf16[256,256]{1,0:T(8,128)(2,1)S(1)}, bf16[256,256]{1,0:T(8,128)(2,1)S(1)}, u32[]{:S(2)}, u32[]{:S(2)}) collective-permute-start(bf16[256,256]{1,0:T(8,128)(2,1)S(1)} %collective-permute-done.11.rest_3_), channel_id=1, source_target_pairs={{0,1},{1,0},{2,3},{3,2},{4,5},{5,4},{6,7},{7,6},{8,9},{9,8},{10,11... | collective-permute-start | bytes 393224 | tf_op jit(solution)/shard_map/ppermute | solution.py:23
  28.8 0.7 copy-start.9
  45.7 17.5 %collective-permute-start.23 = (bf16[5,256,256]{2,1,0:T(8,128)(2,1)}, bf16[5,256,256]{2,1,0:T(8,128)(2,1)S(1)}, u32[]{:S(2)}, u32[]{:S(2)}) collective-permute-start(bf16[5,256,256]{2,1,0:T(8,128)(2,1)} %get-tuple-element.18), channel_id=1, source_target_pairs={{0,1},{1,0},{2,3},{3,2},{4,5},{5,4},{6,7},{7,6},{8,9},{9,8},{10,11... | collective-permute-start | bytes 1966088 | tf_op jit(solution)/shard_map/ppermute | solution.py:23
  46.3 0.6 copy-start.14
  46.3 0.7 copy-start.15
  46.3 0.7 copy-start.16
  46.3 0.8 copy-start.17
  47.1 16.1 %copy-start.1 = (f32[5,256,256]{2,1,0:T(8,128)S(1)}, f32[5,256,256]{2,1,0:T(8,128)}, u32[]{:S(2)}) copy-start(f32[5,256,256]{2,1,0:T(8,128)} %get-tuple-element.17) | copy-start | bytes 3932164
  63.1 2.4 %collective-permute-start.16 = (bf16[5,256,256]{2,1,0:T(8,128)(2,1)}, bf16[5,256,256]{2,1,0:T(8,128)(2,1)S(1)}, u32[]{:S(2)}, u32[]{:S(2)}) collective-permute-start(bf16[5,256,256]{2,1,0:T(8,128)(2,1)} %get-tuple-element.16), channel_id=1, source_target_pairs={{0,1},{1,0},{2,3},{3,2},{4,5},{5,4},{6,7},{7,6},{8,9},{9,8},{10,11... | collective-permute-start | bytes 1966088 | tf_op jit(solution)/shard_map/ppermute | solution.py:23
  63.2 2.3 %copy-start = (f32[5,256,256]{2,1,0:T(8,128)S(1)}, f32[5,256,256]{2,1,0:T(8,128)}, u32[]{:S(2)}) copy-start(f32[5,256,256]{2,1,0:T(8,128)} %get-tuple-element.15) | copy-start | bytes 3932164
  63.4 6.4 %collective-permute-start.24 = (bf16[256,256]{1,0:T(8,128)(2,1)S(1)}, bf16[256,256]{1,0:T(8,128)(2,1)S(1)}, u32[]{:S(2)}, u32[]{:S(2)}) collective-permute-start(bf16[256,256]{1,0:T(8,128)(2,1)S(1)} %get-tuple-element.27), channel_id=1, source_target_pairs={{0,24},{4,28},{8,0},{12,4},{16,8},{20,12},{24,16},{28,20},{1,25},{... | collective-permute-start | bytes 393224 | tf_op jit(solution)/shard_map/ppermute | solution.py:18
  63.7 8.9 %collective-permute-start.26 = (bf16[256,256]{1,0:T(8,128)(2,1)S(1)}, bf16[256,256]{1,0:T(8,128)(2,1)S(1)}, u32[]{:S(2)}, u32[]{:S(2)}) collective-permute-start(bf16[256,256]{1,0:T(8,128)(2,1)S(1)} %get-tuple-element.28), channel_id=1, source_target_pairs={{0,24},{4,28},{8,0},{12,4},{16,8},{20,12},{24,16},{28,20},{1,25},{... | collective-permute-start | bytes 393224 | tf_op jit(solution)/shard_map/ppermute | solution.py:18
  65.7 13.3 %collective-permute-start.17 = (bf16[256,256]{1,0:T(8,128)(2,1)S(1)}, bf16[256,256]{1,0:T(8,128)(2,1)S(1)}, u32[]{:S(2)}, u32[]{:S(2)}) collective-permute-start(bf16[256,256]{1,0:T(8,128)(2,1)S(1)} %get-tuple-element.29), channel_id=1, source_target_pairs={{0,24},{4,28},{8,0},{12,4},{16,8},{20,12},{24,16},{28,20},{1,25},{... | collective-permute-start | bytes 393224 | tf_op jit(solution)/shard_map/ppermute | solution.py:18
  66.0 13.0 %collective-permute-start.19 = (bf16[256,256]{1,0:T(8,128)(2,1)S(1)}, bf16[256,256]{1,0:T(8,128)(2,1)S(1)}, u32[]{:S(2)}, u32[]{:S(2)}) collective-permute-start(bf16[256,256]{1,0:T(8,128)(2,1)S(1)} %get-tuple-element.30), channel_id=1, source_target_pairs={{0,24},{4,28},{8,0},{12,4},{16,8},{20,12},{24,16},{28,20},{1,25},{... | collective-permute-start | bytes 393224 | tf_op jit(solution)/shard_map/ppermute | solution.py:18
  72.7 11.9 %collective-permute-start.25 = (bf16[256,256]{1,0:T(8,128)(2,1)S(1)}, bf16[256,256]{1,0:T(8,128)(2,1)S(1)}, u32[]{:S(2)}, u32[]{:S(2)}) collective-permute-start(bf16[256,256]{1,0:T(8,128)(2,1)S(1)} %get-tuple-element.23), channel_id=1, source_target_pairs={{0,24},{4,28},{8,0},{12,4},{16,8},{20,12},{24,16},{28,20},{1,25},{... | collective-permute-start | bytes 393224 | tf_op jit(solution)/shard_map/ppermute | solution.py:18
  74.7 9.9 %collective-permute-start.27 = (bf16[256,256]{1,0:T(8,128)(2,1)S(1)}, bf16[256,256]{1,0:T(8,128)(2,1)S(1)}, u32[]{:S(2)}, u32[]{:S(2)}) collective-permute-start(bf16[256,256]{1,0:T(8,128)(2,1)S(1)} %get-tuple-element.24), channel_id=1, source_target_pairs={{0,28},{4,0},{8,4},{12,8},{16,12},{20,16},{24,20},{28,24},{1,29},{... | collective-permute-start | bytes 393224 | tf_op jit(solution)/shard_map/ppermute | solution.py:18
  79.0 7.3 %collective-permute-start.18 = (bf16[256,256]{1,0:T(8,128)(2,1)S(1)}, bf16[256,256]{1,0:T(8,128)(2,1)S(1)}, u32[]{:S(2)}, u32[]{:S(2)}) collective-permute-start(bf16[256,256]{1,0:T(8,128)(2,1)S(1)} %get-tuple-element.25), channel_id=1, source_target_pairs={{0,24},{4,28},{8,0},{12,4},{16,8},{20,12},{24,16},{28,20},{1,25},{... | collective-permute-start | bytes 393224 | tf_op jit(solution)/shard_map/ppermute | solution.py:18
  80.3 7.7 %collective-permute-start.20 = (bf16[256,256]{1,0:T(8,128)(2,1)S(1)}, bf16[256,256]{1,0:T(8,128)(2,1)S(1)}, u32[]{:S(2)}, u32[]{:S(2)}) collective-permute-start(bf16[256,256]{1,0:T(8,128)(2,1)S(1)} %get-tuple-element.26), channel_id=1, source_target_pairs={{0,28},{4,0},{8,4},{12,8},{16,12},{20,16},{24,20},{28,24},{1,29},{... | collective-permute-start | bytes 393224 | tf_op jit(solution)/shard_map/ppermute | solution.py:18
  84.6 5.6 %collective-permute-start.28 = (bf16[256,256]{1,0:T(8,128)(2,1)S(1)}, bf16[256,256]{1,0:T(8,128)(2,1)S(1)}, u32[]{:S(2)}, u32[]{:S(2)}) collective-permute-start(bf16[256,256]{1,0:T(8,128)(2,1)S(1)} %fusion.6), channel_id=1, source_target_pairs={{0,2},{1,3},{2,0},{3,1},{4,6},{5,7},{6,4},{7,5},{8,10},{9,11},{10,... | collective-permute-start | bytes 393224 | tf_op jit(solution)/shard_map/ppermute | solution.py:23
  88.1 11.1 %collective-permute-start.21 = (bf16[256,256]{1,0:T(8,128)(2,1)S(1)}, bf16[256,256]{1,0:T(8,128)(2,1)S(1)}, u32[]{:S(2)}, u32[]{:S(2)}) collective-permute-start(bf16[256,256]{1,0:T(8,128)(2,1)S(1)} %fusion.13), channel_id=1, source_target_pairs={{0,2},{1,3},{2,0},{3,1},{4,6},{5,7},{6,4},{7,5},{8,10},{9,11},{10,... | collective-permute-start | bytes 393224 | tf_op jit(solution)/shard_map/ppermute | solution.py:23
  90.3 9.5 %collective-permute-start.29 = (f32[256,256]{1,0:T(8,128)S(1)}, f32[256,256]{1,0:T(8,128)S(1)}, u32[]{:S(2)}, u32[]{:S(2)}) collective-permute-start(f32[256,256]{1,0:T(8,128)S(1)} %convert_add_fusion.2), channel_id=1, source_target_pairs={{0,1},{1,0},{2,3},{3,2},{4,5},{5,4},{6,7},{7,6},{8,9},{9,8},{10,11... | collective-permute-start | bytes 786440 | tf_op jit(solution)/shard_map/ppermute | solution.py:23
  99.2 1.7 %collective-permute-start.22 = (f32[256,256]{1,0:T(8,128)S(1)}, f32[256,256]{1,0:T(8,128)S(1)}, u32[]{:S(2)}, u32[]{:S(2)}) collective-permute-start(f32[256,256]{1,0:T(8,128)S(1)} %convert_add_fusion.3), channel_id=1, source_target_pairs={{0,1},{1,0},{2,3},{3,2},{4,5},{5,4},{6,7},{7,6},{8,9},{9,8},{10,11... | collective-permute-start | bytes 786440 | tf_op jit(solution)/shard_map/ppermute | solution.py:23
where the time goes:
time: 102 us
  Pallas kernels  41 us (40%)
  starting transfers between devices  30.4 us (30%)
  waiting for transfers between devices  22.9 us (22%)
  local copies, waits for them, and re-layouts  3.49 us (3%)
  other arithmetic  3.07 us (3%)
    ppermute x16, starting transfers between devices, along_seq(): return lax.ppermute(block, 'seq', route)  24.9 us
    ppermute x16, waiting for transfers between devices, along_seq(): return lax.ppermute(block, 'seq', route)  20.7 us
    pallas_call x1, Pallas kernels, on_device(): call(probs_kernel, 'probs', 2, in_specs=[smem, by_head, by_head] + [hbm]...  16.2 us
    pallas_call x1, Pallas kernels, on_device(): call(dscores_kernel, 'dscores', 2, in_specs=[smem, by_head, by_head, row,...  16 us
    pallas_call x1, Pallas kernels, on_device(): call(dquery_kernel, 'dquery', 1, in_specs=[smem, tiles] + [hbm] * (2 * re...  8.81 us
    ppermute x14, starting transfers between devices, swap_heads(): return lax.ppermute(block, 'head', route)  5.45 us
    ppermute x14, waiting for transfers between devices, swap_heads(): return lax.ppermute(block, 'head', route)  2.22 us
  transfers between devices with their start and end apart: 30, of which 13 were waited for; matrix products, arithmetic and copies ran while one was open for 3% of the time, Pallas kernels for 40%

commit v1 on v0

v1 whole, which is shorter than its diff:
```python
import functools

import jax
import jax.numpy as jnp
from jax import lax
from jax.experimental import pallas as pl
from jax.experimental.pallas import tpu as pltpu
from jax.sharding import PartitionSpec as P

WINDOW = 2048
LOW = -1e30
VMEM_BYTES = 18 * 1024 * 1024


def along_seq(block, near, step):
    shards, group = lax.axis_size("seq"), lax.axis_size("head")
    route = []
    for shard in range(shards):
        for member in range(group):
            target = (shard + near + (member % 2) * step) % shards
            route.append((shard * group + member, target * group + member))
    return lax.ppermute(block, ("seq", "head"), route)


def swap_heads(block, bit):
    route = [(i, i ^ bit) for i in range(lax.axis_size("head"))]
    return lax.ppermute(block, "head", route)


def dot_t(left, right):
    return lax.dot_general(
        left, right, (((1,), (1,)), ((), ())), preferred_element_type=jnp.float32
    )


def dot(left, right):
    return jnp.dot(left, right, preferred_element_type=jnp.float32)


def fold_rows(block, total, combine):
    rows = total.shape[0]
    for first in range(0, block.shape[0], rows):
        total = combine(total, block[first : first + rows])
    return total


def lower_mask(half):
    keys = lax.broadcasted_iota(jnp.int32, (half, half), 0)
    queries = lax.broadcasted_iota(jnp.int32, (half, half), 1)
    return queries >= keys


def load_rows(own_ref, mine_refs, other_refs, ext, sem, core, full, reach):
    copies = [pltpu.make_async_copy(own_ref, ext.at[pl.ds(reach * full, full)], sem.at[0])]
    for j in range(reach // 2):
        first = pl.multiple_of((reach - 1 - 2 * j - core) * full, full)
        other = pl.multiple_of((reach - 2 - 2 * j + core) * full, full)
        copies.append(
            pltpu.make_async_copy(mine_refs[j], ext.at[pl.ds(first, full)], sem.at[2 * j + 1])
        )
        copies.append(
            pltpu.make_async_copy(other_refs[j], ext.at[pl.ds(other, full)], sem.at[2 * j + 2])
        )
    for each in copies:
        each.start()
    return copies


def unit_product(unit, ext, rows, half, reach, mask, far_bias=None):
    own = reach * 2 * half
    if unit >= 2:
        return dot_t(ext[unit * half : (unit + 1) * half], rows)
    if unit == 0:
        near = dot_t(ext[own : own + half], rows)
        far = dot_t(ext[:half], rows[:half])
        if far_bias is not None:
            far = far + far_bias
        return jnp.concatenate([jnp.where(mask, near[:, :half], far), near[:, half:]], axis=1)
    near = dot_t(ext[own + half : own + 2 * half], rows[half:])
    far = dot_t(ext[half : 2 * half], rows)
    if far_bias is not None:
        far = far + far_bias
    return jnp.concatenate([far[:, :half], jnp.where(mask, near, far[:, half:])], axis=1)


def unit_add(unit, tile, acc, rows, half, reach, mask):
    own = reach * 2 * half
    if unit >= 2:
        acc[unit * half : (unit + 1) * half] += dot(tile, rows)
        return
    left, right = tile[:, :half], tile[:, half:]
    zero = jnp.zeros_like(left)
    if unit == 0:
        both = jnp.concatenate([jnp.where(mask, left, zero), right], axis=1)
        acc[own : own + half] += dot(both, rows)
        acc[:half] += dot(jnp.where(mask, zero, left), rows[:half])
        return
    acc[own + half : own + 2 * half] += dot(jnp.where(mask, right, zero), rows[half:])
    both = jnp.concatenate([left, jnp.where(mask, zero, right)], axis=1)
    acc[half : 2 * half] += dot(both, rows)


def split_out(acc, own_ref, keep_ref, send_ref, core, full, reach):
    own_ref[...] = acc[reach * full :]
    for j in range(reach // 2):
        first = pl.multiple_of((reach - 1 - 2 * j - core) * full, full)
        other = pl.multiple_of((reach - 2 - 2 * j + core) * full, full)
        keep_ref[j] = acc[pl.ds(first, full), :]
        send_ref[j] = acc[pl.ds(other, full), :].astype(send_ref.dtype)


def probs_kernel(reach, scale, place, first_ref, q_ref, g_ref, own_ref, *rest):
    mine_refs, other_refs, rest = rest[: reach // 2], rest[reach // 2 : reach], rest[reach:]
    e_ref, gs_ref, inv_ref, down_ref, keep_ref, send_ref, ext, s_buf, peak_buf, acc, sem = rest
    step, steps = pl.program_id(0), pl.num_programs(0)
    rank, core = place[0], place[1]
    full = own_ref.shape[0]
    half = full // 2
    units = 2 * reach
    mask = lower_mask(half)
    far_bias = jnp.where(rank >= reach, 0.0, LOW).astype(jnp.float32)

    def score(unit, rows, peak):
        block = unit_product(unit, ext, rows, half, reach, mask, far_bias)
        s_buf[unit * half : (unit + 1) * half] = block
        part = fold_rows(block, jnp.full((16, full), LOW, jnp.float32), jnp.maximum)
        if unit >= 2:
            part = jnp.where(rank >= reach - unit // 2, part, LOW)
        return jnp.maximum(peak, part)

    lowest = jnp.full((16, full), LOW, jnp.float32)

    @pl.when(step == 0)
    def _():
        copies = load_rows(own_ref, mine_refs, other_refs, ext, sem, core, full, reach)
        acc[...] = jnp.zeros_like(acc)
        for each in copies:
            each.wait()
        rows = first_ref[...] * jnp.asarray(scale, q_ref.dtype)
        peak = lowest
        for unit in range(units):
            peak = score(unit, rows, peak)
        peak_buf[...] = peak

    rows = q_ref[...] * jnp.asarray(scale, q_ref.dtype)
    level = jnp.max(peak_buf[...], axis=0, keepdims=True)
    total = jnp.zeros((16, full), jnp.float32)
    peak = lowest
    for unit in range(units):
        d = reach - unit // 2
        at = slice(unit * half, (unit + 1) * half)
        high = level if unit < 2 else jnp.where(rank >= d, level, -LOW)
        expo = jnp.exp(s_buf[at] - high)
        total = fold_rows(expo, total, jnp.add)
        e_ref[step, at] = expo.astype(jnp.bfloat16)
        peak = score(unit, rows, peak)
    peak_buf[...] = peak
    inv = 1.0 / jnp.sum(total, axis=0, keepdims=True)
    inv_rows = jnp.broadcast_to(inv, (8, full))
    inv_ref[0] = inv_rows
    scaled = (g_ref[...].astype(jnp.float32) * jnp.transpose(inv_rows)[:, :1]).astype(jnp.bfloat16)
    gs_ref[...] = scaled
    for unit in range(units):
        at = slice(unit * half, (unit + 1) * half)
        unit_add(unit, e_ref[step, at], acc, scaled, half, reach, mask)

    @pl.when(step == steps - 1)
    def _():
        split_out(acc, down_ref, keep_ref, send_ref, core, full, reach)


def dscores_kernel(reach, scale, place, first_ref, first_inv, q_ref, gs_ref, *rest):
    inv_ref, e_ref, own_ref, rest = rest[0], rest[1], rest[2], rest[3:]
    mine_refs, other_refs, rest = rest[: reach // 2], rest[reach // 2 : reach], rest[reach:]
    ds_ref, down_ref, keep_ref, send_ref, ext, dp_buf, delta_buf, acc, sem = rest
    step, steps = pl.program_id(0), pl.num_programs(0)
    core = place[1]
    full = own_ref.shape[0]
    half = full // 2
    units = 2 * reach
    mask = lower_mask(half)

    def product(unit, grads, probs, total):
        at = slice(unit * half, (unit + 1) * half)
        block = unit_product(unit, ext, grads, half, reach, mask)
        dp_buf[at] = block
        return fold_rows(block * probs.astype(jnp.float32), total, jnp.add)

    def keep_delta(total, inv):
        delta_buf[...] = jnp.broadcast_to(
            jnp.sum(total, axis=0, keepdims=True) * inv, delta_buf.shape
        )

    nothing = jnp.zeros((16, full), jnp.float32)

    @pl.when(step == 0)
    def _():
        copies = load_rows(own_ref, mine_refs, other_refs, ext, sem, core, full, reach)
        acc[...] = jnp.zeros_like(acc)
        for each in copies:
            each.wait()
        grads = first_ref[...]
        total = nothing
        for unit in range(units):
            total = product(unit, grads, e_ref[0, unit * half : (unit + 1) * half], total)
        keep_delta(total, first_inv[0, :1])

    rows = q_ref[...] * jnp.asarray(scale, q_ref.dtype)
    grads = gs_ref[...]
    following = jnp.minimum(step + 1, steps - 1)
    delta = delta_buf[:1]
    total = nothing
    for unit in range(units):
        at = slice(unit * half, (unit + 1) * half)
        tile = (e_ref[step, at].astype(jnp.float32) * (dp_buf[at] - delta)).astype(jnp.bfloat16)
        ds_ref[step, at] = tile
        unit_add(unit, tile, acc, rows, half, reach, mask)
        total = product(unit, grads, e_ref[following, at], total)
    keep_delta(total, inv_ref[0, :1])

    @pl.when(step == steps - 1)
    def _():
        split_out(acc, down_ref, keep_ref, send_ref, core, full, reach)


def dot_first(left, right):
    return lax.dot_general(
        left, right, (((0,), (0,)), ((), ())), preferred_element_type=jnp.float32
    )


def dquery_kernel(reach, scale, place, ds_ref, own_ref, *rest):
    mine_refs, other_refs, rest = rest[: reach // 2], rest[reach // 2 : reach], rest[reach:]
    dq_ref, ext, sem = rest
    core = place[1]
    full = own_ref.shape[0]
    half = full // 2
    head = pl.program_id(0)

    @pl.when(pl.program_id(0) == 0)
    def _():
        copies = load_rows(own_ref, mine_refs, other_refs, ext, sem, core, full, reach)
        for each in copies:
            each.wait()

    mask = lower_mask(half)
    zero = jnp.zeros((half, half), jnp.bfloat16)
    own = reach * full
    lo_lo, lo_hi = ds_ref[head, :half, :half], ds_ref[head, :half, half:]
    hi_lo, hi_hi = ds_ref[head, half:full, :half], ds_ref[head, half:full, half:]
    lo = (
        dot_first(jnp.where(mask, lo_lo, zero), ext[own : own + half])
        + dot_first(jnp.where(mask, zero, lo_lo), ext[:half])
        + dot_first(hi_lo, ext[half:full])
    )
    hi = (
        dot_first(lo_hi, ext[own : own + half])
        + dot_first(jnp.where(mask, hi_hi, zero), ext[own + half : own + full])
        + dot_first(jnp.where(mask, zero, hi_hi), ext[half:full])
    )
    total = dot_first(ds_ref[head, full:own], ext[full:own])
    dq_ref[:half] = ((lo + total[:half]) * scale).astype(dq_ref.dtype)
    dq_ref[half:] = ((hi + total[half:]) * scale).astype(dq_ref.dtype)


def gather_relayed(rows, reach):
    mine = [along_seq(rows, 1, 1)]
    for _ in range(1, reach // 2):
        mine.append(along_seq(mine[-1], 2, 0))
    return mine, [swap_heads(block, 1) for block in mine]


def gather_direct(rows, reach):
    return [along_seq(rows, 2 * j + 1, 1) for j in range(reach // 2)]


def pair_sums(keep, send):
    return keep + swap_heads(send, 1).astype(jnp.float32)


def return_direct(parts):
    return [
        along_seq(parts[j].astype(jnp.bfloat16), -2 * j - 1, -1) for j in range(len(parts))
    ]


def sum_heads(down, core):
    half = down.shape[0] // 2
    mine = jnp.where(core == 0, down[:half], down[half:])
    other = jnp.where(core == 0, down[half:], down[:half])
    own = mine + swap_heads(other.astype(jnp.bfloat16), 1).astype(jnp.float32)
    bit = 2
    while bit < lax.axis_size("head"):
        low = own.astype(jnp.bfloat16)
        own = low.astype(jnp.float32) + swap_heads(low, bit).astype(jnp.float32)
        bit *= 2
    other = swap_heads(own, 1)
    first = jnp.where(core == 0, own, other)
    second = jnp.where(core == 0, other, own)
    return jnp.concatenate([first, second], axis=0)


def on_device(query, key_rows, value_rows, grad_out):
    tok_rows, head_dim = key_rows.shape
    heads = query.shape[1] // head_dim
    reach = WINDOW // tok_rows
    half = tok_rows // 2
    scale = head_dim ** (-0.5)
    core = lax.axis_index("head") % 2
    place = jnp.stack([lax.axis_index("seq"), core]).astype(jnp.int32)
    ext_rows = (reach + 1) * tok_rows
    span = reach * tok_rows

    def following(h):
        return jnp.minimum(h + 1, heads - 1)

    smem = pl.BlockSpec(memory_space=pltpu.SMEM)
    vmem = pl.BlockSpec(memory_space=pltpu.VMEM)
    halo = [pl.BlockSpec(memory_space=pl.ANY)] * (reach + 1)
    by_head = pl.BlockSpec((tok_rows, head_dim), lambda h: (0, h))
    by_head_next = pl.BlockSpec((tok_rows, head_dim), lambda h: (0, following(h)))
    by_head_first = pl.BlockSpec((tok_rows, head_dim), lambda h: (0, 0))
    row = pl.BlockSpec((1, 8, tok_rows), lambda h: (h, 0, 0))
    row_next = pl.BlockSpec((1, 8, tok_rows), lambda h: (following(h), 0, 0))
    row_first = pl.BlockSpec((1, 8, tok_rows), lambda h: (0, 0, 0))
    down = pl.BlockSpec((tok_rows, head_dim), lambda h: (0, 0))
    whole = pl.BlockSpec((reach // 2, tok_rows, head_dim), lambda h: (0, 0, 0))
    tile_shape = jax.ShapeDtypeStruct((heads, span, tok_rows), jnp.bfloat16)
    down_shape = jax.ShapeDtypeStruct((tok_rows, head_dim), jnp.float32)
    keep_shape = jax.ShapeDtypeStruct((reach // 2, tok_rows, head_dim), jnp.float32)
    send_shape = jax.ShapeDtypeStruct((reach // 2, tok_rows, head_dim), jnp.bfloat16)
    ext = pltpu.VMEM((ext_rows, head_dim), jnp.bfloat16)
    acc = pltpu.VMEM((ext_rows, head_dim), jnp.float32)
    tile = pltpu.VMEM((span, tok_rows), jnp.float32)
    wide = pltpu.VMEM((16, tok_rows), jnp.float32)
    sems = pltpu.SemaphoreType.DMA((reach + 1,))
    product = 2 * heads * tok_rows * (reach * tok_rows + half) * head_dim

    def call(body, name, products, **spec):
        return pl.pallas_call(
            functools.partial(body, reach, scale),
            grid=(heads,),
            compiler_params=pltpu.CompilerParams(vmem_limit_bytes=VMEM_BYTES),
            cost_estimate=pl.CostEstimate(
                flops=products * product, bytes_accessed=16 * 2**20, transcendentals=0
            ),
            name=name,
            **spec,
        )

    keys_mine, keys_other = gather_relayed(key_rows, reach)
    values_mine = gather_direct(value_rows, reach)

    expo, grads, inv, dv_down, dv_keep, dv_send = call(
        probs_kernel,
        "probs",
        2,
        in_specs=[smem, by_head_first, by_head_next, by_head] + halo,
        out_specs=[vmem, by_head, row, down, whole, whole],
        out_shape=[
            tile_shape,
            jax.ShapeDtypeStruct(grad_out.shape, jnp.bfloat16),
            jax.ShapeDtypeStruct((heads, 8, tok_rows), jnp.float32),
            down_shape,
            keep_shape,
            send_shape,
        ],
        scratch_shapes=[ext, tile, wide, acc, sems],
    )(place, query, query, grad_out, key_rows, *keys_mine, *keys_other)

    values_mine, expo, dv_keep, dv_send = lax.optimization_barrier(
        (values_mine, expo, dv_keep, dv_send)
    )
    values_other = [swap_heads(block, 1) for block in values_mine]
    dv_parts = pair_sums(dv_keep, dv_send)
    dv_parts, expo = lax.optimization_barrier((dv_parts, expo))
    dv_back = return_direct(dv_parts)

    dscores, dk_down, dk_keep, dk_send = call(
        dscores_kernel,
        "dscores",
        2,
        in_specs=[smem, by_head_first, row_first, by_head, by_head_next, row_next, vmem] + halo,
        out_specs=[vmem, down, whole, whole],
        out_shape=[tile_shape, down_shape, keep_shape, send_shape],
        scratch_shapes=[ext, tile, wide, acc, sems],
    )(place, grads, inv, query, grads, inv, expo, value_rows, *values_mine, *values_other)

    dv_back, dk_keep, dk_send = lax.optimization_barrier((dv_back, dk_keep, dk_send))
    for block in dv_back:
        dv_down = dv_down + block.astype(jnp.float32)
    dk_parts = pair_sums(dk_keep, dk_send)
    dk_parts, dscores = lax.optimization_barrier((dk_parts, dscores))
    dk_back = along_seq(dk_parts[-1].astype(jnp.bfloat16), -2, 0)

    (grad_query,) = call(
        dquery_kernel,
        "dquery",
        1,
        in_specs=[smem, vmem] + halo,
        out_specs=[by_head],
        out_shape=[jax.ShapeDtypeStruct(query.shape, query.dtype)],
        scratch_shapes=[ext, sems],
    )(place, dscores, key_rows, *keys_mine, *keys_other)

    dk_back, grad_query = lax.optimization_barrier((dk_back, grad_query))
    for j in range(reach // 2 - 2, -1, -1):
        piece = (dk_parts[j] + dk_back.astype(jnp.float32)).astype(jnp.bfloat16)
        dk_back = along_seq(piece, -2, 0) if j else along_seq(piece, -1, -1)
    grad_value = sum_heads(dv_down, core)
    grad_key = sum_heads(dk_down + dk_back.astype(jnp.float32), core)
    return grad_query, grad_key, grad_value


def solution(mesh):
    return jax.shard_map(
        on_device,
        mesh=mesh,
        in_specs=(P("seq", "head"), P("seq", None), P("seq", None), P("seq", "head")),
        out_specs=(P("seq", "head"), P("seq", None), P("seq", None)),
        check_vma=False,
    )
```

time: 102 us -> 95.3 us (0.934)
  Pallas kernels: 41 us -> 24.3 us
  waiting for transfers between devices: 22.9 us -> 37.9 us
  starting transfers between devices: 30.4 us -> 17.6 us
  local copies, waits for them, and re-layouts: 3.49 us -> 10.8 us
    pallas_call x3, Pallas kernels: 41 us -> 24.3 us  [the longest x1 10.4 us: on_device(): call(probs_kernel, 'probs', 2, in_specs=[smem, by_head_first, by_head_nex...]
    ppermute x16 -> x8, starting transfers between devices: 24.9 us -> 13.9 us  [along_seq(): return lax.ppermute(block, ('seq', 'head'), route)]
    unnamed x36 -> x24, local copies, waits for them, and re-layouts: 1.62 us -> 10.1 us
    ppermute x14 -> x12, waiting for transfers between devices: 2.22 us -> 10.6 us  [swap_heads(): return lax.ppermute(block, 'head', route)]
    ppermute x16 -> x8, waiting for transfers between devices: 20.7 us -> 27.3 us  [along_seq(): return lax.ppermute(block, ('seq', 'head'), route)]
    dynamic_slice x2 -> x0, local copies, waits for them, and re-layouts: 1.83 us -> none  [gather_halo(): piece = lax.dynamic_slice_in_dim(rows, core * half, half, 0)]
    ppermute x14 -> x12, starting transfers between devices: 5.45 us -> 3.7 us  [swap_heads(): return lax.ppermute(block, 'head', route)]
  transfers between devices with their start and end apart: 30 -> 20, of which waited for: 13 -> 10; matrix products, arithmetic and copies ran while one was open for 3% -> 2% of each run, Pallas kernels for 40% -> 26%
where the time goes in v1:
time: 95.3 us; the launch traced here: 95 us
  waiting for transfers between devices  37.9 us (40%)
  Pallas kernels  24.3 us (25%)
  starting transfers between devices  17.6 us (18%)
  local copies, waits for them, and re-layouts  10.8 us (11%)
  other arithmetic  3.44 us (4%)
    ppermute x8, waiting for transfers between devices, along_seq(): return lax.ppermute(block, ('seq', 'head'), route)  27.3 us
    ppermute x8, starting transfers between devices, along_seq(): return lax.ppermute(block, ('seq', 'head'), route)  13.9 us
    ppermute x12, waiting for transfers between devices, swap_heads(): return lax.ppermute(block, 'head', route)  10.6 us
    pallas_call x1, Pallas kernels, on_device(): call(probs_kernel, 'probs', 2, in_specs=[smem, by_head_first, by_head_nex...  10.4 us
    unnamed x24, local copies, waits for them, and re-layouts  10.1 us
    pallas_call x1, Pallas kernels, on_device(): call(dscores_kernel, 'dscores', 2, in_specs=[smem, by_head_first, row_fir...  9.13 us
    pallas_call x1, Pallas kernels, on_device(): call(dquery_kernel, 'dquery', 1, in_specs=[smem, vmem] + halo, out_specs=...  4.81 us
    ppermute x12, starting transfers between devices, swap_heads(): return lax.ppermute(block, 'head', route)  3.7 us
  transfers between devices with their start and end apart: 20, of which 10 were waited for; matrix products, arithmetic and copies ran while one was open for 2% of the time, Pallas kernels for 26%

profile of v1, /device:TPU:0, one launch (start us, length us, event | category | flops | bytes accessed | tf_op | source)
XLA Modules:
  0.0 95.0 jit_solution(2957303825068625427)
XLA Ops:
  0.6 3.0 %collective-permute-start.2 = (bf16[512,256]{1,0:T(8,128)(2,1)}, bf16[512,256]{1,0:T(8,128)(2,1)S(1)}, u32[]{:S(2)}, u32[]{:S(2)}) collective-permute-start(bf16[512,256]{1,0:T(8,128)(2,1)} %own_ref.3), channel_id=1, source_target_pairs={{0,4},{1,9},{2,6},{3,11},{4,8},{5,13},{6,10},{7,15},{8,12},{9,17},... | collective-permute-start | bytes 786440 | tf_op jit(solution)/shard_map/ppermute | solution.py:22
  3.6 9.6 %collective-permute-done.2.rest_0_ = bf16[512,256]{1,0:T(8,128)(2,1)S(1)} collective-permute-done((bf16[512,256]{1,0:T(8,128)(2,1)}, bf16[512,256]{1,0:T(8,128)(2,1)S(1)}, u32[]{:S(2)}, u32[]{:S(2)}) %collective-permute-start.2) | collective-permute-done | bytes 262176 | tf_op jit(solution)/shard_map/ppermute | solution.py:22
  13.2 0.0 collective-permute-start.3
  13.2 0.0 collective-permute-start.4
  13.2 8.2 %collective-permute-done.3.rest_1_ = bf16[512,256]{1,0:T(8,128)(2,1)S(1)} collective-permute-done((bf16[512,256]{1,0:T(8,128)(2,1)S(1)}, bf16[512,256]{1,0:T(8,128)(2,1)S(1)}, u32[]{:S(2)}, u32[]{:S(2)}) %collective-permute-start.3) | collective-permute-done | bytes 262176 | tf_op jit(solution)/shard_map/ppermute | solution.py:22
  21.4 0.0 collective-permute-start.5
  21.4 0.5 collective-permute-start
  21.9 0.0 collective-permute-start.1
  21.9 0.1 pad_add_fusion.place
  22.0 0.0 collective-permute-done.4.rest_2_
  22.0 0.9 collective-permute-done.5.rest_3_
  22.9 0.9 copy-done.2
  23.9 1.2 %copy-done.4 = bf16[512,1024]{1,0:T(8,128)(2,1)S(1)} copy-done((bf16[512,1024]{1,0:T(8,128)(2,1)S(1)}, bf16[512,1024]{1,0:T(8,128)(2,1)}, u32[]{:S(2)}) %copy-start.4) | copy-done | bytes 1048600
  25.1 1.2 %copy-done.5 = bf16[512,1024]{1,0:T(8,128)(2,1)S(1)} copy-done((bf16[512,1024]{1,0:T(8,128)(2,1)S(1)}, bf16[512,1024]{1,0:T(8,128)(2,1)}, u32[]{:S(2)}) %copy-start.5) | copy-done | bytes 1048600
  26.3 10.4 %probs.1 = (bf16[4,2048,512]{2,1,0:T(8,128)(2,1)S(1)}, bf16[512,1024]{1,0:T(8,128)(2,1)S(1)}, f32[4,8,512]{2,1,0:T(8,128)S(1)}, f32[512,256]{1,0:T(8,128)S(1)}, ...) custom-call(s32[2]{0:T(128)S(1)} %pad_add_fusion.place, bf16[512,1024]{1,0:T(8,128)(2,1)S(1)} %copy-done.5, ...), custom_call_target="tpu_custom_call" | custom-call | flops 4831838208 | bytes 16777216 | tf_op jit(solution)/shard_map/probs/pallas_call | solution.py:354
  36.7 0.0 collective-permute-done.rest_3_
  36.7 5.2 %collective-permute-done.1.rest_4_ = bf16[512,256]{1,0:T(8,128)(2,1)S(1)} collective-permute-done((bf16[512,256]{1,0:T(8,128)(2,1)}, bf16[512,256]{1,0:T(8,128)(2,1)S(1)}, u32[]{:S(2)}, u32[]{:S(2)}) %collective-permute-start.1) | collective-permute-done | bytes 262176 | tf_op jit(solution)/shard_map/ppermute | solution.py:22
  42.0 0.0 collective-permute-start.6
  42.0 0.5 collective-permute-start.9
  42.5 0.0 collective-permute-start.10
  42.5 1.4 %collective-permute-done.6 = bf16[2,512,256]{2,1,0:T(8,128)(2,1)S(1)} collective-permute-done((bf16[2,512,256]{2,1,0:T(8,128)(2,1)S(1)}, bf16[2,512,256]{2,1,0:T(8,128)(2,1)S(1)}, u32[]{:S(2)}, u32[]{:S(2)}) %collective-permute-start.6) | collective-permute-done | bytes 524320 | tf_op jit(solution)/shard_map/ppermute | solution.py:27
  43.9 0.1 convert_add_fusion.1
  44.1 0.1 collective-permute-start.8
  44.1 1.0 %collective-permute-start.7 = (bf16[512,256]{1,0:T(8,128)(2,1)S(1)}, bf16[512,256]{1,0:T(8,128)(2,1)S(1)}, u32[]{:S(2)}, u32[]{:S(2)}) collective-permute-start(bf16[512,256]{1,0:T(8,128)(2,1)S(1)} %get-tuple-element.58), channel_id=1, source_target_pairs={{0,28},{1,25},{2,30},{3,27},{4,0},{5,29},{6,2},{7,31},{8,4},{9,1},... | collective-permute-start | bytes 786440 | tf_op jit(solution)/shard_map/ppermute | solution.py:22
  45.1 0.0 collective-permute-done.9.rest_5_
  45.1 0.0 collective-permute-done.10.rest_6_
  45.1 0.0 copy-done.6
  45.1 0.0 copy-done.7
  45.1 0.0 copy-start.3
  45.2 9.1 %dscores.1 = (bf16[4,2048,512]{2,1,0:T(8,128)(2,1)S(1)}, f32[512,256]{1,0:T(8,128)S(1)}, f32[2,512,256]{2,1,0:T(8,128)S(1)}, bf16[2,512,256]{2,1,0:T(8,128)(2,1)S(1)}) custom-call(s32[2]{0:T(128)S(1)} %pad_add_fusion.place, bf16[512,1024]{1,0:T(8,128)(2,1)S(1)} %get-tuple-element.35.first_ref.gs_ref, f32[4,8,512]{2,1,0:T(8,128)S(1)} %get-tuple-element.36.first_inv.rest_0_, ...), custom_call_target="tpu_custom_call" | custom-call | flops 4831838208 | bytes 16777216 | tf_op jit(solution)/shard_map/dscores/pallas_call | solution.py:379
  54.3 0.0 copy-start
  54.3 3.3 %copy-done = bf16[4,2048,512]{2,1,0:T(8,128)(2,1)} copy-done((bf16[4,2048,512]{2,1,0:T(8,128)(2,1)}, bf16[4,2048,512]{2,1,0:T(8,128)(2,1)S(1)}, u32[]{:S(2)}) %copy-start) | copy-done | bytes 8388632
  57.6 0.0 collective-permute-done.8
  57.6 0.0 collective-permute-done.7
  57.6 0.0 copy-start.10
  57.6 0.1 collective-permute-start.11
  57.7 1.9 %collective-permute-done.11 = bf16[2,512,256]{2,1,0:T(8,128)(2,1)S(1)} collective-permute-done((bf16[2,512,256]{2,1,0:T(8,128)(2,1)S(1)}, bf16[2,512,256]{2,1,0:T(8,128)(2,1)S(1)}, u32[]{:S(2)}, u32[]{:S(2)}) %collective-permute-start.11) | collective-permute-done | bytes 524320 | tf_op jit(solution)/shard_map/ppermute | solution.py:27
  59.6 0.1 convert_add_fusion
  59.7 0.0 copy-done.8
  59.7 0.0 copy-done.10
  59.7 0.7 fusion.1
  60.4 5.9 %collective-permute-start.12 = (bf16[512,256]{1,0:T(8,128)(2,1)}, bf16[512,256]{1,0:T(8,128)(2,1)}, u32[]{:S(2)}, u32[]{:S(2)}) collective-permute-start(bf16[512,256]{1,0:T(8,128)(2,1)} %fusion.1), channel_id=1, source_target_pairs={{0,24},{1,25},{2,26},{3,27},{4,28},{5,29},{6,30},{7,31},{8,0},{9,1... | collective-permute-start | bytes 786440 | tf_op jit(solution)/shard_map/ppermute | solution.py:22
  66.4 3.4 %copy-done.1 = bf16[4,2048,512]{2,1,0:T(8,128)(2,1)S(1)} copy-done((bf16[4,2048,512]{2,1,0:T(8,128)(2,1)S(1)}, bf16[4,2048,512]{2,1,0:T(8,128)(2,1)}, u32[]{:S(2)}) %copy-start.1) | copy-done | bytes 8388632
  69.8 4.8 %dquery.1 = bf16[512,1024]{1,0:T(8,128)(2,1)} custom-call(s32[2]{0:T(128)S(1)} %pad_add_fusion.place, bf16[4,2048,512]{2,1,0:T(8,128)(2,1)S(1)} %copy-done.1, bf16[512,256]{1,0:T(8,128)(2,1)S(1)} %copy-done.3, bf16[512,256]{1,0:T(8,128)(2,1)S(1)} %collective-permute-done.2.rest_0_, bf16[512,256]{1,0:T(8,128)(2,1)S(1)} %collective-permute-done.3.rest_1_, ...), custom_call_target="tpu_custom_call" | custom-call | flops 2415919104 | bytes 16777216 | tf_op jit(solution)/shard_map/dquery/pallas_call | solution.py:396
  74.6 0.0 collective-permute-done.12
  74.6 1.0 %fusion = bf16[512,256]{1,0:T(8,128)(2,1)S(1)} fusion(bf16[512,256]{1,0:T(8,128)(2,1)} %collective-permute-done.12, f32[2,512,256]{2,1,0:T(8,128)S(1)} %convert_add_fusion), kind=kLoop, calls=%fused_computation.6 | loop fusion | flops 393216 | bytes 1048576 | tf_op jit(solution)/shard_map/convert_element_type | solution.py:408
  75.6 3.3 %collective-permute-start.13 = (bf16[512,256]{1,0:T(8,128)(2,1)S(1)}, bf16[512,256]{1,0:T(8,128)(2,1)S(1)}, u32[]{:S(2)}, u32[]{:S(2)}) collective-permute-start(bf16[512,256]{1,0:T(8,128)(2,1)S(1)} %fusion), channel_id=1, source_target_pairs={{0,28},{1,25},{2,30},{3,27},{4,0},{5,29},{6,2},{7,31},{8,4},{9,1},... | collective-permute-start | bytes 786440 | tf_op jit(solution)/shard_map/ppermute | solution.py:22
  79.0 0.1 convert_add_fusion.2
  79.1 0.1 collective-permute-start.17
  79.2 4.3 %collective-permute-done.13 = bf16[512,256]{1,0:T(8,128)(2,1)S(1)} collective-permute-done((bf16[512,256]{1,0:T(8,128)(2,1)S(1)}, bf16[512,256]{1,0:T(8,128)(2,1)S(1)}, u32[]{:S(2)}, u32[]{:S(2)}) %collective-permute-start.13) | collective-permute-done | bytes 262176 | tf_op jit(solution)/shard_map/ppermute | solution.py:22
  83.4 0.1 convert_add_fusion.3
  83.5 0.1 collective-permute-start.14
  83.6 0.0 collective-permute-done.17
  83.7 1.6 %collective-permute-start.18 = (bf16[256,256]{1,0:T(8,128)(2,1)S(1)}, bf16[256,256]{1,0:T(8,128)(2,1)S(1)}, u32[]{:S(2)}, u32[]{:S(2)}) collective-permute-start(bf16[256,256]{1,0:T(8,128)(2,1)S(1)} %add_convert_fusion), channel_id=1, source_target_pairs={{0,2},{1,3},{2,0},{3,1},{4,6},{5,7},{6,4},{7,5},{8,10},{9,11},{10,... | collective-permute-start | bytes 393224 | tf_op jit(solution)/shard_map/ppermute | solution.py:27
  85.2 0.0 collective-permute-done.14
  85.3 1.3 %collective-permute-start.15 = (bf16[256,256]{1,0:T(8,128)(2,1)S(1)}, bf16[256,256]{1,0:T(8,128)(2,1)S(1)}, u32[]{:S(2)}, u32[]{:S(2)}) collective-permute-start(bf16[256,256]{1,0:T(8,128)(2,1)S(1)} %add_convert_fusion.1), channel_id=1, source_target_pairs={{0,2},{1,3},{2,0},{3,1},{4,6},{5,7},{6,4},{7,5},{8,10},{9,11},{10,... | collective-permute-start | bytes 393224 | tf_op jit(solution)/shard_map/ppermute | solution.py:27
  86.6 3.5 %collective-permute-done.18 = bf16[256,256]{1,0:T(8,128)(2,1)S(1)} collective-permute-done((bf16[256,256]{1,0:T(8,128)(2,1)S(1)}, bf16[256,256]{1,0:T(8,128)(2,1)S(1)}, u32[]{:S(2)}, u32[]{:S(2)}) %collective-permute-start.18) | collective-permute-done | bytes 131104 | tf_op jit(solution)/shard_map/ppermute | solution.py:27
  90.1 0.1 collective-permute-start.19
  90.2 2.3 %collective-permute-done.15 = bf16[256,256]{1,0:T(8,128)(2,1)S(1)} collective-permute-done((bf16[256,256]{1,0:T(8,128)(2,1)S(1)}, bf16[256,256]{1,0:T(8,128)(2,1)S(1)}, u32[]{:S(2)}, u32[]{:S(2)}) %collective-permute-start.15) | collective-permute-done | bytes 131104 | tf_op jit(solution)/shard_map/ppermute | solution.py:27
  92.5 0.1 collective-permute-start.16
  92.6 0.0 collective-permute-done.19
  92.6 0.8 pad_maximum_fusion.1
  93.5 0.6 collective-permute-done.16
  94.1 0.8 pad_maximum_fusion
  (21 shorter events, 0.4 us)
Async XLA Ops:
  0.6 12.6 %collective-permute-start.2 = (bf16[512,256]{1,0:T(8,128)(2,1)}, bf16[512,256]{1,0:T(8,128)(2,1)S(1)}, u32[]{:S(2)}, u32[]{:S(2)}) collective-permute-start(bf16[512,256]{1,0:T(8,128)(2,1)} %own_ref.3), channel_id=1, source_target_pairs={{0,4},{1,9},{2,6},{3,11},{4,8},{5,13},{6,10},{7,15},{8,12},{9,17},... | collective-permute-start | bytes 786440 | tf_op jit(solution)/shard_map/ppermute | solution.py:22
  13.2 8.2 %collective-permute-start.3 = (bf16[512,256]{1,0:T(8,128)(2,1)S(1)}, bf16[512,256]{1,0:T(8,128)(2,1)S(1)}, u32[]{:S(2)}, u32[]{:S(2)}) collective-permute-start(bf16[512,256]{1,0:T(8,128)(2,1)S(1)} %collective-permute-done.2.rest_0_), channel_id=1, source_target_pairs={{0,8},{1,9},{2,10},{3,11},{4,12},{5,13},{6,14},{7,15},{8,16},{9,17... | collective-permute-start | bytes 786440 | tf_op jit(solution)/shard_map/ppermute | solution.py:22
  13.2 8.8 %collective-permute-start.4 = (bf16[512,256]{1,0:T(8,128)(2,1)S(1)}, bf16[512,256]{1,0:T(8,128)(2,1)S(1)}, u32[]{:S(2)}, u32[]{:S(2)}) collective-permute-start(bf16[512,256]{1,0:T(8,128)(2,1)S(1)} %collective-permute-done.2.rest_0_), channel_id=1, source_target_pairs={{0,1},{1,0},{2,3},{3,2},{4,5},{5,4},{6,7},{7,6},{8,9},{9,8},{10,11... | collective-permute-start | bytes 786440 | tf_op jit(solution)/shard_map/ppermute | solution.py:27
  21.4 1.5 %collective-permute-start.5 = (bf16[512,256]{1,0:T(8,128)(2,1)S(1)}, bf16[512,256]{1,0:T(8,128)(2,1)S(1)}, u32[]{:S(2)}, u32[]{:S(2)}) collective-permute-start(bf16[512,256]{1,0:T(8,128)(2,1)S(1)} %collective-permute-done.3.rest_1_), channel_id=1, source_target_pairs={{0,1},{1,0},{2,3},{3,2},{4,5},{5,4},{6,7},{7,6},{8,9},{9,8},{10,11... | collective-permute-start | bytes 786440 | tf_op jit(solution)/shard_map/ppermute | solution.py:27
  21.4 15.3 %collective-permute-start = (bf16[512,256]{1,0:T(8,128)(2,1)}, bf16[512,256]{1,0:T(8,128)(2,1)S(1)}, u32[]{:S(2)}, u32[]{:S(2)}) collective-permute-start(bf16[512,256]{1,0:T(8,128)(2,1)} %rest_2_.1), channel_id=1, source_target_pairs={{0,4},{1,9},{2,6},{3,11},{4,8},{5,13},{6,10},{7,15},{8,12},{9,17},... | collective-permute-start | bytes 786440 | tf_op jit(solution)/shard_map/ppermute | solution.py:22
  21.9 20.1 %collective-permute-start.1 = (bf16[512,256]{1,0:T(8,128)(2,1)}, bf16[512,256]{1,0:T(8,128)(2,1)S(1)}, u32[]{:S(2)}, u32[]{:S(2)}) collective-permute-start(bf16[512,256]{1,0:T(8,128)(2,1)} %rest_2_.1), channel_id=1, source_target_pairs={{0,12},{1,17},{2,14},{3,19},{4,16},{5,21},{6,18},{7,23},{8,20},{9,... | collective-permute-start | bytes 786440 | tf_op jit(solution)/shard_map/ppermute | solution.py:22
  22.9 1.0 %copy-start.2 = (bf16[512,256]{1,0:T(8,128)(2,1)S(1)}, bf16[512,256]{1,0:T(8,128)(2,1)}, u32[]{:S(2)}) copy-start(bf16[512,256]{1,0:T(8,128)(2,1)} %own_ref.3) | copy-start | bytes 786436
  23.9 1.2 %copy-start.4 = (bf16[512,1024]{1,0:T(8,128)(2,1)S(1)}, bf16[512,1024]{1,0:T(8,128)(2,1)}, u32[]{:S(2)}) copy-start(bf16[512,1024]{1,0:T(8,128)(2,1)} %g_ref.1) | copy-start | bytes 3145732
  25.1 1.2 %copy-start.5 = (bf16[512,1024]{1,0:T(8,128)(2,1)S(1)}, bf16[512,1024]{1,0:T(8,128)(2,1)}, u32[]{:S(2)}) copy-start(bf16[512,1024]{1,0:T(8,128)(2,1)} %q_ref.3) | copy-start | bytes 3145732
  26.3 18.8 %copy-start.6 = (bf16[512,1024]{1,0:T(8,128)(2,1)S(1)}, bf16[512,1024]{1,0:T(8,128)(2,1)}, u32[]{:S(2)}) copy-start(bf16[512,1024]{1,0:T(8,128)(2,1)} %q_ref.3) | copy-start | bytes 3145732
  26.3 18.8 %copy-start.7 = (bf16[512,256]{1,0:T(8,128)(2,1)S(1)}, bf16[512,256]{1,0:T(8,128)(2,1)}, u32[]{:S(2)}) copy-start(bf16[512,256]{1,0:T(8,128)(2,1)} %rest_2_.1) | copy-start | bytes 786436
  42.0 1.9 %collective-permute-start.6 = (bf16[2,512,256]{2,1,0:T(8,128)(2,1)S(1)}, bf16[2,512,256]{2,1,0:T(8,128)(2,1)S(1)}, u32[]{:S(2)}, u32[]{:S(2)}) collective-permute-start(bf16[2,512,256]{2,1,0:T(8,128)(2,1)S(1)} %get-tuple-element.32), channel_id=1, source_target_pairs={{0,1},{1,0},{2,3},{3,2},{4,5},{5,4},{6,7},{7,6},{8,9},{9,8},{10,11... | collective-permute-start | bytes 1572872 | tf_op jit(solution)/shard_map/ppermute | solution.py:27
  42.0 3.2 %collective-permute-start.9 = (bf16[512,256]{1,0:T(8,128)(2,1)S(1)}, bf16[512,256]{1,0:T(8,128)(2,1)S(1)}, u32[]{:S(2)}, u32[]{:S(2)}) collective-permute-start(bf16[512,256]{1,0:T(8,128)(2,1)S(1)} %collective-permute-done.rest_3_), channel_id=1, source_target_pairs={{0,1},{1,0},{2,3},{3,2},{4,5},{5,4},{6,7},{7,6},{8,9},{9,8},{10,11... | collective-permute-start | bytes 786440 | tf_op jit(solution)/shard_map/ppermute | solution.py:27
  42.5 2.7 %collective-permute-start.10 = (bf16[512,256]{1,0:T(8,128)(2,1)S(1)}, bf16[512,256]{1,0:T(8,128)(2,1)S(1)}, u32[]{:S(2)}, u32[]{:S(2)}) collective-permute-start(bf16[512,256]{1,0:T(8,128)(2,1)S(1)} %collective-permute-done.1.rest_4_), channel_id=1, source_target_pairs={{0,1},{1,0},{2,3},{3,2},{4,5},{5,4},{6,7},{7,6},{8,9},{9,8},{10,11... | collective-permute-start | bytes 786440 | tf_op jit(solution)/shard_map/ppermute | solution.py:27
  44.1 13.5 %collective-permute-start.8 = (bf16[512,256]{1,0:T(8,128)(2,1)S(1)}, bf16[512,256]{1,0:T(8,128)(2,1)S(1)}, u32[]{:S(2)}, u32[]{:S(2)}) collective-permute-start(bf16[512,256]{1,0:T(8,128)(2,1)S(1)} %get-tuple-element.57), channel_id=1, source_target_pairs={{0,20},{1,17},{2,22},{3,19},{4,24},{5,21},{6,26},{7,23},{8,28},{9,... | collective-permute-start | bytes 786440 | tf_op jit(solution)/shard_map/ppermute | solution.py:22
  44.1 13.5 %collective-permute-start.7 = (bf16[512,256]{1,0:T(8,128)(2,1)S(1)}, bf16[512,256]{1,0:T(8,128)(2,1)S(1)}, u32[]{:S(2)}, u32[]{:S(2)}) collective-permute-start(bf16[512,256]{1,0:T(8,128)(2,1)S(1)} %get-tuple-element.58), channel_id=1, source_target_pairs={{0,28},{1,25},{2,30},{3,27},{4,0},{5,29},{6,2},{7,31},{8,4},{9,1},... | collective-permute-start | bytes 786440 | tf_op jit(solution)/shard_map/ppermute | solution.py:22
  45.1 21.2 %copy-start.3 = (bf16[512,256]{1,0:T(8,128)(2,1)S(1)}, bf16[512,256]{1,0:T(8,128)(2,1)}, u32[]{:S(2)}) copy-start(bf16[512,256]{1,0:T(8,128)(2,1)} %own_ref.3) | copy-start | bytes 786436
  54.3 3.3 %copy-start = (bf16[4,2048,512]{2,1,0:T(8,128)(2,1)}, bf16[4,2048,512]{2,1,0:T(8,128)(2,1)S(1)}, u32[]{:S(2)}) copy-start(bf16[4,2048,512]{2,1,0:T(8,128)(2,1)S(1)} %get-tuple-element.46.ds_ref) | copy-start | bytes 25165828
  57.6 2.1 %copy-start.8 = (bf16[512,256]{1,0:T(8,128)(2,1)}, bf16[512,256]{1,0:T(8,128)(2,1)S(1)}, u32[]{:S(2)}) copy-start(bf16[512,256]{1,0:T(8,128)(2,1)S(1)} %collective-permute-done.8) | copy-start | bytes 786436
  57.6 2.1 %copy-start.10 = (bf16[512,256]{1,0:T(8,128)(2,1)}, bf16[512,256]{1,0:T(8,128)(2,1)S(1)}, u32[]{:S(2)}) copy-start(bf16[512,256]{1,0:T(8,128)(2,1)S(1)} %collective-permute-done.7) | copy-start | bytes 786436
  57.6 2.0 %collective-permute-start.11 = (bf16[2,512,256]{2,1,0:T(8,128)(2,1)S(1)}, bf16[2,512,256]{2,1,0:T(8,128)(2,1)S(1)}, u32[]{:S(2)}, u32[]{:S(2)}) collective-permute-start(bf16[2,512,256]{2,1,0:T(8,128)(2,1)S(1)} %get-tuple-element.43), channel_id=1, source_target_pairs={{0,1},{1,0},{2,3},{3,2},{4,5},{5,4},{6,7},{7,6},{8,9},{9,8},{10,11... | collective-permute-start | bytes 1572872 | tf_op jit(solution)/shard_map/ppermute | solution.py:27
  60.4 14.2 %collective-permute-start.12 = (bf16[512,256]{1,0:T(8,128)(2,1)}, bf16[512,256]{1,0:T(8,128)(2,1)}, u32[]{:S(2)}, u32[]{:S(2)}) collective-permute-start(bf16[512,256]{1,0:T(8,128)(2,1)} %fusion.1), channel_id=1, source_target_pairs={{0,24},{1,25},{2,26},{3,27},{4,28},{5,29},{6,30},{7,31},{8,0},{9,1... | collective-permute-start | bytes 786440 | tf_op jit(solution)/shard_map/ppermute | solution.py:22
  66.4 3.4 %copy-start.1 = (bf16[4,2048,512]{2,1,0:T(8,128)(2,1)S(1)}, bf16[4,2048,512]{2,1,0:T(8,128)(2,1)}, u32[]{:S(2)}) copy-start(bf16[4,2048,512]{2,1,0:T(8,128)(2,1)} %copy-done) | copy-start | bytes 25165828
  69.8 9.2 %copy-start.9 = (bf16[512,256]{1,0:T(8,128)(2,1)S(1)}, bf16[512,256]{1,0:T(8,128)(2,1)}, u32[]{:S(2)}) copy-start(bf16[512,256]{1,0:T(8,128)(2,1)} %copy-done.8) | copy-start | bytes 786436
  69.8 9.2 %copy-start.11 = (bf16[512,256]{1,0:T(8,128)(2,1)S(1)}, bf16[512,256]{1,0:T(8,128)(2,1)}, u32[]{:S(2)}) copy-start(bf16[512,256]{1,0:T(8,128)(2,1)} %copy-done.10) | copy-start | bytes 786436
  75.6 7.8 %collective-permute-start.13 = (bf16[512,256]{1,0:T(8,128)(2,1)S(1)}, bf16[512,256]{1,0:T(8,128)(2,1)S(1)}, u32[]{:S(2)}, u32[]{:S(2)}) collective-permute-start(bf16[512,256]{1,0:T(8,128)(2,1)S(1)} %fusion), channel_id=1, source_target_pairs={{0,28},{1,25},{2,30},{3,27},{4,0},{5,29},{6,2},{7,31},{8,4},{9,1},... | collective-permute-start | bytes 786440 | tf_op jit(solution)/shard_map/ppermute | solution.py:22
  79.1 4.5 %collective-permute-start.17 = (bf16[256,256]{1,0:T(8,128)(2,1)S(1)}, bf16[256,256]{1,0:T(8,128)(2,1)S(1)}, u32[]{:S(2)}, u32[]{:S(2)}) collective-permute-start(bf16[256,256]{1,0:T(8,128)(2,1)S(1)} %select_convert_fusion), channel_id=1, source_target_pairs={{0,1},{1,0},{2,3},{3,2},{4,5},{5,4},{6,7},{7,6},{8,9},{9,8},{10,11... | collective-permute-start | bytes 393224 | tf_op jit(solution)/shard_map/ppermute | solution.py:27
  83.5 1.7 %collective-permute-start.14 = (bf16[256,256]{1,0:T(8,128)(2,1)S(1)}, bf16[256,256]{1,0:T(8,128)(2,1)S(1)}, u32[]{:S(2)}, u32[]{:S(2)}) collective-permute-start(bf16[256,256]{1,0:T(8,128)(2,1)S(1)} %select_convert_fusion.1), channel_id=1, source_target_pairs={{0,1},{1,0},{2,3},{3,2},{4,5},{5,4},{6,7},{7,6},{8,9},{9,8},{10,11... | collective-permute-start | bytes 393224 | tf_op jit(solution)/shard_map/ppermute | solution.py:27
  83.7 6.4 %collective-permute-start.18 = (bf16[256,256]{1,0:T(8,128)(2,1)S(1)}, bf16[256,256]{1,0:T(8,128)(2,1)S(1)}, u32[]{:S(2)}, u32[]{:S(2)}) collective-permute-start(bf16[256,256]{1,0:T(8,128)(2,1)S(1)} %add_convert_fusion), channel_id=1, source_target_pairs={{0,2},{1,3},{2,0},{3,1},{4,6},{5,7},{6,4},{7,5},{8,10},{9,11},{10,... | collective-permute-start | bytes 393224 | tf_op jit(solution)/shard_map/ppermute | solution.py:27
  85.3 7.2 %collective-permute-start.15 = (bf16[256,256]{1,0:T(8,128)(2,1)S(1)}, bf16[256,256]{1,0:T(8,128)(2,1)S(1)}, u32[]{:S(2)}, u32[]{:S(2)}) collective-permute-start(bf16[256,256]{1,0:T(8,128)(2,1)S(1)} %add_convert_fusion.1), channel_id=1, source_target_pairs={{0,2},{1,3},{2,0},{3,1},{4,6},{5,7},{6,4},{7,5},{8,10},{9,11},{10,... | collective-permute-start | bytes 393224 | tf_op jit(solution)/shard_map/ppermute | solution.py:27
  90.1 2.5 %collective-permute-start.19 = (f32[256,256]{1,0:T(8,128)S(1)}, f32[256,256]{1,0:T(8,128)S(1)}, u32[]{:S(2)}, u32[]{:S(2)}) collective-permute-start(f32[256,256]{1,0:T(8,128)S(1)} %convert_add_fusion.4), channel_id=1, source_target_pairs={{0,1},{1,0},{2,3},{3,2},{4,5},{5,4},{6,7},{7,6},{8,9},{9,8},{10,11... | collective-permute-start | bytes 786440 | tf_op jit(solution)/shard_map/ppermute | solution.py:27
  92.5 1.6 %collective-permute-start.16 = (f32[256,256]{1,0:T(8,128)S(1)}, f32[256,256]{1,0:T(8,128)S(1)}, u32[]{:S(2)}, u32[]{:S(2)}) collective-permute-start(f32[256,256]{1,0:T(8,128)S(1)} %convert_add_fusion.5), channel_id=1, source_target_pairs={{0,1},{1,0},{2,3},{3,2},{4,5},{5,4},{6,7},{7,6},{8,9},{9,8},{10,11... | collective-permute-start | bytes 786440 | tf_op jit(solution)/shard_map/ppermute | solution.py:27

commit v2 on v1

--- a/solution.py
+++ b/solution.py
@@ -263,11 +263,12 @@
     dq_ref[half:] = ((hi + total[half:]) * scale).astype(dq_ref.dtype)
 
 
-def gather_relayed(rows, reach):
-    mine = [along_seq(rows, 1, 1)]
+def gather_relayed(rows, reach, scalars):
+    first, scalars = lax.optimization_barrier((along_seq(rows, 1, 1), scalars))
+    mine = [first]
     for _ in range(1, reach // 2):
         mine.append(along_seq(mine[-1], 2, 0))
-    return mine, [swap_heads(block, 1) for block in mine]
+    return mine, [swap_heads(block, 1) for block in mine], scalars
 
 
 def gather_direct(rows, reach):
@@ -278,16 +279,17 @@
     return keep + swap_heads(send, 1).astype(jnp.float32)
 
 
-def return_direct(parts):
-    return [
-        along_seq(parts[j].astype(jnp.bfloat16), -2 * j - 1, -1) for j in range(len(parts))
-    ]
-
-
-def sum_heads(down, core):
+def relay_on(parts, arrived, reach):
+    for j in range(reach // 2 - 2, -1, -1):
+        piece = (parts[j] + arrived.astype(jnp.float32)).astype(jnp.bfloat16)
+        arrived = along_seq(piece, -2, 0) if j else along_seq(piece, -1, -1)
+    return arrived
+
+
+def sum_heads(down, low_core):
     half = down.shape[0] // 2
-    mine = jnp.where(core == 0, down[:half], down[half:])
-    other = jnp.where(core == 0, down[half:], down[:half])
+    mine = jnp.where(low_core, down[:half], down[half:])
+    other = jnp.where(low_core, down[half:], down[:half])
     own = mine + swap_heads(other.astype(jnp.bfloat16), 1).astype(jnp.float32)
     bit = 2
     while bit < lax.axis_size("head"):
@@ -295,8 +297,8 @@
         own = low.astype(jnp.float32) + swap_heads(low, bit).astype(jnp.float32)
         bit *= 2
     other = swap_heads(own, 1)
-    first = jnp.where(core == 0, own, other)
-    second = jnp.where(core == 0, other, own)
+    first = jnp.where(low_core, own, other)
+    second = jnp.where(low_core, other, own)
     return jnp.concatenate([first, second], axis=0)
 
 
@@ -348,7 +350,7 @@
             **spec,
         )
 
-    keys_mine, keys_other = gather_relayed(key_rows, reach)
+    keys_mine, keys_other, (place, low_core) = gather_relayed(key_rows, reach, (place, core == 0))
     values_mine = gather_direct(value_rows, reach)
 
     expo, grads, inv, dv_down, dv_keep, dv_send = call(
@@ -374,7 +376,7 @@
     values_other = [swap_heads(block, 1) for block in values_mine]
     dv_parts = pair_sums(dv_keep, dv_send)
     dv_parts, expo = lax.optimization_barrier((dv_parts, expo))
-    dv_back = return_direct(dv_parts)
+    dv_back = along_seq(dv_parts[-1].astype(jnp.bfloat16), -2, 0)
 
     dscores, dk_down, dk_keep, dk_send = call(
         dscores_kernel,
@@ -387,11 +389,10 @@
     )(place, grads, inv, query, grads, inv, expo, value_rows, *values_mine, *values_other)
 
     dv_back, dk_keep, dk_send = lax.optimization_barrier((dv_back, dk_keep, dk_send))
-    for block in dv_back:
-        dv_down = dv_down + block.astype(jnp.float32)
     dk_parts = pair_sums(dk_keep, dk_send)
     dk_parts, dscores = lax.optimization_barrier((dk_parts, dscores))
     dk_back = along_seq(dk_parts[-1].astype(jnp.bfloat16), -2, 0)
+    dv_back = relay_on(dv_parts, dv_back, reach)
 
     (grad_query,) = call(
         dquery_kernel,
@@ -403,12 +404,10 @@
         scratch_shapes=[ext, sems],
     )(place, dscores, key_rows, *keys_mine, *keys_other)
 
-    dk_back, grad_query = lax.optimization_barrier((dk_back, grad_query))
-    for j in range(reach // 2 - 2, -1, -1):
-        piece = (dk_parts[j] + dk_back.astype(jnp.float32)).astype(jnp.bfloat16)
-        dk_back = along_seq(piece, -2, 0) if j else along_seq(piece, -1, -1)
-    grad_value = sum_heads(dv_down, core)
-    grad_key = sum_heads(dk_down + dk_back.astype(jnp.float32), core)
+    dk_back, dv_back, grad_query = lax.optimization_barrier((dk_back, dv_back, grad_query))
+    dk_back = relay_on(dk_parts, dk_back, reach)
+    grad_value = sum_heads(dv_down + dv_back.astype(jnp.float32), low_core)
+    grad_key = sum_heads(dk_down + dk_back.astype(jnp.float32), low_core)
     return grad_query, grad_key, grad_value
 
 

time: 95.3 us -> 86.6 us (0.909)
  local copies, waits for them, and re-layouts: 10.8 us -> 3.47 us
  starting transfers between devices: 17.6 us -> 10.8 us
  waiting for transfers between devices: 37.9 us -> 44.4 us
    ppermute x8, starting transfers between devices: 13.9 us -> 4.85 us  [along_seq(): return lax.ppermute(block, ('seq', 'head'), route)]
    ppermute x8, waiting for transfers between devices: 27.3 us -> 34.2 us  [along_seq(): return lax.ppermute(block, ('seq', 'head'), route)]
    unnamed x24 -> x12, local copies, waits for them, and re-layouts: 10.1 us -> 3.41 us
    ppermute x12, starting transfers between devices: 3.7 us -> 5.9 us  [swap_heads(): return lax.ppermute(block, 'head', route)]
  transfers between devices with their start and end apart: 20 -> 20, of which waited for: 10 -> 13; matrix products, arithmetic and copies ran while one was open for 2% -> 2% of each run, Pallas kernels for 26% -> 28%
where the time goes in v2:
time: 86.6 us; the launch traced here: 86.3 us
  waiting for transfers between devices  44.4 us (51%)
  Pallas kernels  24.4 us (28%)
  starting transfers between devices  10.8 us (12%)
  local copies, waits for them, and re-layouts  3.47 us (4%)
  other arithmetic  2.5 us (3%)
    ppermute x8, waiting for transfers between devices, along_seq(): return lax.ppermute(block, ('seq', 'head'), route)  34.2 us
    pallas_call x1, Pallas kernels, on_device(): call(probs_kernel, 'probs', 2, in_specs=[smem, by_head_first, by_head_nex...  10.3 us
    ppermute x12, waiting for transfers between devices, swap_heads(): return lax.ppermute(block, 'head', route)  10.2 us
    pallas_call x1, Pallas kernels, on_device(): call(dscores_kernel, 'dscores', 2, in_specs=[smem, by_head_first, row_fir...  9.23 us
    ppermute x12, starting transfers between devices, swap_heads(): return lax.ppermute(block, 'head', route)  5.9 us
    ppermute x8, starting transfers between devices, along_seq(): return lax.ppermute(block, ('seq', 'head'), route)  4.85 us
    pallas_call x1, Pallas kernels, on_device(): call(dquery_kernel, 'dquery', 1, in_specs=[smem, vmem] + halo, out_specs=...  4.81 us
    unnamed x12, local copies, waits for them, and re-layouts  3.41 us
  transfers between devices with their start and end apart: 20, of which 13 were waited for; matrix products, arithmetic and copies ran while one was open for 2% of the time, Pallas kernels for 28%

profile of v2, /device:TPU:0, one launch (start us, length us, event | category | flops | bytes accessed | tf_op | source)
XLA Modules:
  0.0 86.3 jit_solution(16294326283908726299)
XLA Ops:
  0.6 3.0 %collective-permute-start.2 = (bf16[512,256]{1,0:T(8,128)(2,1)}, bf16[512,256]{1,0:T(8,128)(2,1)S(1)}, u32[]{:S(2)}, u32[]{:S(2)}) collective-permute-start(bf16[512,256]{1,0:T(8,128)(2,1)} %own_ref.3), channel_id=1, source_target_pairs={{0,4},{1,9},{2,6},{3,11},{4,8},{5,13},{6,10},{7,15},{8,12},{9,17},... | collective-permute-start | bytes 786440 | tf_op jit(solution)/shard_map/ppermute | solution.py:22
  3.6 0.1 pad_add_fusion.place
  3.7 9.5 %collective-permute-done.2.rest_0_ = bf16[512,256]{1,0:T(8,128)(2,1)S(1)} collective-permute-done((bf16[512,256]{1,0:T(8,128)(2,1)}, bf16[512,256]{1,0:T(8,128)(2,1)S(1)}, u32[]{:S(2)}, u32[]{:S(2)}) %collective-permute-start.2) | collective-permute-done | bytes 262176 | tf_op jit(solution)/shard_map/ppermute | solution.py:22
  13.2 0.0 collective-permute-start.3
  13.2 0.0 collective-permute-start.4
  13.2 8.2 %collective-permute-done.3.rest_1_ = bf16[512,256]{1,0:T(8,128)(2,1)S(1)} collective-permute-done((bf16[512,256]{1,0:T(8,128)(2,1)S(1)}, bf16[512,256]{1,0:T(8,128)(2,1)S(1)}, u32[]{:S(2)}, u32[]{:S(2)}) %collective-permute-start.3) | collective-permute-done | bytes 262176 | tf_op jit(solution)/shard_map/ppermute | solution.py:22
  21.4 0.0 collective-permute-start.5
  21.4 0.5 collective-permute-start
  21.9 0.0 collective-permute-start.1
  21.9 0.0 collective-permute-done.4.rest_2_
  21.9 1.0 %collective-permute-done.5.rest_3_ = bf16[512,256]{1,0:T(8,128)(2,1)S(1)} collective-permute-done((bf16[512,256]{1,0:T(8,128)(2,1)S(1)}, bf16[512,256]{1,0:T(8,128)(2,1)S(1)}, u32[]{:S(2)}, u32[]{:S(2)}) %collective-permute-start.5) | collective-permute-done | bytes 262176 | tf_op jit(solution)/shard_map/ppermute | solution.py:27
  22.9 0.0 copy-start
  22.9 0.9 %copy-done = bf16[512,256]{1,0:T(8,128)(2,1)S(1)} copy-done((bf16[512,256]{1,0:T(8,128)(2,1)S(1)}, bf16[512,256]{1,0:T(8,128)(2,1)}, u32[]{:S(2)}) %copy-start) | copy-done | bytes 262168
  23.9 0.0 copy-start.2
  23.9 1.2 %copy-done.2 = bf16[512,1024]{1,0:T(8,128)(2,1)S(1)} copy-done((bf16[512,1024]{1,0:T(8,128)(2,1)S(1)}, bf16[512,1024]{1,0:T(8,128)(2,1)}, u32[]{:S(2)}) %copy-start.2) | copy-done | bytes 1048600
  25.1 0.0 copy-start.3
  25.1 1.2 %copy-done.3 = bf16[512,1024]{1,0:T(8,128)(2,1)S(1)} copy-done((bf16[512,1024]{1,0:T(8,128)(2,1)S(1)}, bf16[512,1024]{1,0:T(8,128)(2,1)}, u32[]{:S(2)}) %copy-start.3) | copy-done | bytes 1048600
  26.3 0.0 copy-start.4
  26.3 0.0 copy-start.5
  26.3 10.3 %probs.1 = (bf16[4,2048,512]{2,1,0:T(8,128)(2,1)S(1)}, bf16[512,1024]{1,0:T(8,128)(2,1)S(1)}, f32[4,8,512]{2,1,0:T(8,128)S(1)}, f32[512,256]{1,0:T(8,128)S(1)}, ...) custom-call(s32[2]{0:T(128)S(1)} %pad_add_fusion.place, bf16[512,1024]{1,0:T(8,128)(2,1)S(1)} %copy-done.3, ...), custom_call_target="tpu_custom_call" | custom-call | flops 4831838208 | bytes 16777216 | tf_op jit(solution)/shard_map/probs/pallas_call | solution.py:356
  36.7 0.0 collective-permute-done.rest_3_
  36.7 5.3 %collective-permute-done.1.rest_4_ = bf16[512,256]{1,0:T(8,128)(2,1)S(1)} collective-permute-done((bf16[512,256]{1,0:T(8,128)(2,1)}, bf16[512,256]{1,0:T(8,128)(2,1)S(1)}, u32[]{:S(2)}, u32[]{:S(2)}) %collective-permute-start.1) | collective-permute-done | bytes 262176 | tf_op jit(solution)/shard_map/ppermute | solution.py:22
  42.0 0.0 collective-permute-start.6
  42.0 0.5 collective-permute-start.8
  42.5 0.0 collective-permute-start.9
  42.5 1.4 %collective-permute-done.6 = bf16[2,512,256]{2,1,0:T(8,128)(2,1)S(1)} collective-permute-done((bf16[2,512,256]{2,1,0:T(8,128)(2,1)S(1)}, bf16[2,512,256]{2,1,0:T(8,128)(2,1)S(1)}, u32[]{:S(2)}, u32[]{:S(2)}) %collective-permute-start.6) | collective-permute-done | bytes 524320 | tf_op jit(solution)/shard_map/ppermute | solution.py:27
  43.9 0.1 convert_add_fusion.1
  44.0 0.1 collective-permute-start.7
  44.1 0.2 collective-permute-done.8.rest_5_
  44.2 0.4 collective-permute-done.9.rest_6_
  44.6 0.0 copy-done.4
  44.6 0.0 copy-done.5
  44.6 0.0 copy-start.1
  44.6 9.2 %dscores.1 = (bf16[4,2048,512]{2,1,0:T(8,128)(2,1)S(1)}, f32[512,256]{1,0:T(8,128)S(1)}, f32[2,512,256]{2,1,0:T(8,128)S(1)}, bf16[2,512,256]{2,1,0:T(8,128)(2,1)S(1)}) custom-call(s32[2]{0:T(128)S(1)} %pad_add_fusion.place, bf16[512,1024]{1,0:T(8,128)(2,1)S(1)} %get-tuple-element.40.first_ref.gs_ref, f32[4,8,512]{2,1,0:T(8,128)S(1)} %get-tuple-element.41.first_inv.rest_0_, ...), custom_call_target="tpu_custom_call" | custom-call | flops 4831838208 | bytes 16777216 | tf_op jit(solution)/shard_map/dscores/pallas_call | solution.py:381
  53.9 0.0 collective-permute-done.7
  53.9 0.2 collective-permute-start.10
  54.1 0.1 fusion.1
  54.1 0.6 collective-permute-start.12
  54.7 1.2 %collective-permute-done.10 = bf16[2,512,256]{2,1,0:T(8,128)(2,1)S(1)} collective-permute-done((bf16[2,512,256]{2,1,0:T(8,128)(2,1)S(1)}, bf16[2,512,256]{2,1,0:T(8,128)(2,1)S(1)}, u32[]{:S(2)}, u32[]{:S(2)}) %collective-permute-start.10) | collective-permute-done | bytes 524320 | tf_op jit(solution)/shard_map/ppermute | solution.py:27
  55.9 0.1 convert_add_fusion
  56.0 0.6 collective-permute-start.11
  56.6 0.0 copy-done.1
  56.6 4.8 %dquery.1 = bf16[512,1024]{1,0:T(8,128)(2,1)} custom-call(s32[2]{0:T(128)S(1)} %pad_add_fusion.place, bf16[4,2048,512]{2,1,0:T(8,128)(2,1)S(1)} %get-tuple-element.52.ds_ref, bf16[512,256]{1,0:T(8,128)(2,1)S(1)} %copy-done.1, bf16[512,256]{1,0:T(8,128)(2,1)S(1)} %collective-permute-done.2.rest_0_, bf16[512,256]{1,0:T(8,128)(2,1)S(1)} %collective-permute-done.3.rest_1_, ...), custom_call_target="tpu_custom_call" | custom-call | flops 2415919104 | bytes 16777216 | tf_op jit(solution)/shard_map/dquery/pallas_call | solution.py:397
  61.5 0.0 collective-permute-done.12
  61.5 6.9 %collective-permute-done.11 = bf16[512,256]{1,0:T(8,128)(2,1)S(1)} collective-permute-done((bf16[512,256]{1,0:T(8,128)(2,1)S(1)}, bf16[512,256]{1,0:T(8,128)(2,1)S(1)}, u32[]{:S(2)}, u32[]{:S(2)}) %collective-permute-start.11) | collective-permute-done | bytes 262176 | tf_op jit(solution)/shard_map/ppermute | solution.py:22
  68.3 0.1 fusion
  68.4 0.1 collective-permute-start.13
  68.5 0.1 convert_add_fusion.2
  68.6 1.9 %collective-permute-start.17 = (bf16[256,256]{1,0:T(8,128)(2,1)S(1)}, bf16[256,256]{1,0:T(8,128)(2,1)S(1)}, u32[]{:S(2)}, u32[]{:S(2)}) collective-permute-start(bf16[256,256]{1,0:T(8,128)(2,1)S(1)} %select_convert_fusion), channel_id=1, source_target_pairs={{0,1},{1,0},{2,3},{3,2},{4,5},{5,4},{6,7},{7,6},{8,9},{9,8},{10,11... | collective-permute-start | bytes 393224 | tf_op jit(solution)/shard_map/ppermute | solution.py:27
  70.4 4.4 %collective-permute-done.13 = bf16[512,256]{1,0:T(8,128)(2,1)S(1)} collective-permute-done((bf16[512,256]{1,0:T(8,128)(2,1)S(1)}, bf16[512,256]{1,0:T(8,128)(2,1)S(1)}, u32[]{:S(2)}, u32[]{:S(2)}) %collective-permute-start.13) | collective-permute-done | bytes 262176 | tf_op jit(solution)/shard_map/ppermute | solution.py:22
  74.8 0.1 convert_add_fusion.3
  74.9 0.5 collective-permute-start.14
  75.4 0.0 collective-permute-done.17
  75.5 1.8 %collective-permute-start.18 = (bf16[256,256]{1,0:T(8,128)(2,1)S(1)}, bf16[256,256]{1,0:T(8,128)(2,1)S(1)}, u32[]{:S(2)}, u32[]{:S(2)}) collective-permute-start(bf16[256,256]{1,0:T(8,128)(2,1)S(1)} %add_convert_fusion), channel_id=1, source_target_pairs={{0,2},{1,3},{2,0},{3,1},{4,6},{5,7},{6,4},{7,5},{8,10},{9,11},{10,... | collective-permute-start | bytes 393224 | tf_op jit(solution)/shard_map/ppermute | solution.py:27
  77.2 0.0 collective-permute-done.14
  77.3 0.9 %collective-permute-start.15 = (bf16[256,256]{1,0:T(8,128)(2,1)S(1)}, bf16[256,256]{1,0:T(8,128)(2,1)S(1)}, u32[]{:S(2)}, u32[]{:S(2)}) collective-permute-start(bf16[256,256]{1,0:T(8,128)(2,1)S(1)} %add_convert_fusion.1), channel_id=1, source_target_pairs={{0,2},{1,3},{2,0},{3,1},{4,6},{5,7},{6,4},{7,5},{8,10},{9,11},{10,... | collective-permute-start | bytes 393224 | tf_op jit(solution)/shard_map/ppermute | solution.py:27
  78.2 3.7 %collective-permute-done.18 = bf16[256,256]{1,0:T(8,128)(2,1)S(1)} collective-permute-done((bf16[256,256]{1,0:T(8,128)(2,1)S(1)}, bf16[256,256]{1,0:T(8,128)(2,1)S(1)}, u32[]{:S(2)}, u32[]{:S(2)}) %collective-permute-start.18) | collective-permute-done | bytes 131104 | tf_op jit(solution)/shard_map/ppermute | solution.py:27
  81.9 0.1 collective-permute-start.19
  82.0 1.8 %collective-permute-done.15 = bf16[256,256]{1,0:T(8,128)(2,1)S(1)} collective-permute-done((bf16[256,256]{1,0:T(8,128)(2,1)S(1)}, bf16[256,256]{1,0:T(8,128)(2,1)S(1)}, u32[]{:S(2)}, u32[]{:S(2)}) %collective-permute-start.15) | collective-permute-done | bytes 131104 | tf_op jit(solution)/shard_map/ppermute | solution.py:27
  83.9 0.1 collective-permute-start.16
  83.9 0.0 collective-permute-done.19
  84.0 0.8 pad_maximum_fusion.1
  84.8 0.6 collective-permute-done.16
  85.5 0.8 pad_maximum_fusion
  (10 shorter events, 0.3 us)
Async XLA Ops:
  0.6 12.6 %collective-permute-start.2 = (bf16[512,256]{1,0:T(8,128)(2,1)}, bf16[512,256]{1,0:T(8,128)(2,1)S(1)}, u32[]{:S(2)}, u32[]{:S(2)}) collective-permute-start(bf16[512,256]{1,0:T(8,128)(2,1)} %own_ref.3), channel_id=1, source_target_pairs={{0,4},{1,9},{2,6},{3,11},{4,8},{5,13},{6,10},{7,15},{8,12},{9,17},... | collective-permute-start | bytes 786440 | tf_op jit(solution)/shard_map/ppermute | solution.py:22
  13.2 8.2 %collective-permute-start.3 = (bf16[512,256]{1,0:T(8,128)(2,1)S(1)}, bf16[512,256]{1,0:T(8,128)(2,1)S(1)}, u32[]{:S(2)}, u32[]{:S(2)}) collective-permute-start(bf16[512,256]{1,0:T(8,128)(2,1)S(1)} %collective-permute-done.2.rest_0_), channel_id=1, source_target_pairs={{0,8},{1,9},{2,10},{3,11},{4,12},{5,13},{6,14},{7,15},{8,16},{9,17... | collective-permute-start | bytes 786440 | tf_op jit(solution)/shard_map/ppermute | solution.py:22
  13.2 8.7 %collective-permute-start.4 = (bf16[512,256]{1,0:T(8,128)(2,1)S(1)}, bf16[512,256]{1,0:T(8,128)(2,1)S(1)}, u32[]{:S(2)}, u32[]{:S(2)}) collective-permute-start(bf16[512,256]{1,0:T(8,128)(2,1)S(1)} %collective-permute-done.2.rest_0_), channel_id=1, source_target_pairs={{0,1},{1,0},{2,3},{3,2},{4,5},{5,4},{6,7},{7,6},{8,9},{9,8},{10,11... | collective-permute-start | bytes 786440 | tf_op jit(solution)/shard_map/ppermute | solution.py:27
  21.4 1.5 %collective-permute-start.5 = (bf16[512,256]{1,0:T(8,128)(2,1)S(1)}, bf16[512,256]{1,0:T(8,128)(2,1)S(1)}, u32[]{:S(2)}, u32[]{:S(2)}) collective-permute-start(bf16[512,256]{1,0:T(8,128)(2,1)S(1)} %collective-permute-done.3.rest_1_), channel_id=1, source_target_pairs={{0,1},{1,0},{2,3},{3,2},{4,5},{5,4},{6,7},{7,6},{8,9},{9,8},{10,11... | collective-permute-start | bytes 786440 | tf_op jit(solution)/shard_map/ppermute | solution.py:27
  21.4 15.3 %collective-permute-start = (bf16[512,256]{1,0:T(8,128)(2,1)}, bf16[512,256]{1,0:T(8,128)(2,1)S(1)}, u32[]{:S(2)}, u32[]{:S(2)}) collective-permute-start(bf16[512,256]{1,0:T(8,128)(2,1)} %rest_2_.1), channel_id=1, source_target_pairs={{0,4},{1,9},{2,6},{3,11},{4,8},{5,13},{6,10},{7,15},{8,12},{9,17},... | collective-permute-start | bytes 786440 | tf_op jit(solution)/shard_map/ppermute | solution.py:22
  21.9 20.1 %collective-permute-start.1 = (bf16[512,256]{1,0:T(8,128)(2,1)}, bf16[512,256]{1,0:T(8,128)(2,1)S(1)}, u32[]{:S(2)}, u32[]{:S(2)}) collective-permute-start(bf16[512,256]{1,0:T(8,128)(2,1)} %rest_2_.1), channel_id=1, source_target_pairs={{0,12},{1,17},{2,14},{3,19},{4,16},{5,21},{6,18},{7,23},{8,20},{9,... | collective-permute-start | bytes 786440 | tf_op jit(solution)/shard_map/ppermute | solution.py:22
  22.9 1.0 %copy-start = (bf16[512,256]{1,0:T(8,128)(2,1)S(1)}, bf16[512,256]{1,0:T(8,128)(2,1)}, u32[]{:S(2)}) copy-start(bf16[512,256]{1,0:T(8,128)(2,1)} %own_ref.3) | copy-start | bytes 786436
  23.9 1.2 %copy-start.2 = (bf16[512,1024]{1,0:T(8,128)(2,1)S(1)}, bf16[512,1024]{1,0:T(8,128)(2,1)}, u32[]{:S(2)}) copy-start(bf16[512,1024]{1,0:T(8,128)(2,1)} %g_ref.1) | copy-start | bytes 3145732
  25.1 1.2 %copy-start.3 = (bf16[512,1024]{1,0:T(8,128)(2,1)S(1)}, bf16[512,1024]{1,0:T(8,128)(2,1)}, u32[]{:S(2)}) copy-start(bf16[512,1024]{1,0:T(8,128)(2,1)} %q_ref.3) | copy-start | bytes 3145732
  26.3 18.3 %copy-start.4 = (bf16[512,1024]{1,0:T(8,128)(2,1)S(1)}, bf16[512,1024]{1,0:T(8,128)(2,1)}, u32[]{:S(2)}) copy-start(bf16[512,1024]{1,0:T(8,128)(2,1)} %q_ref.3) | copy-start | bytes 3145732
  26.3 18.3 %copy-start.5 = (bf16[512,256]{1,0:T(8,128)(2,1)S(1)}, bf16[512,256]{1,0:T(8,128)(2,1)}, u32[]{:S(2)}) copy-start(bf16[512,256]{1,0:T(8,128)(2,1)} %rest_2_.1) | copy-start | bytes 786436
  42.0 1.9 %collective-permute-start.6 = (bf16[2,512,256]{2,1,0:T(8,128)(2,1)S(1)}, bf16[2,512,256]{2,1,0:T(8,128)(2,1)S(1)}, u32[]{:S(2)}, u32[]{:S(2)}) collective-permute-start(bf16[2,512,256]{2,1,0:T(8,128)(2,1)S(1)} %get-tuple-element.37), channel_id=1, source_target_pairs={{0,1},{1,0},{2,3},{3,2},{4,5},{5,4},{6,7},{7,6},{8,9},{9,8},{10,11... | collective-permute-start | bytes 1572872 | tf_op jit(solution)/shard_map/ppermute | solution.py:27
  42.0 2.3 %collective-permute-start.8 = (bf16[512,256]{1,0:T(8,128)(2,1)S(1)}, bf16[512,256]{1,0:T(8,128)(2,1)S(1)}, u32[]{:S(2)}, u32[]{:S(2)}) collective-permute-start(bf16[512,256]{1,0:T(8,128)(2,1)S(1)} %collective-permute-done.rest_3_), channel_id=1, source_target_pairs={{0,1},{1,0},{2,3},{3,2},{4,5},{5,4},{6,7},{7,6},{8,9},{9,8},{10,11... | collective-permute-start | bytes 786440 | tf_op jit(solution)/shard_map/ppermute | solution.py:27
  42.5 2.1 %collective-permute-start.9 = (bf16[512,256]{1,0:T(8,128)(2,1)S(1)}, bf16[512,256]{1,0:T(8,128)(2,1)S(1)}, u32[]{:S(2)}, u32[]{:S(2)}) collective-permute-start(bf16[512,256]{1,0:T(8,128)(2,1)S(1)} %collective-permute-done.1.rest_4_), channel_id=1, source_target_pairs={{0,1},{1,0},{2,3},{3,2},{4,5},{5,4},{6,7},{7,6},{8,9},{9,8},{10,11... | collective-permute-start | bytes 786440 | tf_op jit(solution)/shard_map/ppermute | solution.py:27
  44.0 9.8 %collective-permute-start.7 = (bf16[512,256]{1,0:T(8,128)(2,1)S(1)}, bf16[512,256]{1,0:T(8,128)(2,1)S(1)}, u32[]{:S(2)}, u32[]{:S(2)}) collective-permute-start(bf16[512,256]{1,0:T(8,128)(2,1)S(1)} %fusion.2), channel_id=1, source_target_pairs={{0,24},{1,25},{2,26},{3,27},{4,28},{5,29},{6,30},{7,31},{8,0},{9,1... | collective-permute-start | bytes 786440 | tf_op jit(solution)/shard_map/ppermute | solution.py:22
  44.6 12.0 %copy-start.1 = (bf16[512,256]{1,0:T(8,128)(2,1)S(1)}, bf16[512,256]{1,0:T(8,128)(2,1)}, u32[]{:S(2)}) copy-start(bf16[512,256]{1,0:T(8,128)(2,1)} %own_ref.3) | copy-start | bytes 786436
  53.9 2.0 %collective-permute-start.10 = (bf16[2,512,256]{2,1,0:T(8,128)(2,1)S(1)}, bf16[2,512,256]{2,1,0:T(8,128)(2,1)S(1)}, u32[]{:S(2)}, u32[]{:S(2)}) collective-permute-start(bf16[2,512,256]{2,1,0:T(8,128)(2,1)S(1)} %get-tuple-element.48), channel_id=1, source_target_pairs={{0,1},{1,0},{2,3},{3,2},{4,5},{5,4},{6,7},{7,6},{8,9},{9,8},{10,11... | collective-permute-start | bytes 1572872 | tf_op jit(solution)/shard_map/ppermute | solution.py:27
  54.1 7.3 %collective-permute-start.12 = (bf16[512,256]{1,0:T(8,128)(2,1)S(1)}, bf16[512,256]{1,0:T(8,128)(2,1)S(1)}, u32[]{:S(2)}, u32[]{:S(2)}) collective-permute-start(bf16[512,256]{1,0:T(8,128)(2,1)S(1)} %fusion.1), channel_id=1, source_target_pairs={{0,28},{1,25},{2,30},{3,27},{4,0},{5,29},{6,2},{7,31},{8,4},{9,1},... | collective-permute-start | bytes 786440 | tf_op jit(solution)/shard_map/ppermute | solution.py:22
  56.0 12.3 %collective-permute-start.11 = (bf16[512,256]{1,0:T(8,128)(2,1)S(1)}, bf16[512,256]{1,0:T(8,128)(2,1)S(1)}, u32[]{:S(2)}, u32[]{:S(2)}) collective-permute-start(bf16[512,256]{1,0:T(8,128)(2,1)S(1)} %fusion.3), channel_id=1, source_target_pairs={{0,24},{1,25},{2,26},{3,27},{4,28},{5,29},{6,30},{7,31},{8,0},{9,1... | collective-permute-start | bytes 786440 | tf_op jit(solution)/shard_map/ppermute | solution.py:22
  68.4 6.4 %collective-permute-start.13 = (bf16[512,256]{1,0:T(8,128)(2,1)S(1)}, bf16[512,256]{1,0:T(8,128)(2,1)S(1)}, u32[]{:S(2)}, u32[]{:S(2)}) collective-permute-start(bf16[512,256]{1,0:T(8,128)(2,1)S(1)} %fusion), channel_id=1, source_target_pairs={{0,28},{1,25},{2,30},{3,27},{4,0},{5,29},{6,2},{7,31},{8,4},{9,1},... | collective-permute-start | bytes 786440 | tf_op jit(solution)/shard_map/ppermute | solution.py:22
  68.6 6.9 %collective-permute-start.17 = (bf16[256,256]{1,0:T(8,128)(2,1)S(1)}, bf16[256,256]{1,0:T(8,128)(2,1)S(1)}, u32[]{:S(2)}, u32[]{:S(2)}) collective-permute-start(bf16[256,256]{1,0:T(8,128)(2,1)S(1)} %select_convert_fusion), channel_id=1, source_target_pairs={{0,1},{1,0},{2,3},{3,2},{4,5},{5,4},{6,7},{7,6},{8,9},{9,8},{10,11... | collective-permute-start | bytes 393224 | tf_op jit(solution)/shard_map/ppermute | solution.py:27
  74.9 2.3 %collective-permute-start.14 = (bf16[256,256]{1,0:T(8,128)(2,1)S(1)}, bf16[256,256]{1,0:T(8,128)(2,1)S(1)}, u32[]{:S(2)}, u32[]{:S(2)}) collective-permute-start(bf16[256,256]{1,0:T(8,128)(2,1)S(1)} %select_convert_fusion.1), channel_id=1, source_target_pairs={{0,1},{1,0},{2,3},{3,2},{4,5},{5,4},{6,7},{7,6},{8,9},{9,8},{10,11... | collective-permute-start | bytes 393224 | tf_op jit(solution)/shard_map/ppermute | solution.py:27
  75.5 6.4 %collective-permute-start.18 = (bf16[256,256]{1,0:T(8,128)(2,1)S(1)}, bf16[256,256]{1,0:T(8,128)(2,1)S(1)}, u32[]{:S(2)}, u32[]{:S(2)}) collective-permute-start(bf16[256,256]{1,0:T(8,128)(2,1)S(1)} %add_convert_fusion), channel_id=1, source_target_pairs={{0,2},{1,3},{2,0},{3,1},{4,6},{5,7},{6,4},{7,5},{8,10},{9,11},{10,... | collective-permute-start | bytes 393224 | tf_op jit(solution)/shard_map/ppermute | solution.py:27
  77.3 6.5 %collective-permute-start.15 = (bf16[256,256]{1,0:T(8,128)(2,1)S(1)}, bf16[256,256]{1,0:T(8,128)(2,1)S(1)}, u32[]{:S(2)}, u32[]{:S(2)}) collective-permute-start(bf16[256,256]{1,0:T(8,128)(2,1)S(1)} %add_convert_fusion.1), channel_id=1, source_target_pairs={{0,2},{1,3},{2,0},{3,1},{4,6},{5,7},{6,4},{7,5},{8,10},{9,11},{10,... | collective-permute-start | bytes 393224 | tf_op jit(solution)/shard_map/ppermute | solution.py:27
  81.9 2.0 %collective-permute-start.19 = (f32[256,256]{1,0:T(8,128)S(1)}, f32[256,256]{1,0:T(8,128)S(1)}, u32[]{:S(2)}, u32[]{:S(2)}) collective-permute-start(f32[256,256]{1,0:T(8,128)S(1)} %convert_add_fusion.4), channel_id=1, source_target_pairs={{0,1},{1,0},{2,3},{3,2},{4,5},{5,4},{6,7},{7,6},{8,9},{9,8},{10,11... | collective-permute-start | bytes 786440 | tf_op jit(solution)/shard_map/ppermute | solution.py:27
  83.9 1.6 %collective-permute-start.16 = (f32[256,256]{1,0:T(8,128)S(1)}, f32[256,256]{1,0:T(8,128)S(1)}, u32[]{:S(2)}, u32[]{:S(2)}) collective-permute-start(f32[256,256]{1,0:T(8,128)S(1)} %convert_add_fusion.5), channel_id=1, source_target_pairs={{0,1},{1,0},{2,3},{3,2},{4,5},{5,4},{6,7},{7,6},{8,9},{9,8},{10,11... | collective-permute-start | bytes 786440 | tf_op jit(solution)/shard_map/ppermute | solution.py:27

commit v3 on v2

v3 whole, which is shorter than its diff:
```python
import functools

import jax
import jax.numpy as jnp
from jax import lax
from jax.experimental import pallas as pl
from jax.experimental.pallas import tpu as pltpu
from jax.sharding import PartitionSpec as P

WINDOW = 2048
LOW = -1e30
VMEM_BYTES = 18 * 1024 * 1024


def along_seq(block, near, step=0):
    shards, group = lax.axis_size("seq"), lax.axis_size("head")
    route = []
    for shard in range(shards):
        for member in range(group):
            target = (shard + near + (member % 2) * step) % shards
            route.append((shard * group + member, target * group + member))
    return lax.ppermute(block, ("seq", "head"), route)


def swap_heads(block, bit):
    route = [(i, i ^ bit) for i in range(lax.axis_size("head"))]
    return lax.ppermute(block, "head", route)


def dot_t(left, right):
    return lax.dot_general(
        left, right, (((1,), (1,)), ((), ())), preferred_element_type=jnp.float32
    )


def dot(left, right):
    return jnp.dot(left, right, preferred_element_type=jnp.float32)


def fold_rows(block, total, combine):
    rows = total.shape[0]
    for first in range(0, block.shape[0], rows):
        total = combine(total, block[first : first + rows])
    return total


def lower_mask(half):
    keys = lax.broadcasted_iota(jnp.int32, (half, half), 0)
    queries = lax.broadcasted_iota(jnp.int32, (half, half), 1)
    return queries >= keys


def load_rows(own_ref, mine_refs, other_refs, ext, sem, core, full, reach):
    copies = [pltpu.make_async_copy(own_ref, ext.at[pl.ds(reach * full, full)], sem.at[0])]
    for j in range(reach // 2):
        first = pl.multiple_of((reach - 1 - 2 * j - core) * full, full)
        other = pl.multiple_of((reach - 2 - 2 * j + core) * full, full)
        copies.append(
            pltpu.make_async_copy(mine_refs[j], ext.at[pl.ds(first, full)], sem.at[2 * j + 1])
        )
        copies.append(
            pltpu.make_async_copy(other_refs[j], ext.at[pl.ds(other, full)], sem.at[2 * j + 2])
        )
    for each in copies:
        each.start()
    return copies


def unit_product(unit, ext, rows, half, reach, mask, far_bias=None):
    own = reach * 2 * half
    if unit >= 2:
        return dot_t(ext[unit * half : (unit + 1) * half], rows)
    if unit == 0:
        near = dot_t(ext[own : own + half], rows)
        far = dot_t(ext[:half], rows[:half])
        if far_bias is not None:
            far = far + far_bias
        return jnp.concatenate([jnp.where(mask, near[:, :half], far), near[:, half:]], axis=1)
    near = dot_t(ext[own + half : own + 2 * half], rows[half:])
    far = dot_t(ext[half : 2 * half], rows)
    if far_bias is not None:
        far = far + far_bias
    return jnp.concatenate([far[:, :half], jnp.where(mask, near, far[:, half:])], axis=1)


def unit_add(unit, tile, acc, rows, half, reach, mask):
    own = reach * 2 * half
    if unit >= 2:
        acc[unit * half : (unit + 1) * half] += dot(tile, rows)
        return
    left, right = tile[:, :half], tile[:, half:]
    zero = jnp.zeros_like(left)
    if unit == 0:
        both = jnp.concatenate([jnp.where(mask, left, zero), right], axis=1)
        acc[own : own + half] += dot(both, rows)
        acc[:half] += dot(jnp.where(mask, zero, left), rows[:half])
        return
    acc[own + half : own + 2 * half] += dot(jnp.where(mask, right, zero), rows[half:])
    both = jnp.concatenate([left, jnp.where(mask, zero, right)], axis=1)
    acc[half : 2 * half] += dot(both, rows)


def split_out(acc, down_ref, keep_ref, send_ref, core, full, reach):
    down_ref[...] = acc[reach * full :]
    for j in range(reach // 2):
        first = pl.multiple_of((reach - 1 - 2 * j - core) * full, full)
        other = pl.multiple_of((reach - 2 - 2 * j + core) * full, full)
        keep_ref[j] = acc[pl.ds(first, full), :]
        send_ref[j] = acc[pl.ds(other, full), :].astype(send_ref.dtype)


def stage_kernel(scale, q_ref, g_ref, own_ref, q_out, g_out, own_out):
    q_out[...] = q_ref[...] * jnp.asarray(scale, q_ref.dtype)
    g_out[...] = g_ref[...]
    own_out[...] = own_ref[...]


def probs_kernel(reach, scale, place, first_ref, q_ref, g_ref, own_ref, *rest):
    mine_refs, other_refs, rest = rest[: reach // 2], rest[reach // 2 : reach], rest[reach:]
    p_ref, sum_ref, ext, down_ref, keep_ref, send_ref, s_buf, e_buf, peak_buf, acc, sem = rest
    step, steps = pl.program_id(0), pl.num_programs(0)
    rank, core = place[0], place[1]
    full = own_ref.shape[0]
    half = full // 2
    units = 2 * reach
    mask = lower_mask(half)
    far_bias = jnp.where(rank >= reach, 0.0, LOW).astype(jnp.float32)
    lowest = jnp.full((16, full), LOW, jnp.float32)

    def score(unit, rows, peak):
        block = unit_product(unit, ext, rows, half, reach, mask, far_bias)
        s_buf[unit * half : (unit + 1) * half] = block
        part = fold_rows(block, lowest, jnp.maximum)
        if unit >= 2:
            part = jnp.where(rank >= reach - unit // 2, part, LOW)
        return jnp.maximum(peak, part)

    def exponent(unit, level, total):
        at = slice(unit * half, (unit + 1) * half)
        if unit >= 2:
            level = jnp.where(rank >= reach - unit // 2, level, -LOW)
        expo = jnp.exp(s_buf[at] - level)
        e_buf[at] = expo
        return fold_rows(expo, total, jnp.add)

    def add_values(total):
        inv = 1.0 / jnp.sum(total, axis=0, keepdims=True)
        rounded = jnp.zeros((16, full), jnp.float32)
        for unit in range(units):
            at = slice(unit * half, (unit + 1) * half)
            tile = (e_buf[at] * inv).astype(jnp.bfloat16)
            p_ref[step, at] = tile
            rounded = fold_rows(tile.astype(jnp.float32), rounded, jnp.add)
            unit_add(unit, tile, acc, g_ref[...], half, reach, mask)
        rounded = jnp.sum(rounded, axis=0, keepdims=True)
        sum_ref[0] = jnp.broadcast_to(rounded, (8, full))

    @pl.when(step == 0)
    def _():
        copies = load_rows(own_ref, mine_refs, other_refs, ext, sem, core, full, reach)
        acc[...] = jnp.zeros_like(acc)
        for each in copies:
            each.wait()
        peak = lowest
        for unit in range(units):
            peak = score(unit, first_ref[...], peak)
        peak_buf[...] = peak

    @pl.when(step < steps - 1)
    def _():
        level = jnp.max(peak_buf[...], axis=0, keepdims=True)
        total = jnp.zeros((16, full), jnp.float32)
        peak = lowest
        for unit in range(units):
            total = exponent(unit, level, total)
            peak = score(unit, q_ref[...], peak)
        peak_buf[...] = peak
        add_values(total)

    @pl.when(step == steps - 1)
    def _():
        level = jnp.max(peak_buf[...], axis=0, keepdims=True)
        total = jnp.zeros((16, full), jnp.float32)
        for unit in range(units):
            total = exponent(unit, level, total)
        add_values(total)
        split_out(acc, down_ref, keep_ref, send_ref, core, full, reach)


def dscores_kernel(reach, scale, place, first_ref, q_ref, g_ref, first_sum, sum_ref, *rest):
    p_ref, own_ref, rest = rest[0], rest[1], rest[2:]
    mine_refs, other_refs, rest = rest[: reach // 2], rest[reach // 2 : reach], rest[reach:]
    ds_ref, down_ref, keep_ref, send_ref, ext, dp_buf, delta_buf, acc, sem = rest
    step, steps = pl.program_id(0), pl.num_programs(0)
    core = place[1]
    full = own_ref.shape[0]
    half = full // 2
    units = 2 * reach
    mask = lower_mask(half)

    def product(unit, grads, probs, total):
        at = slice(unit * half, (unit + 1) * half)
        block = unit_product(unit, ext, grads, half, reach, mask)
        dp_buf[at] = block
        return fold_rows(block * probs.astype(jnp.float32), total, jnp.add)

    def keep_delta(total, rounded):
        delta = jnp.sum(total, axis=0, keepdims=True) / rounded
        delta_buf[...] = jnp.broadcast_to(delta, delta_buf.shape)

    def dscore(unit, delta):
        at = slice(unit * half, (unit + 1) * half)
        tile = (p_ref[step, at].astype(jnp.float32) * (dp_buf[at] - delta)).astype(jnp.bfloat16)
        ds_ref[step, at] = tile
        return tile

    nothing = jnp.zeros((16, full), jnp.float32)

    @pl.when(step == 0)
    def _():
        copies = load_rows(own_ref, mine_refs, other_refs, ext, sem, core, full, reach)
        acc[...] = jnp.zeros_like(acc)
        for each in copies:
            each.wait()
        total = nothing
        for unit in range(units):
            tile = p_ref[0, unit * half : (unit + 1) * half]
            total = product(unit, first_ref[...], tile, total)
        keep_delta(total, first_sum[0, :1])

    @pl.when(step < steps - 1)
    def _():
        following = step + 1
        delta = delta_buf[:1]
        total = nothing
        for unit in range(units):
            unit_add(unit, dscore(unit, delta), acc, q_ref[...], half, reach, mask)
            tile = p_ref[following, unit * half : (unit + 1) * half]
            total = product(unit, g_ref[...], tile, total)
        keep_delta(total, sum_ref[0, :1])

    @pl.when(step == steps - 1)
    def _():
        delta = delta_buf[:1]
        for unit in range(units):
            unit_add(unit, dscore(unit, delta), acc, q_ref[...], half, reach, mask)
        split_out(acc, down_ref, keep_ref, send_ref, core, full, reach)


def dot_first(left, right):
    return lax.dot_general(
        left, right, (((0,), (0,)), ((), ())), preferred_element_type=jnp.float32
    )


def dquery_kernel(reach, scale, ds_ref, ext, dq_ref):
    full = ds_ref.shape[2]
    half = full // 2
    head = pl.program_id(0)
    mask = lower_mask(half)
    zero = jnp.zeros((half, half), jnp.bfloat16)
    own = reach * full
    lo_lo, lo_hi = ds_ref[head, :half, :half], ds_ref[head, :half, half:]
    hi_lo, hi_hi = ds_ref[head, half:full, :half], ds_ref[head, half:full, half:]
    lo = (
        dot_first(jnp.where(mask, lo_lo, zero), ext[own : own + half])
        + dot_first(jnp.where(mask, zero, lo_lo), ext[:half])
        + dot_first(hi_lo, ext[half:full])
    )
    hi = (
        dot_first(lo_hi, ext[own : own + half])
        + dot_first(jnp.where(mask, hi_hi, zero), ext[own + half : own + full])
        + dot_first(jnp.where(mask, zero, hi_hi), ext[half:full])
    )
    total = dot_first(ds_ref[head, full:own], ext[full:own])
    dq_ref[:half] = ((lo + total[:half]) * scale).astype(dq_ref.dtype)
    dq_ref[half:] = ((hi + total[half:]) * scale).astype(dq_ref.dtype)


def gather_halo(keys, values, reach, early):
    block, early = lax.optimization_barrier((along_seq(keys, 1, 1), early))
    mine = [block]
    for _ in range(1, reach // 2):
        mine.append(along_seq(mine[-1], 2, 0))
    last, value_block = lax.optimization_barrier((mine[-1], along_seq(values, 1, 1)))
    mine[-1] = last
    value_blocks = [value_block]
    for _ in range(1, reach // 2):
        value_blocks.append(along_seq(value_blocks[-1], 2, 0))
    return mine, [swap_heads(each, 1) for each in mine], value_blocks, early


def pair_sums(keep, send):
    return keep + swap_heads(send, 1).astype(jnp.float32)


def relay_back(parts, arrived):
    for j in range(len(parts) - 2, -1, -1):
        piece = (parts[j] + arrived.astype(jnp.float32)).astype(jnp.bfloat16)
        arrived = along_seq(piece, -2) if j else along_seq(piece, -1, -1)
    return arrived


def sum_chips(own):
    bit = 2
    while bit < lax.axis_size("head"):
        low = own.astype(jnp.bfloat16)
        own = low.astype(jnp.float32) + swap_heads(low, bit).astype(jnp.float32)
        bit *= 2
    return own


def own_half(down, low_core):
    half = down.shape[0] // 2
    mine = jnp.where(low_core, down[:half], down[half:])
    other = jnp.where(low_core, down[half:], down[:half])
    return mine + swap_heads(other.astype(jnp.bfloat16), 1).astype(jnp.float32)


def both_halves(own, low_core):
    other = swap_heads(own, 1)
    first_is_own = jnp.stack([low_core, jnp.logical_not(low_core)])[:, None, None]
    halves = jnp.where(first_is_own, own[None], other[None])
    return halves.reshape(2 * own.shape[0], own.shape[1])


def on_device(query, key_rows, value_rows, grad_out):
    tok_rows, head_dim = key_rows.shape
    heads = query.shape[1] // head_dim
    reach = WINDOW // tok_rows
    half = tok_rows // 2
    scale = head_dim ** (-0.5)
    core = lax.axis_index("head") % 2
    place = jnp.stack([lax.axis_index("seq"), core]).astype(jnp.int32)
    ext_rows = (reach + 1) * tok_rows
    span = reach * tok_rows

    def following(h):
        return jnp.minimum(h + 1, heads - 1)

    smem = pl.BlockSpec(memory_space=pltpu.SMEM)
    vmem = pl.BlockSpec(memory_space=pltpu.VMEM)
    halo = [pl.BlockSpec(memory_space=pl.ANY)] * (reach + 1)
    by_head = pl.BlockSpec((tok_rows, head_dim), lambda h: (0, h))
    by_head_next = pl.BlockSpec((tok_rows, head_dim), lambda h: (0, following(h)))
    by_head_first = pl.BlockSpec((tok_rows, head_dim), lambda h: (0, 0))
    row = pl.BlockSpec((1, 8, tok_rows), lambda h: (h, 0, 0))
    row_next = pl.BlockSpec((1, 8, tok_rows), lambda h: (following(h), 0, 0))
    row_first = pl.BlockSpec((1, 8, tok_rows), lambda h: (0, 0, 0))
    tile_shape = jax.ShapeDtypeStruct((heads, span, tok_rows), jnp.bfloat16)
    row_shape = jax.ShapeDtypeStruct((heads, 8, tok_rows), jnp.float32)

    down = pl.BlockSpec((tok_rows, head_dim), lambda h: (0, 0))
    whole = pl.BlockSpec((reach // 2, tok_rows, head_dim), lambda h: (0, 0, 0))
    sums = [down, whole, whole]
    sums_shapes = [
        jax.ShapeDtypeStruct((tok_rows, head_dim), jnp.float32),
        jax.ShapeDtypeStruct((reach // 2, tok_rows, head_dim), jnp.float32),
        jax.ShapeDtypeStruct((reach // 2, tok_rows, head_dim), jnp.bfloat16),
    ]
    ext = pltpu.VMEM((ext_rows, head_dim), jnp.bfloat16)
    acc = pltpu.VMEM((ext_rows, head_dim), jnp.float32)
    tile = pltpu.VMEM((span, tok_rows), jnp.float32)
    wide = pltpu.VMEM((16, tok_rows), jnp.float32)
    sems = pltpu.SemaphoreType.DMA((reach + 1,))
    product = 2 * heads * tok_rows * (reach * tok_rows + half) * head_dim

    def call(body, name, products, **spec):
        return pl.pallas_call(
            functools.partial(body, reach, scale),
            grid=(heads,),
            compiler_params=pltpu.CompilerParams(vmem_limit_bytes=VMEM_BYTES),
            cost_estimate=pl.CostEstimate(
                flops=products * product, bytes_accessed=16 * 2**20, transcendentals=0
            ),
            name=name,
            **spec,
        )

    staged = pl.pallas_call(
        functools.partial(stage_kernel, scale),
        out_shape=[
            jax.ShapeDtypeStruct(query.shape, query.dtype),
            jax.ShapeDtypeStruct(grad_out.shape, grad_out.dtype),
            jax.ShapeDtypeStruct(key_rows.shape, key_rows.dtype),
        ],
        in_specs=[vmem, vmem, vmem],
        out_specs=[vmem, vmem, vmem],
        compiler_params=pltpu.CompilerParams(vmem_limit_bytes=VMEM_BYTES),
        name="stage",
    )(query, grad_out, key_rows)
    early = (place, core == 0, staged)
    keys_mine, keys_other, values_mine, early = gather_halo(key_rows, value_rows, reach, early)
    place, low_core, (query_scaled, grads_own, keys_own) = early

    probs, rounded, keys_ext, dv_down, dv_keep, dv_send = call(
        probs_kernel,
        "probs",
        2,
        in_specs=[smem, by_head_first, by_head_next, by_head] + halo,
        out_specs=[vmem, row, vmem, *sums],
        out_shape=[
            tile_shape,
            row_shape,
            jax.ShapeDtypeStruct((ext_rows, head_dim), jnp.bfloat16),
            *sums_shapes,
        ],
        scratch_shapes=[tile, tile, wide, acc, sems],
    )(place, query_scaled, query_scaled, grads_own, keys_own, *keys_mine, *keys_other)

    values_mine, probs, dv_keep, dv_send = lax.optimization_barrier(
        (values_mine, probs, dv_keep, dv_send)
    )
    values_other = [swap_heads(block, 1) for block in values_mine]
    dv_parts = pair_sums(dv_keep, dv_send)
    dv_parts, probs = lax.optimization_barrier((dv_parts, probs))
    dv_back = along_seq(dv_parts[-1].astype(jnp.bfloat16), -2)

    dscores, dk_down, dk_keep, dk_send = call(
        dscores_kernel,
        "dscores",
        2,
        in_specs=[smem, by_head_first, by_head, by_head_next, row_first, row_next, vmem] + halo,
        out_specs=[vmem, *sums],
        out_shape=[tile_shape, *sums_shapes],
        scratch_shapes=[ext, tile, wide, acc, sems],
    )(
        place, grads_own, query_scaled, grads_own, rounded, rounded, probs, value_rows,
        *values_mine, *values_other,
    )

    dv_back, dk_keep, dk_send = lax.optimization_barrier((dv_back, dk_keep, dk_send))
    dk_parts = pair_sums(dk_keep, dk_send)
    dk_parts, dscores = lax.optimization_barrier((dk_parts, dscores))
    dk_back = along_seq(dk_parts[-1].astype(jnp.bfloat16), -2)
    dv_back = relay_back(dv_parts, dv_back)

    (grad_query,) = call(
        dquery_kernel,
        "dquery",
        1,
        in_specs=[vmem, vmem],
        out_specs=[by_head],
        out_shape=[jax.ShapeDtypeStruct(query.shape, query.dtype)],
    )(dscores, keys_ext)

    dk_back, dv_back, grad_query = lax.optimization_barrier((dk_back, dv_back, grad_query))
    dk_back = relay_back(dk_parts, dk_back)
    dv_own = sum_chips(dv_down + dv_back.astype(jnp.float32))
    dv_own, dk_back = lax.optimization_barrier((dv_own, dk_back))
    grad_value = dv_own + swap_heads(dv_own, 1)
    dk_own = own_half(dk_down + dk_back.astype(jnp.float32), low_core)
    grad_key = both_halves(sum_chips(dk_own), low_core)
    return grad_query, grad_key, grad_value


def solution(mesh):
    return jax.shard_map(
        on_device,
        mesh=mesh,
        in_specs=(P("seq", "head"), P("seq", None), P("seq", None), P("seq", "head")),
        out_specs=(P("seq", "head"), P("seq", None), P("seq", None)),
        check_vma=False,
    )
```

time: 86.6 us -> 79.3 us (0.916)
  waiting for transfers between devices: 44.4 us -> 33 us
  starting transfers between devices: 10.8 us -> 16.9 us
  Pallas kernels: 24.4 us -> 22.3 us
    ppermute x8, waiting for transfers between devices: 34.2 us -> 21.3 us  [along_seq(): return lax.ppermute(block, ('seq', 'head'), route)]
    ppermute x8, starting transfers between devices: 4.85 us -> 13.7 us  [along_seq(): return lax.ppermute(block, ('seq', 'head'), route)]
    ppermute x12 -> x11, starting transfers between devices: 5.9 us -> 3.19 us  [swap_heads(): return lax.ppermute(block, 'head', route)]
    concatenate x2 -> x0, other arithmetic: 1.66 us -> none  [sum_heads(): return jnp.concatenate([first, second], axis=0)]
    ppermute x12 -> x11, waiting for transfers between devices: 10.2 us -> 11.7 us  [swap_heads(): return lax.ppermute(block, 'head', route)]
    pallas_call x2 -> x3, Pallas kernels: 14 us -> 12.6 us  [the longest x1 8.32 us: on_device(): call(dscores_kernel, 'dscores', 2, in_specs=[smem, by_head_first, by_head...]
    unnamed x12 -> x8, local copies, waits for them, and re-layouts: 3.41 us -> 3.4 us
  transfers between devices with their start and end apart: 20 -> 19, of which waited for: 13 -> 12; matrix products, arithmetic and copies ran while one was open for 2% -> 2% of each run, Pallas kernels for 28% -> 28%
where the time goes in v3:
time: 79.3 us; the launch traced here: 79.1 us
  waiting for transfers between devices  33 us (42%)
  Pallas kernels  22.3 us (28%)
  starting transfers between devices  16.9 us (21%)
  local copies, waits for them, and re-layouts  3.55 us (4%)
  other arithmetic  2.57 us (3%)
    ppermute x8, waiting for transfers between devices, along_seq(): return lax.ppermute(block, ('seq', 'head'), route)  21.3 us
    ppermute x8, starting transfers between devices, along_seq(): return lax.ppermute(block, ('seq', 'head'), route)  13.7 us
    ppermute x11, waiting for transfers between devices, swap_heads(): return lax.ppermute(block, 'head', route)  11.7 us
    pallas_call x1, Pallas kernels, on_device(): call(probs_kernel, 'probs', 2, in_specs=[smem, by_head_first, by_head_nex...  9.73 us
    pallas_call x1, Pallas kernels, on_device(): call(dscores_kernel, 'dscores', 2, in_specs=[smem, by_head_first, by_head...  8.32 us
    pallas_call x1, Pallas kernels, on_device(): call(dquery_kernel, 'dquery', 1, in_specs=[vmem, vmem], out_specs=[by_hea...  4.08 us
    unnamed x8, local copies, waits for them, and re-layouts  3.4 us
    ppermute x11, starting transfers between devices, swap_heads(): return lax.ppermute(block, 'head', route)  3.19 us
  transfers between devices with their start and end apart: 19, of which 12 were waited for; matrix products, arithmetic and copies ran while one was open for 2% of the time, Pallas kernels for 28%

profile of v3, /device:TPU:0, one launch (start us, length us, event | category | flops | bytes accessed | tf_op | source)
XLA Modules:
  0.0 79.1 jit_solution(12708068307978415839)
XLA Ops:
  0.6 3.0 %collective-permute-start = (bf16[512,256]{1,0:T(8,128)(2,1)}, bf16[512,256]{1,0:T(8,128)(2,1)S(1)}, u32[]{:S(2)}, u32[]{:S(2)}) collective-permute-start(bf16[512,256]{1,0:T(8,128)(2,1)} %own_ref.1), channel_id=1, source_target_pairs={{0,4},{1,9},{2,6},{3,11},{4,8},{5,13},{6,10},{7,15},{8,12},{9,17},... | collective-permute-start | bytes 786440 | tf_op jit(solution)/shard_map/ppermute | solution.py:22
  3.6 1.5 %collective-permute-start.2 = (bf16[512,256]{1,0:T(8,128)(2,1)}, bf16[512,256]{1,0:T(8,128)(2,1)S(1)}, u32[]{:S(2)}, u32[]{:S(2)}) collective-permute-start(bf16[512,256]{1,0:T(8,128)(2,1)} %rest_1_.1), channel_id=1, source_target_pairs={{0,4},{1,9},{2,6},{3,11},{4,8},{5,13},{6,10},{7,15},{8,12},{9,17},... | collective-permute-start | bytes 786440 | tf_op jit(solution)/shard_map/ppermute | solution.py:22
  5.2 0.0 copy-start
  5.2 1.2 %copy-done = bf16[512,1024]{1,0:T(8,128)(2,1)S(1)} copy-done((bf16[512,1024]{1,0:T(8,128)(2,1)S(1)}, bf16[512,1024]{1,0:T(8,128)(2,1)}, u32[]{:S(2)}) %copy-start) | copy-done | bytes 1048600
  6.4 0.0 copy-start.1
  6.4 1.2 %copy-done.1 = bf16[512,1024]{1,0:T(8,128)(2,1)S(1)} copy-done((bf16[512,1024]{1,0:T(8,128)(2,1)S(1)}, bf16[512,1024]{1,0:T(8,128)(2,1)}, u32[]{:S(2)}) %copy-start.1) | copy-done | bytes 1048600
  7.6 0.0 copy-start.2
  7.6 0.9 %copy-done.2 = bf16[512,256]{1,0:T(8,128)(2,1)S(1)} copy-done((bf16[512,256]{1,0:T(8,128)(2,1)S(1)}, bf16[512,256]{1,0:T(8,128)(2,1)}, u32[]{:S(2)}) %copy-start.2) | copy-done | bytes 262168
  8.6 0.2 stage.1
  8.7 0.1 pad_add_fusion.1.place
  8.8 5.2 %collective-permute-done.rest_0_ = bf16[512,256]{1,0:T(8,128)(2,1)S(1)} collective-permute-done((bf16[512,256]{1,0:T(8,128)(2,1)}, bf16[512,256]{1,0:T(8,128)(2,1)S(1)}, u32[]{:S(2)}, u32[]{:S(2)}) %collective-permute-start) | collective-permute-done | bytes 262176 | tf_op jit(solution)/shard_map/ppermute | solution.py:22
  14.0 0.0 copy-start.3
  14.0 0.0 collective-permute-start.1
  14.0 0.0 collective-permute-start.4
  14.0 5.6 %collective-permute-done.2.rest_2_ = bf16[512,256]{1,0:T(8,128)(2,1)S(1)} collective-permute-done((bf16[512,256]{1,0:T(8,128)(2,1)}, bf16[512,256]{1,0:T(8,128)(2,1)S(1)}, u32[]{:S(2)}, u32[]{:S(2)}) %collective-permute-start.2) | collective-permute-done | bytes 262176 | tf_op jit(solution)/shard_map/ppermute | solution.py:22
  19.6 2.6 %collective-permute-done.1.rest_1_ = bf16[512,256]{1,0:T(8,128)(2,1)S(1)} collective-permute-done((bf16[512,256]{1,0:T(8,128)(2,1)S(1)}, bf16[512,256]{1,0:T(8,128)(2,1)S(1)}, u32[]{:S(2)}, u32[]{:S(2)}) %collective-permute-start.1) | collective-permute-done | bytes 262176 | tf_op jit(solution)/shard_map/ppermute | solution.py:22
  22.2 0.0 collective-permute-start.5
  22.2 0.0 collective-permute-start.3
  22.2 0.0 collective-permute-done.4.rest_2_
  22.2 1.5 %collective-permute-done.5.rest_3_ = bf16[512,256]{1,0:T(8,128)(2,1)S(1)} collective-permute-done((bf16[512,256]{1,0:T(8,128)(2,1)S(1)}, bf16[512,256]{1,0:T(8,128)(2,1)S(1)}, u32[]{:S(2)}, u32[]{:S(2)}) %collective-permute-start.5) | collective-permute-done | bytes 262176 | tf_op jit(solution)/shard_map/ppermute | solution.py:27
  23.7 9.7 %probs.1 = (bf16[4,2048,512]{2,1,0:T(8,128)(2,1)S(1)}, f32[4,8,512]{2,1,0:T(8,128)S(1)}, bf16[2560,256]{1,0:T(8,128)(2,1)S(1)}, f32[512,256]{1,0:T(8,128)S(1)}, ...) custom-call(s32[2]{0:T(128)S(1)} %pad_add_fusion.1.place, ...), custom_call_target="tpu_custom_call" | custom-call | flops 4831838208 | bytes 16777216 | tf_op jit(solution)/shard_map/probs/pallas_call | solution.py:396
  33.5 0.0 collective-permute-done.3.rest_3_
  33.5 0.2 collective-permute-start.6
  33.7 0.4 collective-permute-start.8
  34.1 0.1 collective-permute-start.9
  34.2 1.3 %collective-permute-done.6 = bf16[2,512,256]{2,1,0:T(8,128)(2,1)S(1)} collective-permute-done((bf16[2,512,256]{2,1,0:T(8,128)(2,1)S(1)}, bf16[2,512,256]{2,1,0:T(8,128)(2,1)S(1)}, u32[]{:S(2)}, u32[]{:S(2)}) %collective-permute-start.6) | collective-permute-done | bytes 524320 | tf_op jit(solution)/shard_map/ppermute | solution.py:27
  35.5 0.1 convert_add_fusion.1
  35.6 2.4 %collective-permute-start.7 = (bf16[512,256]{1,0:T(8,128)(2,1)S(1)}, bf16[512,256]{1,0:T(8,128)(2,1)S(1)}, u32[]{:S(2)}, u32[]{:S(2)}) collective-permute-start(bf16[512,256]{1,0:T(8,128)(2,1)S(1)} %fusion.2), channel_id=1, source_target_pairs={{0,24},{1,25},{2,26},{3,27},{4,28},{5,29},{6,30},{7,31},{8,0},{9,1... | collective-permute-start | bytes 786440 | tf_op jit(solution)/shard_map/ppermute | solution.py:22
  38.0 0.0 collective-permute-done.8.rest_4_
  38.0 0.0 collective-permute-done.9.rest_5_
  38.0 0.0 copy-done.3
  38.0 8.3 %dscores.1 = (bf16[4,2048,512]{2,1,0:T(8,128)(2,1)S(1)}, f32[512,256]{1,0:T(8,128)S(1)}, f32[2,512,256]{2,1,0:T(8,128)S(1)}, bf16[2,512,256]{2,1,0:T(8,128)(2,1)S(1)}) custom-call(s32[2]{0:T(128)S(1)} %pad_add_fusion.1.place, bf16[512,1024]{1,0:T(8,128)(2,1)S(1)} %get-tuple-element.48.g_ref.first_ref, ...), custom_call_target="tpu_custom_call" | custom-call | flops 4831838208 | bytes 16777216 | tf_op jit(solution)/shard_map/dscores/pallas_call | solution.py:419
  46.3 0.0 collective-permute-done.7
  46.3 0.1 collective-permute-start.10
  46.4 0.1 fusion.1
  46.5 4.1 %collective-permute-start.12 = (bf16[512,256]{1,0:T(8,128)(2,1)S(1)}, bf16[512,256]{1,0:T(8,128)(2,1)S(1)}, u32[]{:S(2)}, u32[]{:S(2)}) collective-permute-start(bf16[512,256]{1,0:T(8,128)(2,1)S(1)} %fusion.1), channel_id=1, source_target_pairs={{0,28},{1,25},{2,30},{3,27},{4,0},{5,29},{6,2},{7,31},{8,4},{9,1},... | collective-permute-start | bytes 786440 | tf_op jit(solution)/shard_map/ppermute | solution.py:22
  50.6 0.0 collective-permute-done.10
  50.6 0.1 convert_add_fusion
  50.7 0.1 collective-permute-start.11
  50.8 4.1 %dquery.1 = bf16[512,1024]{1,0:T(8,128)(2,1)} custom-call(bf16[4,2048,512]{2,1,0:T(8,128)(2,1)S(1)} %get-tuple-element.69.ds_ref, bf16[2560,256]{1,0:T(8,128)(2,1)S(1)} %get-tuple-element.70.ext), custom_call_target="tpu_custom_call" | custom-call | flops 2415919104 | bytes 16777216 | tf_op jit(solution)/shard_map/dquery/pallas_call | solution.py:438
  54.9 2.5 %collective-permute-done.12 = bf16[512,256]{1,0:T(8,128)(2,1)S(1)} collective-permute-done((bf16[512,256]{1,0:T(8,128)(2,1)S(1)}, bf16[512,256]{1,0:T(8,128)(2,1)S(1)}, u32[]{:S(2)}, u32[]{:S(2)}) %collective-permute-start.12) | collective-permute-done | bytes 262176 | tf_op jit(solution)/shard_map/ppermute | solution.py:22
  57.3 3.5 %collective-permute-done.11 = bf16[512,256]{1,0:T(8,128)(2,1)S(1)} collective-permute-done((bf16[512,256]{1,0:T(8,128)(2,1)S(1)}, bf16[512,256]{1,0:T(8,128)(2,1)S(1)}, u32[]{:S(2)}, u32[]{:S(2)}) %collective-permute-start.11) | collective-permute-done | bytes 262176 | tf_op jit(solution)/shard_map/ppermute | solution.py:22
  60.8 0.1 add_convert_fusion
  60.9 1.7 %collective-permute-start.13 = (bf16[512,256]{1,0:T(8,128)(2,1)S(1)}, bf16[512,256]{1,0:T(8,128)(2,1)S(1)}, u32[]{:S(2)}, u32[]{:S(2)}) collective-permute-start(bf16[512,256]{1,0:T(8,128)(2,1)S(1)} %add_convert_fusion), channel_id=1, source_target_pairs={{0,2},{1,3},{2,0},{3,1},{4,6},{5,7},{6,4},{7,5},{8,10},{9,11},{10,... | collective-permute-start | bytes 786440 | tf_op jit(solution)/shard_map/ppermute | solution.py:27
  62.6 0.1 fusion
  62.7 2.6 %collective-permute-start.14 = (bf16[512,256]{1,0:T(8,128)(2,1)S(1)}, bf16[512,256]{1,0:T(8,128)(2,1)S(1)}, u32[]{:S(2)}, u32[]{:S(2)}) collective-permute-start(bf16[512,256]{1,0:T(8,128)(2,1)S(1)} %fusion), channel_id=1, source_target_pairs={{0,28},{1,25},{2,30},{3,27},{4,0},{5,29},{6,2},{7,31},{8,4},{9,1},... | collective-permute-start | bytes 786440 | tf_op jit(solution)/shard_map/ppermute | solution.py:22
  65.3 2.0 %collective-permute-done.13 = bf16[512,256]{1,0:T(8,128)(2,1)S(1)} collective-permute-done((bf16[512,256]{1,0:T(8,128)(2,1)S(1)}, bf16[512,256]{1,0:T(8,128)(2,1)S(1)}, u32[]{:S(2)}, u32[]{:S(2)}) %collective-permute-start.13) | collective-permute-done | bytes 262176 | tf_op jit(solution)/shard_map/ppermute | solution.py:27
  67.3 0.1 convert_add_fusion.3
  67.4 1.9 %collective-permute-done.14 = bf16[512,256]{1,0:T(8,128)(2,1)S(1)} collective-permute-done((bf16[512,256]{1,0:T(8,128)(2,1)S(1)}, bf16[512,256]{1,0:T(8,128)(2,1)S(1)}, u32[]{:S(2)}, u32[]{:S(2)}) %collective-permute-start.14) | collective-permute-done | bytes 262176 | tf_op jit(solution)/shard_map/ppermute | solution.py:22
  69.3 0.1 convert_add_fusion.2
  69.4 0.1 collective-permute-start.15
  69.5 1.3 %collective-permute-done.15 = bf16[256,256]{1,0:T(8,128)(2,1)S(1)} collective-permute-done((bf16[256,256]{1,0:T(8,128)(2,1)S(1)}, bf16[256,256]{1,0:T(8,128)(2,1)S(1)}, u32[]{:S(2)}, u32[]{:S(2)}) %collective-permute-start.15) | collective-permute-done | bytes 131104 | tf_op jit(solution)/shard_map/ppermute | solution.py:27
  70.9 0.5 collective-permute-start.16
  71.4 0.0 collective-permute-start.18
  71.4 5.1 %collective-permute-done.16 = bf16[256,256]{1,0:T(8,128)(2,1)S(1)} collective-permute-done((bf16[256,256]{1,0:T(8,128)(2,1)S(1)}, bf16[256,256]{1,0:T(8,128)(2,1)S(1)}, u32[]{:S(2)}, u32[]{:S(2)}) %collective-permute-start.16) | collective-permute-done | bytes 131104 | tf_op jit(solution)/shard_map/ppermute | solution.py:27
  76.5 0.1 collective-permute-start.17
  76.6 0.1 pad_add_fusion
  76.7 0.1 broadcast_in_dim.35
  76.8 0.0 collective-permute-done.18
  76.8 0.9 %add.44 = f32[512,256]{1,0:T(8,128)} add(f32[512,256]{1,0:T(8,128)S(1)} %convert_add_fusion.3, f32[512,256]{1,0:T(8,128)S(1)} %collective-permute-done.18) | non-fusion elementwise | flops 131072 | bytes 1572864 | tf_op jit(solution)/shard_map/add | solution.py:451
  77.7 0.5 collective-permute-done.17
  78.1 0.9 %bitcast_select_fusion = f32[512,256]{1,0:T(8,128)} fusion(f32[256,256]{1,0:T(8,128)S(1)} %collective-permute-done.17, f32[256,256]{1,0:T(8,128)S(1)} %convert_add_fusion.4, pred[512]{0:T(512)(128)(4,1)S(1)} %broadcast_in_dim.36), kind=kLoop, calls=%fused_computation.4 | loop fusion | flops 131072 | bytes 1049088 | tf_op jit(solution)/shard_map/jit(_where)/select_n | solution.py:323
  (6 shorter events, 0.2 us)
Async XLA Ops:
  0.6 13.4 %collective-permute-start = (bf16[512,256]{1,0:T(8,128)(2,1)}, bf16[512,256]{1,0:T(8,128)(2,1)S(1)}, u32[]{:S(2)}, u32[]{:S(2)}) collective-permute-start(bf16[512,256]{1,0:T(8,128)(2,1)} %own_ref.1), channel_id=1, source_target_pairs={{0,4},{1,9},{2,6},{3,11},{4,8},{5,13},{6,10},{7,15},{8,12},{9,17},... | collective-permute-start | bytes 786440 | tf_op jit(solution)/shard_map/ppermute | solution.py:22
  3.6 16.0 %collective-permute-start.2 = (bf16[512,256]{1,0:T(8,128)(2,1)}, bf16[512,256]{1,0:T(8,128)(2,1)S(1)}, u32[]{:S(2)}, u32[]{:S(2)}) collective-permute-start(bf16[512,256]{1,0:T(8,128)(2,1)} %rest_1_.1), channel_id=1, source_target_pairs={{0,4},{1,9},{2,6},{3,11},{4,8},{5,13},{6,10},{7,15},{8,12},{9,17},... | collective-permute-start | bytes 786440 | tf_op jit(solution)/shard_map/ppermute | solution.py:22
  5.2 1.2 %copy-start = (bf16[512,1024]{1,0:T(8,128)(2,1)S(1)}, bf16[512,1024]{1,0:T(8,128)(2,1)}, u32[]{:S(2)}) copy-start(bf16[512,1024]{1,0:T(8,128)(2,1)} %q_ref.1) | copy-start | bytes 3145732
  6.4 1.2 %copy-start.1 = (bf16[512,1024]{1,0:T(8,128)(2,1)S(1)}, bf16[512,1024]{1,0:T(8,128)(2,1)}, u32[]{:S(2)}) copy-start(bf16[512,1024]{1,0:T(8,128)(2,1)} %g_ref.1) | copy-start | bytes 3145732
  7.6 0.9 %copy-start.2 = (bf16[512,256]{1,0:T(8,128)(2,1)S(1)}, bf16[512,256]{1,0:T(8,128)(2,1)}, u32[]{:S(2)}) copy-start(bf16[512,256]{1,0:T(8,128)(2,1)} %own_ref.1) | copy-start | bytes 786436
  14.0 23.9 %copy-start.3 = (bf16[512,256]{1,0:T(8,128)(2,1)S(1)}, bf16[512,256]{1,0:T(8,128)(2,1)}, u32[]{:S(2)}) copy-start(bf16[512,256]{1,0:T(8,128)(2,1)} %rest_1_.1) | copy-start | bytes 786436
  14.0 8.2 %collective-permute-start.1 = (bf16[512,256]{1,0:T(8,128)(2,1)S(1)}, bf16[512,256]{1,0:T(8,128)(2,1)S(1)}, u32[]{:S(2)}, u32[]{:S(2)}) collective-permute-start(bf16[512,256]{1,0:T(8,128)(2,1)S(1)} %collective-permute-done.rest_0_), channel_id=1, source_target_pairs={{0,8},{1,9},{2,10},{3,11},{4,12},{5,13},{6,14},{7,15},{8,16},{9,17... | collective-permute-start | bytes 786440 | tf_op jit(solution)/shard_map/ppermute | solution.py:22
  14.0 8.2 %collective-permute-start.4 = (bf16[512,256]{1,0:T(8,128)(2,1)S(1)}, bf16[512,256]{1,0:T(8,128)(2,1)S(1)}, u32[]{:S(2)}, u32[]{:S(2)}) collective-permute-start(bf16[512,256]{1,0:T(8,128)(2,1)S(1)} %collective-permute-done.rest_0_), channel_id=1, source_target_pairs={{0,1},{1,0},{2,3},{3,2},{4,5},{5,4},{6,7},{7,6},{8,9},{9,8},{10,11... | collective-permute-start | bytes 786440 | tf_op jit(solution)/shard_map/ppermute | solution.py:27
  22.2 1.5 %collective-permute-start.5 = (bf16[512,256]{1,0:T(8,128)(2,1)S(1)}, bf16[512,256]{1,0:T(8,128)(2,1)S(1)}, u32[]{:S(2)}, u32[]{:S(2)}) collective-permute-start(bf16[512,256]{1,0:T(8,128)(2,1)S(1)} %collective-permute-done.1.rest_1_), channel_id=1, source_target_pairs={{0,1},{1,0},{2,3},{3,2},{4,5},{5,4},{6,7},{7,6},{8,9},{9,8},{10,11... | collective-permute-start | bytes 786440 | tf_op jit(solution)/shard_map/ppermute | solution.py:27
  22.2 11.3 %collective-permute-start.3 = (bf16[512,256]{1,0:T(8,128)(2,1)S(1)}, bf16[512,256]{1,0:T(8,128)(2,1)S(1)}, u32[]{:S(2)}, u32[]{:S(2)}) collective-permute-start(bf16[512,256]{1,0:T(8,128)(2,1)S(1)} %collective-permute-done.2.rest_2_), channel_id=1, source_target_pairs={{0,8},{1,9},{2,10},{3,11},{4,12},{5,13},{6,14},{7,15},{8,16},{9,17... | collective-permute-start | bytes 786440 | tf_op jit(solution)/shard_map/ppermute | solution.py:22
  33.5 2.0 %collective-permute-start.6 = (bf16[2,512,256]{2,1,0:T(8,128)(2,1)S(1)}, bf16[2,512,256]{2,1,0:T(8,128)(2,1)S(1)}, u32[]{:S(2)}, u32[]{:S(2)}) collective-permute-start(bf16[2,512,256]{2,1,0:T(8,128)(2,1)S(1)} %get-tuple-element.55), channel_id=1, source_target_pairs={{0,1},{1,0},{2,3},{3,2},{4,5},{5,4},{6,7},{7,6},{8,9},{9,8},{10,11... | collective-permute-start | bytes 1572872 | tf_op jit(solution)/shard_map/ppermute | solution.py:27
  33.7 4.3 %collective-permute-start.8 = (bf16[512,256]{1,0:T(8,128)(2,1)S(1)}, bf16[512,256]{1,0:T(8,128)(2,1)S(1)}, u32[]{:S(2)}, u32[]{:S(2)}) collective-permute-start(bf16[512,256]{1,0:T(8,128)(2,1)S(1)} %collective-permute-done.2.rest_2_), channel_id=1, source_target_pairs={{0,1},{1,0},{2,3},{3,2},{4,5},{5,4},{6,7},{7,6},{8,9},{9,8},{10,11... | collective-permute-start | bytes 786440 | tf_op jit(solution)/shard_map/ppermute | solution.py:27
  34.1 3.9 %collective-permute-start.9 = (bf16[512,256]{1,0:T(8,128)(2,1)S(1)}, bf16[512,256]{1,0:T(8,128)(2,1)S(1)}, u32[]{:S(2)}, u32[]{:S(2)}) collective-permute-start(bf16[512,256]{1,0:T(8,128)(2,1)S(1)} %collective-permute-done.3.rest_3_), channel_id=1, source_target_pairs={{0,1},{1,0},{2,3},{3,2},{4,5},{5,4},{6,7},{7,6},{8,9},{9,8},{10,11... | collective-permute-start | bytes 786440 | tf_op jit(solution)/shard_map/ppermute | solution.py:27
  35.6 10.7 %collective-permute-start.7 = (bf16[512,256]{1,0:T(8,128)(2,1)S(1)}, bf16[512,256]{1,0:T(8,128)(2,1)S(1)}, u32[]{:S(2)}, u32[]{:S(2)}) collective-permute-start(bf16[512,256]{1,0:T(8,128)(2,1)S(1)} %fusion.2), channel_id=1, source_target_pairs={{0,24},{1,25},{2,26},{3,27},{4,28},{5,29},{6,30},{7,31},{8,0},{9,1... | collective-permute-start | bytes 786440 | tf_op jit(solution)/shard_map/ppermute | solution.py:22
  46.3 4.3 %collective-permute-start.10 = (bf16[2,512,256]{2,1,0:T(8,128)(2,1)S(1)}, bf16[2,512,256]{2,1,0:T(8,128)(2,1)S(1)}, u32[]{:S(2)}, u32[]{:S(2)}) collective-permute-start(bf16[2,512,256]{2,1,0:T(8,128)(2,1)S(1)} %get-tuple-element.65), channel_id=1, source_target_pairs={{0,1},{1,0},{2,3},{3,2},{4,5},{5,4},{6,7},{7,6},{8,9},{9,8},{10,11... | collective-permute-start | bytes 1572872 | tf_op jit(solution)/shard_map/ppermute | solution.py:27
  46.5 10.9 %collective-permute-start.12 = (bf16[512,256]{1,0:T(8,128)(2,1)S(1)}, bf16[512,256]{1,0:T(8,128)(2,1)S(1)}, u32[]{:S(2)}, u32[]{:S(2)}) collective-permute-start(bf16[512,256]{1,0:T(8,128)(2,1)S(1)} %fusion.1), channel_id=1, source_target_pairs={{0,28},{1,25},{2,30},{3,27},{4,0},{5,29},{6,2},{7,31},{8,4},{9,1},... | collective-permute-start | bytes 786440 | tf_op jit(solution)/shard_map/ppermute | solution.py:22
  50.7 10.1 %collective-permute-start.11 = (bf16[512,256]{1,0:T(8,128)(2,1)S(1)}, bf16[512,256]{1,0:T(8,128)(2,1)S(1)}, u32[]{:S(2)}, u32[]{:S(2)}) collective-permute-start(bf16[512,256]{1,0:T(8,128)(2,1)S(1)} %fusion.3), channel_id=1, source_target_pairs={{0,24},{1,25},{2,26},{3,27},{4,28},{5,29},{6,30},{7,31},{8,0},{9,1... | collective-permute-start | bytes 786440 | tf_op jit(solution)/shard_map/ppermute | solution.py:22
  60.9 6.4 %collective-permute-start.13 = (bf16[512,256]{1,0:T(8,128)(2,1)S(1)}, bf16[512,256]{1,0:T(8,128)(2,1)S(1)}, u32[]{:S(2)}, u32[]{:S(2)}) collective-permute-start(bf16[512,256]{1,0:T(8,128)(2,1)S(1)} %add_convert_fusion), channel_id=1, source_target_pairs={{0,2},{1,3},{2,0},{3,1},{4,6},{5,7},{6,4},{7,5},{8,10},{9,11},{10,... | collective-permute-start | bytes 786440 | tf_op jit(solution)/shard_map/ppermute | solution.py:27
  62.7 6.6 %collective-permute-start.14 = (bf16[512,256]{1,0:T(8,128)(2,1)S(1)}, bf16[512,256]{1,0:T(8,128)(2,1)S(1)}, u32[]{:S(2)}, u32[]{:S(2)}) collective-permute-start(bf16[512,256]{1,0:T(8,128)(2,1)S(1)} %fusion), channel_id=1, source_target_pairs={{0,28},{1,25},{2,30},{3,27},{4,0},{5,29},{6,2},{7,31},{8,4},{9,1},... | collective-permute-start | bytes 786440 | tf_op jit(solution)/shard_map/ppermute | solution.py:22
  69.4 1.4 %collective-permute-start.15 = (bf16[256,256]{1,0:T(8,128)(2,1)S(1)}, bf16[256,256]{1,0:T(8,128)(2,1)S(1)}, u32[]{:S(2)}, u32[]{:S(2)}) collective-permute-start(bf16[256,256]{1,0:T(8,128)(2,1)S(1)} %select_convert_fusion), channel_id=1, source_target_pairs={{0,1},{1,0},{2,3},{3,2},{4,5},{5,4},{6,7},{7,6},{8,9},{9,8},{10,11... | collective-permute-start | bytes 393224 | tf_op jit(solution)/shard_map/ppermute | solution.py:27
  70.9 5.6 %collective-permute-start.16 = (bf16[256,256]{1,0:T(8,128)(2,1)S(1)}, bf16[256,256]{1,0:T(8,128)(2,1)S(1)}, u32[]{:S(2)}, u32[]{:S(2)}) collective-permute-start(bf16[256,256]{1,0:T(8,128)(2,1)S(1)} %add_convert_fusion.1), channel_id=1, source_target_pairs={{0,2},{1,3},{2,0},{3,1},{4,6},{5,7},{6,4},{7,5},{8,10},{9,11},{10,... | collective-permute-start | bytes 393224 | tf_op jit(solution)/shard_map/ppermute | solution.py:27
  71.4 5.4 %collective-permute-start.18 = (f32[512,256]{1,0:T(8,128)S(1)}, f32[512,256]{1,0:T(8,128)S(1)}, u32[]{:S(2)}, u32[]{:S(2)}) collective-permute-start(f32[512,256]{1,0:T(8,128)S(1)} %convert_add_fusion.3), channel_id=1, source_target_pairs={{0,1},{1,0},{2,3},{3,2},{4,5},{5,4},{6,7},{7,6},{8,9},{9,8},{10,11... | collective-permute-start | bytes 1572872 | tf_op jit(solution)/shard_map/ppermute | solution.py:27
  76.5 1.6 %collective-permute-start.17 = (f32[256,256]{1,0:T(8,128)S(1)}, f32[256,256]{1,0:T(8,128)S(1)}, u32[]{:S(2)}, u32[]{:S(2)}) collective-permute-start(f32[256,256]{1,0:T(8,128)S(1)} %convert_add_fusion.4), channel_id=1, source_target_pairs={{0,1},{1,0},{2,3},{3,2},{4,5},{5,4},{6,7},{7,6},{8,9},{9,8},{10,11... | collective-permute-start | bytes 786440 | tf_op jit(solution)/shard_map/ppermute | solution.py:27

commit v4 on v3

--- a/solution.py
+++ b/solution.py
@@ -12,13 +12,14 @@
 VMEM_BYTES = 18 * 1024 * 1024
 
 
-def along_seq(block, near, step=0):
+def along_seq(block, near, step=0, ring=True):
     shards, group = lax.axis_size("seq"), lax.axis_size("head")
     route = []
     for shard in range(shards):
         for member in range(group):
-            target = (shard + near + (member % 2) * step) % shards
-            route.append((shard * group + member, target * group + member))
+            target = shard + near + (member % 2) * step
+            if ring or 0 <= target < shards:
+                route.append((shard * group + member, target % shards * group + member))
     return lax.ppermute(block, ("seq", "head"), route)
 
 
@@ -281,8 +282,8 @@
     block, early = lax.optimization_barrier((along_seq(keys, 1, 1), early))
     mine = [block]
     for _ in range(1, reach // 2):
-        mine.append(along_seq(mine[-1], 2, 0))
-    last, value_block = lax.optimization_barrier((mine[-1], along_seq(values, 1, 1)))
+        mine.append(along_seq(mine[-1], 2, ring=False))
+    last, value_block = lax.optimization_barrier((mine[-1], along_seq(values, 1, 1, ring=False)))
     mine[-1] = last
     value_blocks = [value_block]
     for _ in range(1, reach // 2):
@@ -414,7 +415,7 @@
     values_other = [swap_heads(block, 1) for block in values_mine]
     dv_parts = pair_sums(dv_keep, dv_send)
     dv_parts, probs = lax.optimization_barrier((dv_parts, probs))
-    dv_back = along_seq(dv_parts[-1].astype(jnp.bfloat16), -2)
+    dv_back = along_seq(dv_parts[-1].astype(jnp.bfloat16), -2, ring=False)
 
     dscores, dk_down, dk_keep, dk_send = call(
         dscores_kernel,
@@ -432,7 +433,7 @@
     dv_back, dk_keep, dk_send = lax.optimization_barrier((dv_back, dk_keep, dk_send))
     dk_parts = pair_sums(dk_keep, dk_send)
     dk_parts, dscores = lax.optimization_barrier((dk_parts, dscores))
-    dk_back = along_seq(dk_parts[-1].astype(jnp.bfloat16), -2)
+    dk_back = along_seq(dk_parts[-1].astype(jnp.bfloat16), -2, ring=False)
     dv_back = relay_back(dv_parts, dv_back)
 
     (grad_query,) = call(
@@ -444,7 +445,8 @@
         out_shape=[jax.ShapeDtypeStruct(query.shape, query.dtype)],
     )(dscores, keys_ext)
 
-    dk_back, dv_back, grad_query = lax.optimization_barrier((dk_back, dv_back, grad_query))
+    dv_back, grad_query = lax.optimization_barrier((dv_back, grad_query))
+    dk_back, grad_query = lax.optimization_barrier((dk_back, grad_query))
     dk_back = relay_back(dk_parts, dk_back)
     dv_own = sum_chips(dv_down + dv_back.astype(jnp.float32))
     dv_own, dk_back = lax.optimization_barrier((dv_own, dk_back))

time: 79.3 us -> 75.9 us (0.957)
  waiting for transfers between devices: 33 us -> 19.4 us
  starting transfers between devices: 16.9 us -> 26.9 us
    ppermute x8, waiting for transfers between devices: 21.3 us -> 11.4 us  [along_seq(): return lax.ppermute(block, ('seq', 'head'), route)]
    ppermute x8, starting transfers between devices: 13.7 us -> 22.8 us  [along_seq(): return lax.ppermute(block, ('seq', 'head'), route)]
    ppermute x11, waiting for transfers between devices: 11.7 us -> 8.03 us  [swap_heads(): return lax.ppermute(block, 'head', route)]
    ppermute x11, starting transfers between devices: 3.19 us -> 4.11 us  [swap_heads(): return lax.ppermute(block, 'head', route)]
  transfers between devices with their start and end apart: 19 -> 19, of which waited for: 12 -> 10; matrix products, arithmetic and copies ran while one was open for 2% -> 2% of each run, Pallas kernels for 28% -> 30%
where the time goes in v4:
time: 75.9 us; the launch traced here: 75.6 us
  starting transfers between devices  26.9 us (35%)
  Pallas kernels  22.3 us (29%)
  waiting for transfers between devices  19.4 us (26%)
  local copies, waits for them, and re-layouts  3.55 us (5%)
  other arithmetic  2.57 us (3%)
  between operations  0.84 us (1%)
    ppermute x8, starting transfers between devices, along_seq(): return lax.ppermute(block, ('seq', 'head'), route)  22.8 us
    ppermute x8, waiting for transfers between devices, along_seq(): return lax.ppermute(block, ('seq', 'head'), route)  11.4 us
    pallas_call x1, Pallas kernels, on_device(): call(probs_kernel, 'probs', 2, in_specs=[smem, by_head_first, by_head_nex...  9.74 us
    pallas_call x1, Pallas kernels, on_device(): call(dscores_kernel, 'dscores', 2, in_specs=[smem, by_head_first, by_head...  8.32 us
    ppermute x11, waiting for transfers between devices, swap_heads(): return lax.ppermute(block, 'head', route)  8.03 us
    ppermute x11, starting transfers between devices, swap_heads(): return lax.ppermute(block, 'head', route)  4.11 us
    pallas_call x1, Pallas kernels, on_device(): call(dquery_kernel, 'dquery', 1, in_specs=[vmem, vmem], out_specs=[by_hea...  4.08 us
    unnamed x8, local copies, waits for them, and re-layouts  3.4 us
  transfers between devices with their start and end apart: 19, of which 10 were waited for; matrix products, arithmetic and copies ran while one was open for 2% of the time, Pallas kernels for 30%

profile of v4, /device:TPU:0, one launch (start us, length us, event | category | flops | bytes accessed | tf_op | source)
XLA Modules:
  0.0 75.6 jit_solution(571390094211596719)
XLA Ops:
  0.6 3.0 %collective-permute-start = (bf16[512,256]{1,0:T(8,128)(2,1)}, bf16[512,256]{1,0:T(8,128)(2,1)S(1)}, u32[]{:S(2)}, u32[]{:S(2)}) collective-permute-start(bf16[512,256]{1,0:T(8,128)(2,1)} %own_ref.1), channel_id=1, source_target_pairs={{0,4},{1,9},{2,6},{3,11},{4,8},{5,13},{6,10},{7,15},{8,12},{9,17},... | collective-permute-start | bytes 786440 | tf_op jit(solution)/shard_map/ppermute | solution.py:23
  3.6 3.4 %collective-permute-start.2 = (bf16[512,256]{1,0:T(8,128)(2,1)}, bf16[512,256]{1,0:T(8,128)(2,1)S(1)}, u32[]{:S(2)}, u32[]{:S(2)}) collective-permute-start(bf16[512,256]{1,0:T(8,128)(2,1)} %rest_1_.1), channel_id=1, source_target_pairs={{0,4},{1,9},{2,6},{3,11},{4,8},{5,13},{6,10},{7,15},{8,12},{9,17},... | collective-permute-start | bytes 786440 | tf_op jit(solution)/shard_map/ppermute | solution.py:23
  7.1 0.0 copy-start
  7.1 1.2 %copy-done = bf16[512,1024]{1,0:T(8,128)(2,1)S(1)} copy-done((bf16[512,1024]{1,0:T(8,128)(2,1)S(1)}, bf16[512,1024]{1,0:T(8,128)(2,1)}, u32[]{:S(2)}) %copy-start) | copy-done | bytes 1048600
  8.3 0.0 copy-start.1
  8.3 1.2 %copy-done.1 = bf16[512,1024]{1,0:T(8,128)(2,1)S(1)} copy-done((bf16[512,1024]{1,0:T(8,128)(2,1)S(1)}, bf16[512,1024]{1,0:T(8,128)(2,1)}, u32[]{:S(2)}) %copy-start.1) | copy-done | bytes 1048600
  9.6 0.0 copy-start.2
  9.6 0.9 %copy-done.2 = bf16[512,256]{1,0:T(8,128)(2,1)S(1)} copy-done((bf16[512,256]{1,0:T(8,128)(2,1)S(1)}, bf16[512,256]{1,0:T(8,128)(2,1)}, u32[]{:S(2)}) %copy-start.2) | copy-done | bytes 262168
  10.5 0.2 stage.1
  10.7 0.1 pad_add_fusion.1.place
  10.8 2.4 %collective-permute-done.rest_0_ = bf16[512,256]{1,0:T(8,128)(2,1)S(1)} collective-permute-done((bf16[512,256]{1,0:T(8,128)(2,1)}, bf16[512,256]{1,0:T(8,128)(2,1)S(1)}, u32[]{:S(2)}, u32[]{:S(2)}) %collective-permute-start) | collective-permute-done | bytes 262176 | tf_op jit(solution)/shard_map/ppermute | solution.py:23
  13.2 0.0 copy-start.3
  13.2 2.8 %collective-permute-start.1 = (bf16[512,256]{1,0:T(8,128)(2,1)S(1)}, bf16[512,256]{1,0:T(8,128)(2,1)S(1)}, u32[]{:S(2)}, u32[]{:S(2)}) collective-permute-start(bf16[512,256]{1,0:T(8,128)(2,1)S(1)} %collective-permute-done.rest_0_), channel_id=1, source_target_pairs={{0,8},{1,9},{2,10},{3,11},{4,12},{5,13},{6,14},{7,15},{8,16},{9,17... | collective-permute-start | bytes 786440 | tf_op jit(solution)/shard_map/ppermute | solution.py:23
  16.1 0.1 collective-permute-start.4
  16.1 0.0 collective-permute-done.2.rest_2_
  16.1 3.8 %collective-permute-done.1.rest_1_ = bf16[512,256]{1,0:T(8,128)(2,1)S(1)} collective-permute-done((bf16[512,256]{1,0:T(8,128)(2,1)S(1)}, bf16[512,256]{1,0:T(8,128)(2,1)S(1)}, u32[]{:S(2)}, u32[]{:S(2)}) %collective-permute-start.1) | collective-permute-done | bytes 262176 | tf_op jit(solution)/shard_map/ppermute | solution.py:23
  19.9 0.0 collective-permute-start.5
  19.9 2.5 %collective-permute-start.3 = (bf16[512,256]{1,0:T(8,128)(2,1)S(1)}, bf16[512,256]{1,0:T(8,128)(2,1)S(1)}, u32[]{:S(2)}, u32[]{:S(2)}) collective-permute-start(bf16[512,256]{1,0:T(8,128)(2,1)S(1)} %collective-permute-done.2.rest_2_), channel_id=1, source_target_pairs={{0,8},{1,9},{2,10},{3,11},{4,12},{5,13},{6,14},{7,15},{8,16},{9,17... | collective-permute-start | bytes 786440 | tf_op jit(solution)/shard_map/ppermute | solution.py:23
  22.4 0.0 collective-permute-done.4.rest_2_
  22.4 0.0 collective-permute-done.5.rest_3_
  22.4 9.7 %probs.1 = (bf16[4,2048,512]{2,1,0:T(8,128)(2,1)S(1)}, f32[4,8,512]{2,1,0:T(8,128)S(1)}, bf16[2560,256]{1,0:T(8,128)(2,1)S(1)}, f32[512,256]{1,0:T(8,128)S(1)}, ...) custom-call(s32[2]{0:T(128)S(1)} %pad_add_fusion.1.place, ...), custom_call_target="tpu_custom_call" | custom-call | flops 4831838208 | bytes 16777216 | tf_op jit(solution)/shard_map/probs/pallas_call | solution.py:397
  32.2 0.0 collective-permute-done.3.rest_3_
  32.2 0.3 collective-permute-start.6
  32.4 0.3 collective-permute-start.8
  32.7 0.2 collective-permute-start.9
  33.0 1.2 %collective-permute-done.6 = bf16[2,512,256]{2,1,0:T(8,128)(2,1)S(1)} collective-permute-done((bf16[2,512,256]{2,1,0:T(8,128)(2,1)S(1)}, bf16[2,512,256]{2,1,0:T(8,128)(2,1)S(1)}, u32[]{:S(2)}, u32[]{:S(2)}) %collective-permute-start.6) | collective-permute-done | bytes 524320 | tf_op jit(solution)/shard_map/ppermute | solution.py:28
  34.1 0.1 convert_add_fusion.1
  34.3 1.3 %collective-permute-start.7 = (bf16[512,256]{1,0:T(8,128)(2,1)S(1)}, bf16[512,256]{1,0:T(8,128)(2,1)S(1)}, u32[]{:S(2)}, u32[]{:S(2)}) collective-permute-start(bf16[512,256]{1,0:T(8,128)(2,1)S(1)} %fusion.2), channel_id=1, source_target_pairs={{8,0},{9,1},{10,2},{11,3},{12,4},{13,5},{14,6},{15,7},{16,8},{17,9... | collective-permute-start | bytes 786440 | tf_op jit(solution)/shard_map/ppermute | solution.py:23
  35.6 0.0 collective-permute-done.8.rest_4_
  35.6 0.0 collective-permute-done.9.rest_5_
  35.6 0.0 copy-done.3
  35.6 8.3 %dscores.1 = (bf16[4,2048,512]{2,1,0:T(8,128)(2,1)S(1)}, f32[512,256]{1,0:T(8,128)S(1)}, f32[2,512,256]{2,1,0:T(8,128)S(1)}, bf16[2,512,256]{2,1,0:T(8,128)(2,1)S(1)}) custom-call(s32[2]{0:T(128)S(1)} %pad_add_fusion.1.place, bf16[512,1024]{1,0:T(8,128)(2,1)S(1)} %get-tuple-element.49.g_ref.first_ref, ...), custom_call_target="tpu_custom_call" | custom-call | flops 4831838208 | bytes 16777216 | tf_op jit(solution)/shard_map/dscores/pallas_call | solution.py:420
  43.9 0.7 collective-permute-done.7
  44.6 0.0 collective-permute-start.10
  44.6 0.1 fusion.1
  44.7 5.9 %collective-permute-start.12 = (bf16[512,256]{1,0:T(8,128)(2,1)S(1)}, bf16[512,256]{1,0:T(8,128)(2,1)S(1)}, u32[]{:S(2)}, u32[]{:S(2)}) collective-permute-start(bf16[512,256]{1,0:T(8,128)(2,1)S(1)} %fusion.1), channel_id=1, source_target_pairs={{0,28},{1,25},{2,30},{3,27},{4,0},{5,29},{6,2},{7,31},{8,4},{9,1},... | collective-permute-start | bytes 786440 | tf_op jit(solution)/shard_map/ppermute | solution.py:23
  50.6 0.0 collective-permute-done.10
  50.6 0.1 convert_add_fusion
  50.7 1.3 %collective-permute-start.11 = (bf16[512,256]{1,0:T(8,128)(2,1)S(1)}, bf16[512,256]{1,0:T(8,128)(2,1)S(1)}, u32[]{:S(2)}, u32[]{:S(2)}) collective-permute-start(bf16[512,256]{1,0:T(8,128)(2,1)S(1)} %fusion.3), channel_id=1, source_target_pairs={{8,0},{9,1},{10,2},{11,3},{12,4},{13,5},{14,6},{15,7},{16,8},{17,9... | collective-permute-start | bytes 786440 | tf_op jit(solution)/shard_map/ppermute | solution.py:23
  52.0 4.1 %dquery.1 = bf16[512,1024]{1,0:T(8,128)(2,1)} custom-call(bf16[4,2048,512]{2,1,0:T(8,128)(2,1)S(1)} %get-tuple-element.70.ds_ref, bf16[2560,256]{1,0:T(8,128)(2,1)S(1)} %get-tuple-element.71.ext), custom_call_target="tpu_custom_call" | custom-call | flops 2415919104 | bytes 16777216 | tf_op jit(solution)/shard_map/dquery/pallas_call | solution.py:439
  56.1 0.0 collective-permute-done.12
  56.1 0.1 add_convert_fusion
  56.2 1.5 %collective-permute-start.13 = (bf16[512,256]{1,0:T(8,128)(2,1)S(1)}, bf16[512,256]{1,0:T(8,128)(2,1)S(1)}, u32[]{:S(2)}, u32[]{:S(2)}) collective-permute-start(bf16[512,256]{1,0:T(8,128)(2,1)S(1)} %add_convert_fusion), channel_id=1, source_target_pairs={{0,2},{1,3},{2,0},{3,1},{4,6},{5,7},{6,4},{7,5},{8,10},{9,11},{10,... | collective-permute-start | bytes 786440 | tf_op jit(solution)/shard_map/ppermute | solution.py:28
  57.7 1.6 %collective-permute-done.11 = bf16[512,256]{1,0:T(8,128)(2,1)S(1)} collective-permute-done((bf16[512,256]{1,0:T(8,128)(2,1)S(1)}, bf16[512,256]{1,0:T(8,128)(2,1)S(1)}, u32[]{:S(2)}, u32[]{:S(2)}) %collective-permute-start.11) | collective-permute-done | bytes 262176 | tf_op jit(solution)/shard_map/ppermute | solution.py:23
  59.4 0.1 fusion
  59.4 2.5 %collective-permute-start.14 = (bf16[512,256]{1,0:T(8,128)(2,1)S(1)}, bf16[512,256]{1,0:T(8,128)(2,1)S(1)}, u32[]{:S(2)}, u32[]{:S(2)}) collective-permute-start(bf16[512,256]{1,0:T(8,128)(2,1)S(1)} %fusion), channel_id=1, source_target_pairs={{0,28},{1,25},{2,30},{3,27},{4,0},{5,29},{6,2},{7,31},{8,4},{9,1},... | collective-permute-start | bytes 786440 | tf_op jit(solution)/shard_map/ppermute | solution.py:23
  62.0 1.0 %collective-permute-done.13 = bf16[512,256]{1,0:T(8,128)(2,1)S(1)} collective-permute-done((bf16[512,256]{1,0:T(8,128)(2,1)S(1)}, bf16[512,256]{1,0:T(8,128)(2,1)S(1)}, u32[]{:S(2)}, u32[]{:S(2)}) %collective-permute-start.13) | collective-permute-done | bytes 262176 | tf_op jit(solution)/shard_map/ppermute | solution.py:28
  62.9 0.1 convert_add_fusion.3
  63.0 2.9 %collective-permute-done.14 = bf16[512,256]{1,0:T(8,128)(2,1)S(1)} collective-permute-done((bf16[512,256]{1,0:T(8,128)(2,1)S(1)}, bf16[512,256]{1,0:T(8,128)(2,1)S(1)}, u32[]{:S(2)}, u32[]{:S(2)}) %collective-permute-start.14) | collective-permute-done | bytes 262176 | tf_op jit(solution)/shard_map/ppermute | solution.py:23
  65.9 0.1 convert_add_fusion.2
  66.0 0.1 collective-permute-start.15
  66.0 1.3 %collective-permute-done.15 = bf16[256,256]{1,0:T(8,128)(2,1)S(1)} collective-permute-done((bf16[256,256]{1,0:T(8,128)(2,1)S(1)}, bf16[256,256]{1,0:T(8,128)(2,1)S(1)}, u32[]{:S(2)}, u32[]{:S(2)}) %collective-permute-start.15) | collective-permute-done | bytes 131104 | tf_op jit(solution)/shard_map/ppermute | solution.py:28
  67.4 1.6 %collective-permute-start.16 = (bf16[256,256]{1,0:T(8,128)(2,1)S(1)}, bf16[256,256]{1,0:T(8,128)(2,1)S(1)}, u32[]{:S(2)}, u32[]{:S(2)}) collective-permute-start(bf16[256,256]{1,0:T(8,128)(2,1)S(1)} %add_convert_fusion.1), channel_id=1, source_target_pairs={{0,2},{1,3},{2,0},{3,1},{4,6},{5,7},{6,4},{7,5},{8,10},{9,11},{10,... | collective-permute-start | bytes 393224 | tf_op jit(solution)/shard_map/ppermute | solution.py:28
  69.0 0.0 collective-permute-start.18
  69.0 4.1 %collective-permute-done.16 = bf16[256,256]{1,0:T(8,128)(2,1)S(1)} collective-permute-done((bf16[256,256]{1,0:T(8,128)(2,1)S(1)}, bf16[256,256]{1,0:T(8,128)(2,1)S(1)}, u32[]{:S(2)}, u32[]{:S(2)}) %collective-permute-start.16) | collective-permute-done | bytes 131104 | tf_op jit(solution)/shard_map/ppermute | solution.py:28
  73.1 0.1 collective-permute-start.17
  73.1 0.1 pad_add_fusion
  73.2 0.1 broadcast_in_dim.35
  73.3 0.0 collective-permute-done.18
  73.3 0.9 %add.44 = f32[512,256]{1,0:T(8,128)} add(f32[512,256]{1,0:T(8,128)S(1)} %convert_add_fusion.3, f32[512,256]{1,0:T(8,128)S(1)} %collective-permute-done.18) | non-fusion elementwise | flops 131072 | bytes 1572864 | tf_op jit(solution)/shard_map/add | solution.py:453
  74.2 0.5 collective-permute-done.17
  74.7 0.9 %bitcast_select_fusion = f32[512,256]{1,0:T(8,128)} fusion(f32[256,256]{1,0:T(8,128)S(1)} %collective-permute-done.17, f32[256,256]{1,0:T(8,128)S(1)} %convert_add_fusion.4, pred[512]{0:T(512)(128)(4,1)S(1)} %broadcast_in_dim.36), kind=kLoop, calls=%fused_computation.4 | loop fusion | flops 131072 | bytes 1049088 | tf_op jit(solution)/shard_map/jit(_where)/select_n | solution.py:324
  (6 shorter events, 0.2 us)
Async XLA Ops:
  0.6 12.6 %collective-permute-start = (bf16[512,256]{1,0:T(8,128)(2,1)}, bf16[512,256]{1,0:T(8,128)(2,1)S(1)}, u32[]{:S(2)}, u32[]{:S(2)}) collective-permute-start(bf16[512,256]{1,0:T(8,128)(2,1)} %own_ref.1), channel_id=1, source_target_pairs={{0,4},{1,9},{2,6},{3,11},{4,8},{5,13},{6,10},{7,15},{8,12},{9,17},... | collective-permute-start | bytes 786440 | tf_op jit(solution)/shard_map/ppermute | solution.py:23
  3.6 12.5 %collective-permute-start.2 = (bf16[512,256]{1,0:T(8,128)(2,1)}, bf16[512,256]{1,0:T(8,128)(2,1)S(1)}, u32[]{:S(2)}, u32[]{:S(2)}) collective-permute-start(bf16[512,256]{1,0:T(8,128)(2,1)} %rest_1_.1), channel_id=1, source_target_pairs={{0,4},{1,9},{2,6},{3,11},{4,8},{5,13},{6,10},{7,15},{8,12},{9,17},... | collective-permute-start | bytes 786440 | tf_op jit(solution)/shard_map/ppermute | solution.py:23
  7.1 1.2 %copy-start = (bf16[512,1024]{1,0:T(8,128)(2,1)S(1)}, bf16[512,1024]{1,0:T(8,128)(2,1)}, u32[]{:S(2)}) copy-start(bf16[512,1024]{1,0:T(8,128)(2,1)} %q_ref.1) | copy-start | bytes 3145732
  8.3 1.2 %copy-start.1 = (bf16[512,1024]{1,0:T(8,128)(2,1)S(1)}, bf16[512,1024]{1,0:T(8,128)(2,1)}, u32[]{:S(2)}) copy-start(bf16[512,1024]{1,0:T(8,128)(2,1)} %g_ref.1) | copy-start | bytes 3145732
  9.6 0.9 %copy-start.2 = (bf16[512,256]{1,0:T(8,128)(2,1)S(1)}, bf16[512,256]{1,0:T(8,128)(2,1)}, u32[]{:S(2)}) copy-start(bf16[512,256]{1,0:T(8,128)(2,1)} %own_ref.1) | copy-start | bytes 786436
  13.2 22.4 %copy-start.3 = (bf16[512,256]{1,0:T(8,128)(2,1)S(1)}, bf16[512,256]{1,0:T(8,128)(2,1)}, u32[]{:S(2)}) copy-start(bf16[512,256]{1,0:T(8,128)(2,1)} %rest_1_.1) | copy-start | bytes 786436
  13.2 6.7 %collective-permute-start.1 = (bf16[512,256]{1,0:T(8,128)(2,1)S(1)}, bf16[512,256]{1,0:T(8,128)(2,1)S(1)}, u32[]{:S(2)}, u32[]{:S(2)}) collective-permute-start(bf16[512,256]{1,0:T(8,128)(2,1)S(1)} %collective-permute-done.rest_0_), channel_id=1, source_target_pairs={{0,8},{1,9},{2,10},{3,11},{4,12},{5,13},{6,14},{7,15},{8,16},{9,17... | collective-permute-start | bytes 786440 | tf_op jit(solution)/shard_map/ppermute | solution.py:23
  16.1 6.3 %collective-permute-start.4 = (bf16[512,256]{1,0:T(8,128)(2,1)S(1)}, bf16[512,256]{1,0:T(8,128)(2,1)S(1)}, u32[]{:S(2)}, u32[]{:S(2)}) collective-permute-start(bf16[512,256]{1,0:T(8,128)(2,1)S(1)} %collective-permute-done.rest_0_), channel_id=1, source_target_pairs={{0,1},{1,0},{2,3},{3,2},{4,5},{5,4},{6,7},{7,6},{8,9},{9,8},{10,11... | collective-permute-start | bytes 786440 | tf_op jit(solution)/shard_map/ppermute | solution.py:28
  19.9 2.5 %collective-permute-start.5 = (bf16[512,256]{1,0:T(8,128)(2,1)S(1)}, bf16[512,256]{1,0:T(8,128)(2,1)S(1)}, u32[]{:S(2)}, u32[]{:S(2)}) collective-permute-start(bf16[512,256]{1,0:T(8,128)(2,1)S(1)} %collective-permute-done.1.rest_1_), channel_id=1, source_target_pairs={{0,1},{1,0},{2,3},{3,2},{4,5},{5,4},{6,7},{7,6},{8,9},{9,8},{10,11... | collective-permute-start | bytes 786440 | tf_op jit(solution)/shard_map/ppermute | solution.py:28
  19.9 12.2 %collective-permute-start.3 = (bf16[512,256]{1,0:T(8,128)(2,1)S(1)}, bf16[512,256]{1,0:T(8,128)(2,1)S(1)}, u32[]{:S(2)}, u32[]{:S(2)}) collective-permute-start(bf16[512,256]{1,0:T(8,128)(2,1)S(1)} %collective-permute-done.2.rest_2_), channel_id=1, source_target_pairs={{0,8},{1,9},{2,10},{3,11},{4,12},{5,13},{6,14},{7,15},{8,16},{9,17... | collective-permute-start | bytes 786440 | tf_op jit(solution)/shard_map/ppermute | solution.py:23
  32.2 2.0 %collective-permute-start.6 = (bf16[2,512,256]{2,1,0:T(8,128)(2,1)S(1)}, bf16[2,512,256]{2,1,0:T(8,128)(2,1)S(1)}, u32[]{:S(2)}, u32[]{:S(2)}) collective-permute-start(bf16[2,512,256]{2,1,0:T(8,128)(2,1)S(1)} %get-tuple-element.56), channel_id=1, source_target_pairs={{0,1},{1,0},{2,3},{3,2},{4,5},{5,4},{6,7},{7,6},{8,9},{9,8},{10,11... | collective-permute-start | bytes 1572872 | tf_op jit(solution)/shard_map/ppermute | solution.py:28
  32.4 3.1 %collective-permute-start.8 = (bf16[512,256]{1,0:T(8,128)(2,1)S(1)}, bf16[512,256]{1,0:T(8,128)(2,1)S(1)}, u32[]{:S(2)}, u32[]{:S(2)}) collective-permute-start(bf16[512,256]{1,0:T(8,128)(2,1)S(1)} %collective-permute-done.2.rest_2_), channel_id=1, source_target_pairs={{0,1},{1,0},{2,3},{3,2},{4,5},{5,4},{6,7},{7,6},{8,9},{9,8},{10,11... | collective-permute-start | bytes 786440 | tf_op jit(solution)/shard_map/ppermute | solution.py:28
  32.7 2.9 %collective-permute-start.9 = (bf16[512,256]{1,0:T(8,128)(2,1)S(1)}, bf16[512,256]{1,0:T(8,128)(2,1)S(1)}, u32[]{:S(2)}, u32[]{:S(2)}) collective-permute-start(bf16[512,256]{1,0:T(8,128)(2,1)S(1)} %collective-permute-done.3.rest_3_), channel_id=1, source_target_pairs={{0,1},{1,0},{2,3},{3,2},{4,5},{5,4},{6,7},{7,6},{8,9},{9,8},{10,11... | collective-permute-start | bytes 786440 | tf_op jit(solution)/shard_map/ppermute | solution.py:28
  34.3 10.3 %collective-permute-start.7 = (bf16[512,256]{1,0:T(8,128)(2,1)S(1)}, bf16[512,256]{1,0:T(8,128)(2,1)S(1)}, u32[]{:S(2)}, u32[]{:S(2)}) collective-permute-start(bf16[512,256]{1,0:T(8,128)(2,1)S(1)} %fusion.2), channel_id=1, source_target_pairs={{8,0},{9,1},{10,2},{11,3},{12,4},{13,5},{14,6},{15,7},{16,8},{17,9... | collective-permute-start | bytes 786440 | tf_op jit(solution)/shard_map/ppermute | solution.py:23
  44.6 6.0 %collective-permute-start.10 = (bf16[2,512,256]{2,1,0:T(8,128)(2,1)S(1)}, bf16[2,512,256]{2,1,0:T(8,128)(2,1)S(1)}, u32[]{:S(2)}, u32[]{:S(2)}) collective-permute-start(bf16[2,512,256]{2,1,0:T(8,128)(2,1)S(1)} %get-tuple-element.66), channel_id=1, source_target_pairs={{0,1},{1,0},{2,3},{3,2},{4,5},{5,4},{6,7},{7,6},{8,9},{9,8},{10,11... | collective-permute-start | bytes 1572872 | tf_op jit(solution)/shard_map/ppermute | solution.py:28
  44.7 11.5 %collective-permute-start.12 = (bf16[512,256]{1,0:T(8,128)(2,1)S(1)}, bf16[512,256]{1,0:T(8,128)(2,1)S(1)}, u32[]{:S(2)}, u32[]{:S(2)}) collective-permute-start(bf16[512,256]{1,0:T(8,128)(2,1)S(1)} %fusion.1), channel_id=1, source_target_pairs={{0,28},{1,25},{2,30},{3,27},{4,0},{5,29},{6,2},{7,31},{8,4},{9,1},... | collective-permute-start | bytes 786440 | tf_op jit(solution)/shard_map/ppermute | solution.py:23
  50.7 8.6 %collective-permute-start.11 = (bf16[512,256]{1,0:T(8,128)(2,1)S(1)}, bf16[512,256]{1,0:T(8,128)(2,1)S(1)}, u32[]{:S(2)}, u32[]{:S(2)}) collective-permute-start(bf16[512,256]{1,0:T(8,128)(2,1)S(1)} %fusion.3), channel_id=1, source_target_pairs={{8,0},{9,1},{10,2},{11,3},{12,4},{13,5},{14,6},{15,7},{16,8},{17,9... | collective-permute-start | bytes 786440 | tf_op jit(solution)/shard_map/ppermute | solution.py:23
  56.2 6.7 %collective-permute-start.13 = (bf16[512,256]{1,0:T(8,128)(2,1)S(1)}, bf16[512,256]{1,0:T(8,128)(2,1)S(1)}, u32[]{:S(2)}, u32[]{:S(2)}) collective-permute-start(bf16[512,256]{1,0:T(8,128)(2,1)S(1)} %add_convert_fusion), channel_id=1, source_target_pairs={{0,2},{1,3},{2,0},{3,1},{4,6},{5,7},{6,4},{7,5},{8,10},{9,11},{10,... | collective-permute-start | bytes 786440 | tf_op jit(solution)/shard_map/ppermute | solution.py:28
  59.4 6.4 %collective-permute-start.14 = (bf16[512,256]{1,0:T(8,128)(2,1)S(1)}, bf16[512,256]{1,0:T(8,128)(2,1)S(1)}, u32[]{:S(2)}, u32[]{:S(2)}) collective-permute-start(bf16[512,256]{1,0:T(8,128)(2,1)S(1)} %fusion), channel_id=1, source_target_pairs={{0,28},{1,25},{2,30},{3,27},{4,0},{5,29},{6,2},{7,31},{8,4},{9,1},... | collective-permute-start | bytes 786440 | tf_op jit(solution)/shard_map/ppermute | solution.py:23
  66.0 1.4 %collective-permute-start.15 = (bf16[256,256]{1,0:T(8,128)(2,1)S(1)}, bf16[256,256]{1,0:T(8,128)(2,1)S(1)}, u32[]{:S(2)}, u32[]{:S(2)}) collective-permute-start(bf16[256,256]{1,0:T(8,128)(2,1)S(1)} %select_convert_fusion), channel_id=1, source_target_pairs={{0,1},{1,0},{2,3},{3,2},{4,5},{5,4},{6,7},{7,6},{8,9},{9,8},{10,11... | collective-permute-start | bytes 393224 | tf_op jit(solution)/shard_map/ppermute | solution.py:28
  67.4 5.6 %collective-permute-start.16 = (bf16[256,256]{1,0:T(8,128)(2,1)S(1)}, bf16[256,256]{1,0:T(8,128)(2,1)S(1)}, u32[]{:S(2)}, u32[]{:S(2)}) collective-permute-start(bf16[256,256]{1,0:T(8,128)(2,1)S(1)} %add_convert_fusion.1), channel_id=1, source_target_pairs={{0,2},{1,3},{2,0},{3,1},{4,6},{5,7},{6,4},{7,5},{8,10},{9,11},{10,... | collective-permute-start | bytes 393224 | tf_op jit(solution)/shard_map/ppermute | solution.py:28
  69.0 4.4 %collective-permute-start.18 = (f32[512,256]{1,0:T(8,128)S(1)}, f32[512,256]{1,0:T(8,128)S(1)}, u32[]{:S(2)}, u32[]{:S(2)}) collective-permute-start(f32[512,256]{1,0:T(8,128)S(1)} %convert_add_fusion.3), channel_id=1, source_target_pairs={{0,1},{1,0},{2,3},{3,2},{4,5},{5,4},{6,7},{7,6},{8,9},{9,8},{10,11... | collective-permute-start | bytes 1572872 | tf_op jit(solution)/shard_map/ppermute | solution.py:28
  73.1 1.6 %collective-permute-start.17 = (f32[256,256]{1,0:T(8,128)S(1)}, f32[256,256]{1,0:T(8,128)S(1)}, u32[]{:S(2)}, u32[]{:S(2)}) collective-permute-start(f32[256,256]{1,0:T(8,128)S(1)} %convert_add_fusion.4), channel_id=1, source_target_pairs={{0,1},{1,0},{2,3},{3,2},{4,5},{5,4},{6,7},{7,6},{8,9},{9,8},{10,11... | collective-permute-start | bytes 786440 | tf_op jit(solution)/shard_map/ppermute | solution.py:28
